TPU v7x, 128 devices: a whole 4x4x4 slice. The times are simulated.
128 devices in a mesh: section: 4 (over x_lo, core), dev: 32 (over x_hi, z, y).
Axes of the slice: x: 4 (x_hi: 2, x_lo: 2; x = x_hi * 2 + x_lo), y: 4, z: 4, core: 2. Of those that a mesh axis runs over, the one named last changes fastest.
Arguments:
- queries: bfloat16 [4, 128, 128, 576], P('section', 'dev'), may hold values from -32 to 32
- res_cache: bfloat16 [4, 64, 4096, 576], P('section', 'dev'), may hold values from -5 to 5
- res_lengths: int32 [4, 64], P('section', 'dev'), may hold values from 2048 to 4096, as said below
- inc_cache: bfloat16 [4, 64, 4096, 576], P('section', None, 'dev'), may hold values from -5 to 5
- inc_lengths: int32 [4, 64], replicated, may hold values from 2048 to 4096, as said below
- matching: int32 [4, 64], replicated, may hold values from 0 to 63, as said below
Outputs:
- attended: bfloat16 [4, 128, 128, 512], P('section', 'dev')
Inputs may be any that keep to these rules, and one draw needn't show every extreme that they name: `res_lengths`: in each group some resident request has exactly 4096 live slots. `inc_lengths`: in each prefill group some request has exactly 4096 live slots. `matching`: each row is a permutation of 0 to 63.
All inputs are finite; a program needn't handle non-finite values.
Results may differ from a plain program's by a relative error of at most 0.0034.
Values may be sent and summed in bfloat16 or wider, within the bound.
No kernel may reach another device: no remote copies, remote signals or barrier semaphores. Data moves between devices by JAX's collectives and lax.ppermute only.
A program may use at most 192 MiB of HBM per device.

v0:
```python
import jax
import jax.numpy as jnp
from jax import lax
from jax.sharding import PartitionSpec as P

KV_RANK = 512


score_scale = 192.0 ** (-0.5)


def from_behind(block, axis, distance):
    devices = range(lax.axis_size(axis))
    route = [((i - distance) % len(devices), i) for i in devices]
    return lax.ppermute(block, axis, route)


def attend(query_row, cache_rows, length):
    scores = jnp.dot(query_row, cache_rows.T, preferred_element_type=jnp.float32) * score_scale
    live_mask = jnp.arange(cache_rows.shape[0], dtype=jnp.int32) < length
    scores = jnp.where(live_mask[None, :], scores, -1e30)
    row_top = jnp.max(scores, axis=1, keepdims=True)
    weights = jnp.exp(scores - row_top)
    row_total = jnp.sum(weights, axis=1, keepdims=True)
    row_probs = weights.astype(jnp.bfloat16)
    latent = jnp.dot(row_probs, cache_rows[:, :KV_RANK], preferred_element_type=jnp.float32)
    return (latent / row_total).astype(jnp.bfloat16)


def attend_items(items):
    return attend(items[0], items[1], items[2])


def per_device(queries, res_cache, res_lengths, inc_cache, inc_lengths, matching):
    sections = lax.axis_size("section")
    half_way = sections // 2
    section_id = lax.axis_index("section")
    source = (section_id + half_way) % sections
    own_match = lax.dynamic_index_in_dim(matching, section_id, 0, keepdims=False)
    ordered = jnp.take(inc_cache[0], own_match, axis=0)
    spread = lax.all_to_all(ordered, "dev", split_axis=0, concat_axis=1, tiled=True)
    arrived = from_behind(spread, "section", half_way)
    inc_count = arrived.shape[0]
    slot_ids = lax.axis_index("dev") * inc_count + jnp.arange(inc_count, dtype=jnp.int32)
    partner_match = lax.dynamic_index_in_dim(matching, source, 0, keepdims=False)
    requests = jnp.take(partner_match, slot_ids, axis=0)
    partner_lengths = lax.dynamic_index_in_dim(inc_lengths, source, 0, keepdims=False)
    arrived_lengths = jnp.take(partner_lengths, requests, axis=0)
    local_queries = queries[0]
    all_caches = jnp.concatenate([res_cache[0], arrived], axis=0)
    all_lengths = jnp.concatenate([res_lengths[0], arrived_lengths], axis=0)
    result = lax.map(attend_items, (local_queries, all_caches, all_lengths))
    return result[None]


def solution(mesh):
    placed = (
        P("section", "dev", None, None),
        P("section", "dev", None, None),
        P("section", "dev"),
        P("section", None, "dev", None),
        P(),
        P(),
    )
    return jax.shard_map(
        per_device,
        mesh=mesh,
        in_specs=placed,
        out_specs=P("section", "dev", None, None),
        check_vma=False,
    )
```

profile of v0, /device:TPU:0, one launch (start us, length us, event | category | flops | bytes accessed | tf_op | source)
XLA Modules:
  0.0 463.4 jit_solution(5139698223012117115)
XLA Ops:
  0.0 0.7 fusion.25
  0.7 0.7 compare_and_fusion
  1.4 9.8 %gather_fusion = bf16[64,128,576]{1,2,0:T(8,128)(2,1)} fusion(bf16[64,128,576]{1,2,0:T(8,128)(2,1)} %bitcast.52, s32[1024]{0:T(1024)S(1)} %pad_clamp_fusion), kind=kCustom, calls=%fused_computation.2 | custom fusion | bytes 18874624 | tf_op jit(solution)/shard_map/jit(_take)/gather | solution.py:40
  11.2 8.3 %broadcast_select_fusion = bf16[64,128,576]{1,2,0:T(8,128)(2,1)} fusion(bf16[64,128,576]{1,2,0:T(8,128)(2,1)} %gather_fusion, pred[64]{0:T(512)(128)(4,1)S(1)} %compare_and_fusion), kind=kLoop, calls=%fused_computation.23 | loop fusion | flops 4718592 | bytes 18874432 | tf_op jit(solution)/shard_map/jit(_take)/select_n | solution.py:40
  19.5 118.8 %all_to_all.18 = bf16[64,128,576]{1,2,0:T(8,128)(2,1)} all-to-all(bf16[64,128,576]{1,2,0:T(8,128)(2,1)} %broadcast_select_fusion), channel_id=1, replica_groups=mesh['section'=4,'dev'=32] {'dev'}, dimensions={0} | all-to-all | bytes 18874368 | tf_op jit(solution)/shard_map/all_to_all | solution.py:41
  138.3 13.4 %copy.18 = bf16[32,2,128,576]{2,0,3,1:T(8,128)(2,1)} copy(bf16[32,2,128,576]{2,3,1,0:T(8,128)(2,1)} %bitcast.50) | data formatting | bytes 18874368 | tf_op jit(solution)/shard_map/all_to_all | solution.py:41
  151.7 14.9 %all_to_all.16 = bf16[2,4096,576]{1,2,0:T(8,128)(2,1)} reshape(bf16[2,32,128,576]{2,1,3,0:T(8,128)(2,1)} %bitcast.51) | data formatting | bytes 18874368 | tf_op jit(solution)/shard_map/all_to_all | solution.py:41
  166.6 0.6 collective-permute-start
  167.2 0.3 copy.13
  167.5 0.7 fusion.24
  168.2 0.6 gather_fusion.1
  168.9 0.6 gather_fusion.2
  169.6 0.0 copy-done.4
  169.6 0.1 pad_add_fusion
  169.7 199.9 %collective-permute-done = bf16[2,4096,576]{1,2,0:T(8,128)(2,1)} collective-permute-done((bf16[2,4096,576]{1,2,0:T(8,128)(2,1)}, bf16[2,4096,576]{1,2,0:T(8,128)(2,1)}, u32[]{:S(2)}, u32[]{:S(2)}) %collective-permute-start) | collective-permute-done | bytes 9437216 | tf_op jit(solution)/shard_map/ppermute | solution.py:15
  369.6 16.5 %pad_maximum_fusion = bf16[4,4096,576]{1,2,0:T(8,128)(2,1)} fusion(bf16[2,4096,576]{1,2,0:T(8,128)(2,1)} %collective-permute-done, bf16[2,4096,576]{1,2,0:T(8,128)(2,1)} %bitcast.53), kind=kLoop, calls=%fused_computation.21 | loop fusion | flops 9437184 | bytes 37748736 | tf_op jit(solution)/shard_map/concatenate | solution.py:50
  386.0 76.6 %while.10 = (s32[]{:T(128)}, bf16[4,128,512]{2,1,0:T(8,128)(2,1)S(1)}, s32[4]{0:T(128)S(1)}, bf16[4,128,576]{2,1,0:T(8,128)(2,1)S(1)}, bf16[4,4096,576]{1,2,0:T(8,128)(2,1)}, /*index=5*/s32[]{:T(128)}) while((s32[]{:T(128)}, bf16[4,128,512]{2,1,0:T(8,128)(2,1)S(1)}, s32[4]{0:T(128)S(1)}, bf16[4,128,576]{2,1,0:T(8,128)(2,1)S(1)}, ...), condition=%wide.region_3.5_spmd, body=%wide.region_0.4_spmd.sunk | while | flops 1144655616 | bytes 53259904 | solution.py:52
  386.0 5.1 %constant_dynamic-slice_fusion.6 = bf16[1,4096,576]{1,2,0:T(8,128)(2,1)} fusion(bf16[4,4096,576]{1,2,0:T(8,128)(2,1)} %get-tuple-element.102, s32[]{:T(128)S(6)} %copy.24), kind=kLoop, calls=%fused_computation.19.clone.2 | loop fusion | bytes 9437188 | tf_op jit(solution)/shard_map/while/body/jit(dynamic_index_in_dim)/dynamic_slice | solution.py:52
  391.1 7.7 %copy.20 = bf16[1,4096,576]{2,1,0:T(8,128)(2,1)} copy(bf16[1,4096,576]{1,2,0:T(8,128)(2,1)} %constant_dynamic-slice_fusion.6) | data formatting | bytes 9437184 | tf_op jit(solution)/shard_map/while/body/jit(dynamic_index_in_dim)/dynamic_slice | solution.py:52
  398.8 0.6 dynamic_slice.55
  399.4 0.9 iota_compare_fusion.2
  400.3 3.6 fusion.34
  403.9 0.4 fusion.35
  404.4 0.8 fusion.36
  405.2 5.1 %constant_dynamic-slice_fusion.6 = bf16[1,4096,576]{1,2,0:T(8,128)(2,1)} fusion(bf16[4,4096,576]{1,2,0:T(8,128)(2,1)} %get-tuple-element.102, s32[]{:T(128)S(6)} %copy.24), kind=kLoop, calls=%fused_computation.19.clone.2 | loop fusion | bytes 9437188 | tf_op jit(solution)/shard_map/while/body/jit(dynamic_index_in_dim)/dynamic_slice | solution.py:52
  410.3 7.7 %copy.20 = bf16[1,4096,576]{2,1,0:T(8,128)(2,1)} copy(bf16[1,4096,576]{1,2,0:T(8,128)(2,1)} %constant_dynamic-slice_fusion.6) | data formatting | bytes 9437184 | tf_op jit(solution)/shard_map/while/body/jit(dynamic_index_in_dim)/dynamic_slice | solution.py:52
  417.9 0.6 dynamic_slice.55
  418.5 0.9 iota_compare_fusion.2
  419.5 3.6 fusion.34
  423.1 0.4 fusion.35
  423.5 0.8 fusion.36
  424.3 5.1 %constant_dynamic-slice_fusion.6 = bf16[1,4096,576]{1,2,0:T(8,128)(2,1)} fusion(bf16[4,4096,576]{1,2,0:T(8,128)(2,1)} %get-tuple-element.102, s32[]{:T(128)S(6)} %copy.24), kind=kLoop, calls=%fused_computation.19.clone.2 | loop fusion | bytes 9437188 | tf_op jit(solution)/shard_map/while/body/jit(dynamic_index_in_dim)/dynamic_slice | solution.py:52
  429.4 7.7 %copy.20 = bf16[1,4096,576]{2,1,0:T(8,128)(2,1)} copy(bf16[1,4096,576]{1,2,0:T(8,128)(2,1)} %constant_dynamic-slice_fusion.6) | data formatting | bytes 9437184 | tf_op jit(solution)/shard_map/while/body/jit(dynamic_index_in_dim)/dynamic_slice | solution.py:52
  437.1 0.6 dynamic_slice.55
  437.7 0.9 iota_compare_fusion.2
  438.6 3.6 fusion.34
  442.2 0.4 fusion.35
  442.7 0.8 fusion.36
  443.5 5.1 %constant_dynamic-slice_fusion.6 = bf16[1,4096,576]{1,2,0:T(8,128)(2,1)} fusion(bf16[4,4096,576]{1,2,0:T(8,128)(2,1)} %get-tuple-element.102, s32[]{:T(128)S(6)} %copy.24), kind=kLoop, calls=%fused_computation.19.clone.2 | loop fusion | bytes 9437188 | tf_op jit(solution)/shard_map/while/body/jit(dynamic_index_in_dim)/dynamic_slice | solution.py:52
  448.6 7.7 %copy.20 = bf16[1,4096,576]{2,1,0:T(8,128)(2,1)} copy(bf16[1,4096,576]{1,2,0:T(8,128)(2,1)} %constant_dynamic-slice_fusion.6) | data formatting | bytes 9437184 | tf_op jit(solution)/shard_map/while/body/jit(dynamic_index_in_dim)/dynamic_slice | solution.py:52
  456.2 0.6 dynamic_slice.55
  456.8 0.9 iota_compare_fusion.2
  457.8 3.6 fusion.34
  461.4 0.4 fusion.35
  461.8 0.8 fusion.36
  462.6 0.0 copy-start.5
  462.6 0.0 copy-start.1
  462.6 0.8 copy-done.5
  (22 shorter events, 0.1 us)
Async XLA Ops:
  0.0 168.9 %copy-start = (s32[4,64]{1,0:T(4,128)S(1)}, s32[4,64]{1,0:T(4,128)}, u32[]{:S(2)}) copy-start(s32[4,64]{1,0:T(4,128)} %param.14) | copy-start | bytes 3076
  151.7 15.5 %copy-start.3 = (bf16[1,4,128,576]{2,3,1,0:T(8,128)(2,1)S(1)}, bf16[1,4,128,576]{2,3,1,0:T(8,128)(2,1)}, u32[]{:S(2)}) copy-start(bf16[1,4,128,576]{2,3,1,0:T(8,128)(2,1)} %param.10) | copy-start | bytes 1769476
  151.7 17.9 %copy-start.4 = (s32[1,2]{1,0:T(1,128)S(1)}, s32[1,2]{1,0:T(1,128)}, u32[]{:S(2)}) copy-start(s32[1,2]{1,0:T(1,128)} %param.12) | copy-start | bytes 28
  166.6 203.0 %collective-permute-start = (bf16[2,4096,576]{1,2,0:T(8,128)(2,1)}, bf16[2,4096,576]{1,2,0:T(8,128)(2,1)}, u32[]{:S(2)}, u32[]{:S(2)}) collective-permute-start(bf16[2,4096,576]{1,2,0:T(8,128)(2,1)} %all_to_all.16), channel_id=1, source_target_pairs={{64,0},{96,32},{0,64},{32,96},{65,1},{97,33},{1,65},{33,97},{66,2}... | collective-permute-start | bytes 28311560 | tf_op jit(solution)/shard_map/ppermute | solution.py:15
  398.8 5.6 %copy-start.2 = (bf16[1,4096,576]{2,1,0:T(8,128)(2,1)S(1)}, bf16[1,4096,576]{2,1,0:T(8,128)(2,1)}, u32[]{:S(2)}) copy-start(bf16[1,4096,576]{2,1,0:T(8,128)(2,1)} %copy.20) | copy-start | bytes 14155780 | tf_op jit(solution)/shard_map/while
  417.9 5.6 %copy-start.2 = (bf16[1,4096,576]{2,1,0:T(8,128)(2,1)S(1)}, bf16[1,4096,576]{2,1,0:T(8,128)(2,1)}, u32[]{:S(2)}) copy-start(bf16[1,4096,576]{2,1,0:T(8,128)(2,1)} %copy.20) | copy-start | bytes 14155780 | tf_op jit(solution)/shard_map/while
  437.1 5.6 %copy-start.2 = (bf16[1,4096,576]{2,1,0:T(8,128)(2,1)S(1)}, bf16[1,4096,576]{2,1,0:T(8,128)(2,1)}, u32[]{:S(2)}) copy-start(bf16[1,4096,576]{2,1,0:T(8,128)(2,1)} %copy.20) | copy-start | bytes 14155780 | tf_op jit(solution)/shard_map/while
  456.2 5.6 %copy-start.2 = (bf16[1,4096,576]{2,1,0:T(8,128)(2,1)S(1)}, bf16[1,4096,576]{2,1,0:T(8,128)(2,1)}, u32[]{:S(2)}) copy-start(bf16[1,4096,576]{2,1,0:T(8,128)(2,1)} %copy.20) | copy-start | bytes 14155780 | tf_op jit(solution)/shard_map/while
  462.6 0.8 copy-start.5
  462.6 0.8 copy-start.1
where the time goes:
time: 465 us; the launch traced here: 463 us
  waiting for transfers between devices  200 us (43%)
  blocking collectives  119 us (26%)
  local copies, waits for them, and re-layouts  94.6 us (20%)
  other arithmetic  31.8 us (7%)
  matrix products  17.5 us (4%)
    ppermute x1, waiting for transfers between devices, from_behind(): return lax.ppermute(block, axis, route)  200 us
    all_to_all x1, blocking collectives, per_device(): lax.all_to_all(ordered, 'dev', split_axis=0, concat_axis=1, tiled=True)  119 us
    dynamic_slice x12, local copies, waits for them, and re-layouts, per_device(): result = lax.map(attend_items, (local_queries, all_caches, all_lengths))  53.4 us
    all_to_all x2, local copies, waits for them, and re-layouts, per_device(): lax.all_to_all(ordered, 'dev', split_axis=0, concat_axis=1, tiled=True)  28.3 us
    concatenate x1, other arithmetic, per_device(): all_caches = jnp.concatenate([res_cache[0], arrived], axis=0)  16.5 us
    dot_general x4, matrix products, attend(): jnp.dot(query_row, cache_rows.T, preferred_element_type=jnp.float32)  14.4 us
    gather x1, local copies, waits for them, and re-layouts, per_device(): ordered = jnp.take(inc_cache[0], own_match, axis=0)  9.79 us
  transfers between devices with their start and end apart: 1, of which 1 were waited for; matrix products, arithmetic and copies ran while one was open for 1% of the time, Pallas kernels for 0%

commit v1 on v0

v1 whole, which is shorter than its diff:
```python
import functools

import jax
import jax.numpy as jnp
from jax import lax
from jax.experimental import pallas as pl
from jax.experimental.pallas import tpu as pltpu
from jax.sharding import PartitionSpec as P

KV_RANK = 512
SCALE = 192.0 ** (-0.5)
DEAD = -1e30
RING = 4
STAT_ROWS = 16
AXES = ("section", "dev")
VMEM_LIMIT = 48 * 1024 * 1024


def place(x, z, y, core):
    section = (x % 2) * 2 + core
    dev = ((x % RING) // 2) * 16 + (z % RING) * 4 + (y % RING)
    return section * 32 + dev


def move(block, dx=0, dz=0, dy=0):
    route = [
        (place(x, z, y, core), place(x + dx, z + dz, y + dy, core))
        for x in range(RING)
        for z in range(RING)
        for y in range(RING)
        for core in range(2)
    ]
    return lax.ppermute(block, AXES, route)


def positions():
    section = lax.axis_index("section")
    dev = lax.axis_index("dev")
    x_hi, z, y = dev // 16, (dev // 4) % 4, dev % 4
    x_lo = section // 2
    hi_plus = jnp.where(x_lo == 0, x_hi, 1 - x_hi)
    return jnp.stack([section, x_hi, z, y, hi_plus, 1 - hi_plus]).astype(jnp.int32)


def request_of(meta, matching, half, side, cache_step, query_step):
    x_hi = meta[4 + side]
    if half == 0:
        z, y = (meta[2] + query_step) % RING, (meta[3] + cache_step) % RING
    else:
        z, y = (meta[2] + cache_step) % RING, (meta[3] + query_step) % RING
    return matching[meta[0], (x_hi * 16 + z * 4 + y) * 2 + half]


def gather_kernel(steps, meta, matching, cache, *rest):
    outs, sems = rest[:-1], rest[-1]
    copies = []
    slot = 0
    for out, (half, step) in zip(outs, steps):
        for query_step in range(RING):
            for side in range(2):
                request = request_of(meta, matching, half, side, step, query_step)
                copy = pltpu.make_async_copy(
                    cache.at[request], out.at[query_step * 2 + side], sems.at[slot]
                )
                copy.start()
                copies.append(copy)
                slot += 1
    for copy in copies:
        copy.wait()


def gather_requests(steps, meta, matching, cache):
    width, span = cache.shape[1:]
    shape = jax.ShapeDtypeStruct((2 * RING, width, span), cache.dtype)
    size = len(steps) * 2 * RING * width * span * 4
    return pl.pallas_call(
        functools.partial(gather_kernel, steps),
        out_shape=[shape] * len(steps),
        grid_spec=pltpu.PrefetchScalarGridSpec(
            num_scalar_prefetch=2,
            grid=(1,),
            in_specs=[pl.BlockSpec(memory_space=pl.ANY)],
            out_specs=[pl.BlockSpec(memory_space=pl.ANY)] * len(steps),
            scratch_shapes=[pltpu.SemaphoreType.DMA((len(steps) * 2 * RING,))],
        ),
        compiler_params=pltpu.CompilerParams(vmem_limit_bytes=VMEM_LIMIT),
        cost_estimate=pl.CostEstimate(flops=0, bytes_accessed=size, transcendentals=0),
        name="gather_requests",
    )(meta, matching, cache)


def attend_block(query, keys, live):
    scores = jnp.dot(query, keys, preferred_element_type=jnp.float32) * SCALE
    scores = jnp.where(live, scores, DEAD)
    top = jnp.max(scores, axis=1, keepdims=True)
    weights = jnp.exp(scores - top)
    total = jnp.sum(weights, axis=1, keepdims=True)
    mixed = lax.dot_general(
        weights.astype(jnp.bfloat16),
        keys[:KV_RANK],
        (((1,), (1,)), ((), ())),
        preferred_element_type=jnp.float32,
    )
    return mixed / total, top + jnp.log(total)


def resident_kernel(lengths, query, keys, out):
    item = pl.program_id(0)
    live = lax.broadcasted_iota(jnp.int32, (1, keys.shape[2]), 1) < lengths[item]
    mixed, _ = attend_block(query[0].T, keys[0], live)
    out[0] = mixed.astype(jnp.bfloat16)


def resident_rows(lengths, queries, cache):
    count, width, span = cache.shape
    heads = queries.shape[2]
    return pl.pallas_call(
        resident_kernel,
        out_shape=jax.ShapeDtypeStruct((queries.shape[0], heads, KV_RANK), jnp.bfloat16),
        grid_spec=pltpu.PrefetchScalarGridSpec(
            num_scalar_prefetch=1,
            grid=(count,),
            in_specs=[
                pl.BlockSpec((1, width, heads), lambda i, lengths: (i, 0, 0)),
                pl.BlockSpec((1, width, span), lambda i, lengths: (i, 0, 0)),
            ],
            out_specs=pl.BlockSpec((1, heads, KV_RANK), lambda i, lengths: (i, 0, 0)),
        ),
        compiler_params=pltpu.CompilerParams(vmem_limit_bytes=VMEM_LIMIT),
        cost_estimate=pl.CostEstimate(
            flops=2 * count * heads * span * (width + KV_RANK),
            bytes_accessed=2 * count * width * span,
            transcendentals=count * heads * span,
        ),
        name="resident_rows",
    )(lengths, queries, cache)


def split_stat(row):
    high = row.astype(jnp.bfloat16).astype(jnp.float32)
    rest = row - high
    middle = rest.astype(jnp.bfloat16).astype(jnp.float32)
    return high, middle, rest - middle


def put_stat(out, index, row):
    heads = row.shape[1]
    high, middle, low = split_stat(row)
    rows = lax.broadcasted_iota(jnp.int32, (STAT_ROWS, heads), 0)
    block = jnp.where(rows == 0, high, jnp.where(rows == 1, middle, jnp.where(rows == 2, low, 0.0)))
    out[index, heads:, :heads] = block.astype(jnp.bfloat16)
    out[index, heads:, heads:] = jnp.zeros((STAT_ROWS, KV_RANK - heads), jnp.bfloat16)


def partial_kernel(half, meta, matching, lengths, q0, q1, q2, q3, near_a, near_b, k1, k2, k3, o0, o1, o2, o3, query):
    query_step = pl.program_id(0)
    heads = query.shape[1]
    for step, source in enumerate((q0, q1, q2, q3)):

        @pl.when(query_step == step)
        def _():
            query[0] = source[0].T
            query[1] = source[1].T

    span = near_a.shape[2]
    lane = lax.broadcasted_iota(jnp.int32, (1, span), 1)
    slots = []
    for step in range(RING):
        z, y = meta[2], meta[3]
        if half == 0:
            y = (y + RING - step) % RING
        else:
            z = (z + RING - step) % RING
        slots.append(lane + (meta[1] * 16 + z * 4 + y) * span)
    slots = jnp.concatenate(slots, axis=1)
    results = []
    for side, near in enumerate((near_a, near_b)):
        request = request_of(meta, matching, half, side, 0, query_step)
        live = slots < lengths[meta[0], request]
        keys = jnp.concatenate([near[0], k1[side], k2[side], k3[side]], axis=1)
        mixed, stat = attend_block(query[side], keys, live)
        stat_row = jnp.broadcast_to(stat, (heads, heads)).T[:1]
        results.append((mixed.astype(jnp.bfloat16), stat_row))
    for step, out in enumerate((o0, o1, o2, o3)):

        @pl.when(query_step == step)
        def _():
            for side, (mixed, stat_row) in enumerate(results):
                out[side, :heads] = mixed
                put_stat(out, side, stat_row)


def partials(half, meta, matching, lengths, queries, cache, arrived):
    width, span = cache.shape[1:]
    heads = queries[0].shape[2]
    whole_query = pl.BlockSpec((2, width, heads), lambda i, *_: (0, 0, 0))

    def near(side):
        return pl.BlockSpec(
            (1, width, span),
            lambda i, meta, matching, lengths: (request_of(meta, matching, half, side, 0, i), 0, 0),
        )

    far = pl.BlockSpec((2, width, span), lambda i, *_: (i, 0, 0))
    out_block = pl.BlockSpec((2, heads + STAT_ROWS, KV_RANK), lambda i, *_: (0, 0, 0))
    shape = jax.ShapeDtypeStruct((2, heads + STAT_ROWS, KV_RANK), jnp.bfloat16)
    work = 2 * RING * heads * RING * span
    return pl.pallas_call(
        functools.partial(partial_kernel, half),
        out_shape=[shape] * RING,
        grid_spec=pltpu.PrefetchScalarGridSpec(
            num_scalar_prefetch=3,
            grid=(RING,),
            in_specs=[whole_query] * RING + [near(0), near(1)] + [far] * 3,
            out_specs=[out_block] * RING,
            scratch_shapes=[pltpu.VMEM((2, heads, width), jnp.bfloat16)],
        ),
        compiler_params=pltpu.CompilerParams(vmem_limit_bytes=VMEM_LIMIT),
        cost_estimate=pl.CostEstimate(
            flops=2 * work * (width + KV_RANK),
            bytes_accessed=2 * 2 * RING * RING * width * span,
            transcendentals=work,
        ),
        name="partials",
    )(meta, matching, lengths, *queries, cache, cache, *arrived)


def merge(parts):
    heads = parts[0].shape[0] - STAT_ROWS
    stats = []
    for part in parts:
        rows = part[heads:, :heads].astype(jnp.float32)
        stats.append(rows[0:1] + rows[1:2] + rows[2:3])
    top = functools.reduce(jnp.maximum, stats)
    shares = [jnp.exp(stat - top) for stat in stats]
    total = functools.reduce(jnp.add, shares)
    mixed = 0.0
    for part, share in zip(parts, shares):
        column = jnp.broadcast_to(share / total, (heads, heads)).T[:, :1]
        mixed = mixed + part[:heads].astype(jnp.float32) * column
    return mixed, top + jnp.log(total)


def middle_kernel(*refs):
    ins, outs = refs[: 2 * RING], refs[2 * RING :]
    heads = ins[0].shape[1] - STAT_ROWS
    for half in range(2):
        for side in range(2):
            mixed, stat_row = merge([ref[side] for ref in ins[half * RING : (half + 1) * RING]])
            outs[side][half, :heads] = mixed.astype(jnp.bfloat16)
            put_stat(outs[side], half, stat_row)


def middle(parts):
    shape = jax.ShapeDtypeStruct(parts[0].shape, parts[0].dtype)
    return pl.pallas_call(
        middle_kernel,
        out_shape=[shape] * 2,
        compiler_params=pltpu.CompilerParams(vmem_limit_bytes=VMEM_LIMIT),
        name="middle",
    )(*parts)


def last_kernel(base, plus, minus, out):
    del base
    for half in range(2):
        mixed, _ = merge([plus[half], minus[half]])
        out[half] = mixed.astype(jnp.bfloat16)


def last(base, plus, minus):
    count, heads, rank = base.shape
    whole = pl.BlockSpec(plus.shape, lambda i: (0, 0, 0))
    return pl.pallas_call(
        last_kernel,
        out_shape=jax.ShapeDtypeStruct(base.shape, base.dtype),
        grid=(1,),
        in_specs=[pl.BlockSpec(memory_space=pl.ANY), whole, whole],
        out_specs=pl.BlockSpec((count // 2, heads, rank), lambda i: (1, 0, 0)),
        input_output_aliases={0: 0},
        compiler_params=pltpu.CompilerParams(vmem_limit_bytes=VMEM_LIMIT),
        name="last",
    )(base, plus, minus)


def per_device(queries, res_cache, res_lengths, inc_cache, inc_lengths, matching):
    meta = positions()
    queries = jnp.swapaxes(queries[0], 1, 2)
    res_cache = jnp.swapaxes(res_cache[0], 1, 2)
    inc_cache = jnp.swapaxes(inc_cache[0], 1, 2)

    handed = queries[2:]
    from_minus = move(handed, dx=1)
    from_plus = move(handed, dx=-1)

    a1, a3, b1, b3 = gather_requests(((0, 1), (0, 3), (1, 1), (1, 3)), meta, matching, inc_cache)
    a2, b2 = gather_requests(((0, 2), (1, 2)), meta, matching, inc_cache)
    a1 = move(a1, dy=1)
    b1 = move(b1, dz=1)
    a3 = move(a3, dy=-1)
    b3 = move(b3, dz=-1)
    a2 = move(a2, dy=2)
    b2 = move(b2, dz=2)

    qa = jnp.stack([from_plus[0], from_minus[0]])
    qb = jnp.stack([from_plus[1], from_minus[1]])
    qa_all = [qa] + [move(qa, dz=-step) for step in (1, 2, 3)]
    qb_all = [qb] + [move(qb, dy=-step) for step in (1, 2, 3)]

    base = resident_rows(res_lengths[0], queries, res_cache)

    pa = partials(0, meta, matching, inc_lengths, qa_all, inc_cache, (a1, a2, a3))
    pb = partials(1, meta, matching, inc_lengths, qb_all, inc_cache, (b1, b2, b3))
    pa = [pa[0]] + [move(pa[step], dz=step) for step in (1, 2, 3)]
    pb = [pb[0]] + [move(pb[step], dy=step) for step in (1, 2, 3)]
    to_plus, to_minus = middle(pa + pb)
    plus = move(to_plus, dx=1)
    minus = move(to_minus, dx=-1)
    return last(base, plus, minus)[None]


def solution(mesh):
    placed = (
        P("section", "dev", None, None),
        P("section", "dev", None, None),
        P("section", "dev"),
        P("section", None, "dev", None),
        P(),
        P(),
    )
    return jax.shard_map(
        per_device,
        mesh=mesh,
        in_specs=placed,
        out_specs=P("section", "dev", None, None),
        check_vma=False,
    )
```

time: 465 us -> 185 us (0.40)
  blocking collectives: 119 us -> 0 us
  waiting for transfers between devices: 200 us -> 83 us
  local copies, waits for them, and re-layouts: 94.6 us -> 1.8 us
  Pallas kernels: 0 us -> 65.3 us
  starting transfers between devices: 0.63 us -> 33.2 us
  other arithmetic: 31.8 us -> 0.06 us
  matrix products: 17.5 us -> 0 us
    all_to_all x1 -> x0, blocking collectives: 119 us -> none  [per_device(): lax.all_to_all(ordered, 'dev', split_axis=0, concat_axis=1, tiled=True)]
    ppermute x1 -> x22, waiting for transfers between devices: 200 us -> 83 us  [move(): return lax.ppermute(block, AXES, route)]
    pallas_call x0 -> x7, Pallas kernels: none -> 65.3 us  [the longest x2 40.9 us: gather_requests(): pl.pallas_call(functools.partial(gather_kernel, steps), out_shape=[shape]...]
    dynamic_slice x12 -> x0, local copies, waits for them, and re-layouts: 53.4 us -> none  [per_device(): result = lax.map(attend_items, (local_queries, all_caches, all_lengths))]
    ppermute x1 -> x22, starting transfers between devices: 0.63 us -> 33.2 us  [move(): return lax.ppermute(block, AXES, route)]
    all_to_all x2 -> x0, local copies, waits for them, and re-layouts: 28.3 us -> none  [per_device(): lax.all_to_all(ordered, 'dev', split_axis=0, concat_axis=1, tiled=True)]
    dot_general x8 -> x0, matrix products: 17.5 us -> none  [the longest x4 14.4 us: attend(): jnp.dot(query_row, cache_rows.T, preferred_element_type=jnp.float32)]
    concatenate x2 -> x0, other arithmetic: 16.6 us -> none  [the longest x1 16.5 us: per_device(): all_caches = jnp.concatenate([res_cache[0], arrived], axis=0)]
  transfers between devices with their start and end apart: 1 -> 22, of which waited for: 1 -> 9; matrix products, arithmetic and copies ran while one was open for 1% -> 0% of each run, Pallas kernels for 0% -> 35%
where the time goes in v1:
time: 185 us; the launch traced here: 183 us
  waiting for transfers between devices  83 us (45%)
  Pallas kernels  65.3 us (35%)
  starting transfers between devices  33.2 us (18%)
    ppermute x22, waiting for transfers between devices, move(): return lax.ppermute(block, AXES, route)  83 us
    pallas_call x2, Pallas kernels, gather_requests(): pl.pallas_call(functools.partial(gather_kernel, steps), out_shape=[shape]...  40.9 us
    ppermute x22, starting transfers between devices, move(): return lax.ppermute(block, AXES, route)  33.2 us
    pallas_call x2, Pallas kernels, partials(): pl.pallas_call(functools.partial(partial_kernel, half), out_shape=[shape]...  13.4 us
    pallas_call x1, Pallas kernels, resident_rows(): pl.pallas_call(resident_kernel, out_shape=jax.ShapeDtypeStruct((queries.s...  9.1 us
  transfers between devices with their start and end apart: 22, of which 9 were waited for; matrix products, arithmetic and copies ran while one was open for 0% of the time, Pallas kernels for 35%

profile of v1, /device:TPU:0, one launch (start us, length us, event | category | flops | bytes accessed | tf_op | source)
XLA Modules:
  0.0 183.4 jit_solution(4917969733990243887)
XLA Ops:
  0.0 1.0 slice.20
  1.0 2.9 %collective-permute-start = (bf16[2,576,128]{2,1,0:T(8,128)(2,1)S(1)}, bf16[2,576,128]{2,1,0:T(8,128)(2,1)S(1)}, u32[]{:S(2)}, u32[]{:S(2)}) collective-permute-start(bf16[2,576,128]{2,1,0:T(8,128)(2,1)S(1)} %slice.20), channel_id=1, source_target_pairs={{0,80},{32,112},{1,81},{33,113},{2,82},{34,114},{3,83},{35,115},{4... | collective-permute-start | bytes 884744 | tf_op jit(solution)/shard_map/ppermute | solution.py:33
  3.9 0.0 collective-permute-start.1
  3.9 0.1 stack.33.meta
  4.0 0.7 copy-done.1
  4.7 3.3 %gather_requests.2 = (bf16[8,576,128]{2,1,0:T(8,128)(2,1)S(1)}, bf16[8,576,128]{2,1,0:T(8,128)(2,1)S(1)}, bf16[8,576,128]{2,1,0:T(8,128)(2,1)S(1)}, bf16[8,576,128]{2,1,0:T(8,128)(2,1)S(1)}) custom-call(s32[6]{0:T(128)S(1)} %stack.33.meta, s32[4,64]{1,0:T(4,128)S(1)} %copy-done.1, bf16[64,576,128]{2,1,0:T(8,128)(2,1)} %bitcast.20), custom_call_target="tpu_custom_call" | custom-call | bytes 9437184 | tf_op jit(solution)/shard_map/gather_requests/pallas_call | solution.py:76
  8.0 2.0 %collective-permute-start.14 = (bf16[8,576,128]{2,1,0:T(8,128)(2,1)S(1)}, bf16[8,576,128]{2,1,0:T(8,128)(2,1)S(1)}, u32[]{:S(2)}, u32[]{:S(2)}) collective-permute-start(bf16[8,576,128]{2,1,0:T(8,128)(2,1)S(1)} %get-tuple-element.28), channel_id=1, source_target_pairs={{0,4},{32,36},{1,5},{33,37},{2,6},{34,38},{3,7},{35,39},{4,8},{36,... | collective-permute-start | bytes 3538952 | tf_op jit(solution)/shard_map/ppermute | solution.py:33
  10.0 0.2 collective-permute-done
  10.2 3.4 %collective-permute-done.1 = bf16[2,576,128]{2,1,0:T(8,128)(2,1)S(1)} collective-permute-done((bf16[2,576,128]{2,1,0:T(8,128)(2,1)S(1)}, bf16[2,576,128]{2,1,0:T(8,128)(2,1)S(1)}, u32[]{:S(2)}, u32[]{:S(2)}) %collective-permute-start.1) | collective-permute-done | bytes 294944 | tf_op jit(solution)/shard_map/ppermute | solution.py:33
  13.6 3.1 %collective-permute-start.11 = (bf16[2,576,128]{2,1,0:T(8,128)(2,1)S(1)}, bf16[2,576,128]{2,1,0:T(8,128)(2,1)S(1)}, u32[]{:S(2)}, u32[]{:S(2)}) collective-permute-start(bf16[2,576,128]{2,1,0:T(8,128)(2,1)S(1)} %pad_maximum_fusion.1.q0), channel_id=1, source_target_pairs={{0,3},{32,35},{1,0},{33,32},{2,1},{34,33},{3,2},{35,34},{4,7},{36,... | collective-permute-start | bytes 884744 | tf_op jit(solution)/shard_map/ppermute | solution.py:33
  16.7 0.6 collective-permute-start.12
  17.4 4.0 %collective-permute-start.16 = (bf16[8,576,128]{2,1,0:T(8,128)(2,1)S(1)}, bf16[8,576,128]{2,1,0:T(8,128)(2,1)S(1)}, u32[]{:S(2)}, u32[]{:S(2)}) collective-permute-start(bf16[8,576,128]{2,1,0:T(8,128)(2,1)S(1)} %get-tuple-element.30), channel_id=1, source_target_pairs={{0,12},{32,44},{1,13},{33,45},{2,14},{34,46},{3,15},{35,47},{4,0},... | collective-permute-start | bytes 3538952 | tf_op jit(solution)/shard_map/ppermute | solution.py:33
  21.4 37.6 %gather_requests.3 = (bf16[8,576,128]{2,1,0:T(8,128)(2,1)S(1)}, bf16[8,576,128]{2,1,0:T(8,128)(2,1)}) custom-call(s32[6]{0:T(128)S(1)} %stack.33.meta, s32[4,64]{1,0:T(4,128)S(1)} %copy-done.1, bf16[64,576,128]{2,1,0:T(8,128)(2,1)} %bitcast.21), custom_call_target="tpu_custom_call" | custom-call | bytes 4718592 | tf_op jit(solution)/shard_map/gather_requests/pallas_call | solution.py:76
  59.0 0.1 collective-permute-start.15
  59.1 1.0 collective-permute-start.13
  60.2 0.0 collective-permute-done.12.q2
  60.2 0.6 collective-permute-start.2
  60.8 6.3 %collective-permute-done.13.q3 = bf16[2,576,128]{2,1,0:T(8,128)(2,1)S(1)} collective-permute-done((bf16[2,576,128]{2,1,0:T(8,128)(2,1)S(1)}, bf16[2,576,128]{2,1,0:T(8,128)(2,1)S(1)}, u32[]{:S(2)}, u32[]{:S(2)}) %collective-permute-start.13) | collective-permute-done | bytes 294944 | tf_op jit(solution)/shard_map/ppermute | solution.py:33
  67.1 0.0 collective-permute-start.5
  67.1 23.5 %collective-permute-done.2.q1 = bf16[2,576,128]{2,1,0:T(8,128)(2,1)S(1)} collective-permute-done((bf16[2,576,128]{2,1,0:T(8,128)(2,1)S(1)}, bf16[2,576,128]{2,1,0:T(8,128)(2,1)S(1)}, u32[]{:S(2)}, u32[]{:S(2)}) %collective-permute-start.2) | collective-permute-done | bytes 294944 | tf_op jit(solution)/shard_map/ppermute | solution.py:33
  90.6 1.1 collective-permute-start.7
  91.6 0.0 collective-permute-done.14.k1
  91.6 2.0 %collective-permute-start.6 = (bf16[8,576,128]{2,1,0:T(8,128)(2,1)S(1)}, bf16[8,576,128]{2,1,0:T(8,128)(2,1)S(1)}, u32[]{:S(2)}, u32[]{:S(2)}) collective-permute-start(bf16[8,576,128]{2,1,0:T(8,128)(2,1)S(1)} %get-tuple-element.22), channel_id=1, source_target_pairs={{0,2},{32,34},{1,3},{33,35},{2,0},{34,32},{3,1},{35,33},{4,6},{36,... | collective-permute-start | bytes 3538952 | tf_op jit(solution)/shard_map/ppermute | solution.py:33
  93.6 0.0 collective-permute-done.16.k3
  93.6 1.0 collective-permute-start.3
  94.7 2.4 %collective-permute-start.4 = (bf16[2,576,128]{2,1,0:T(8,128)(2,1)S(1)}, bf16[2,576,128]{2,1,0:T(8,128)(2,1)S(1)}, u32[]{:S(2)}, u32[]{:S(2)}) collective-permute-start(bf16[2,576,128]{2,1,0:T(8,128)(2,1)S(1)} %pad_maximum_fusion.q0), channel_id=1, source_target_pairs={{0,4},{32,36},{1,5},{33,37},{2,6},{34,38},{3,7},{35,39},{4,8},{36,... | collective-permute-start | bytes 884744 | tf_op jit(solution)/shard_map/ppermute | solution.py:33
  97.1 6.7 %partials.3 = (bf16[2,144,512]{2,1,0:T(8,128)(2,1)S(1)}, bf16[2,144,512]{2,1,0:T(8,128)(2,1)S(1)}, bf16[2,144,512]{2,1,0:T(8,128)(2,1)S(1)}, bf16[2,144,512]{2,1,0:T(8,128)(2,1)S(1)}) custom-call(s32[6]{0:T(128)S(1)} %stack.33.meta, s32[4,64]{1,0:T(4,128)S(1)} %copy-done.1, s32[4,64]{1,0:T(4,128)S(1)} %copy-done.2, ...), custom_call_target="tpu_custom_call" | custom-call | flops 1140850688 | bytes 4718592 | tf_op jit(solution)/shard_map/partials/pallas_call | solution.py:208
  103.8 1.3 collective-permute-done.3.q2
  105.1 1.3 collective-permute-start.17
  106.3 2.4 %collective-permute-done.4.q3 = bf16[2,576,128]{2,1,0:T(8,128)(2,1)S(1)} collective-permute-done((bf16[2,576,128]{2,1,0:T(8,128)(2,1)S(1)}, bf16[2,576,128]{2,1,0:T(8,128)(2,1)S(1)}, u32[]{:S(2)}, u32[]{:S(2)}) %collective-permute-start.4) | collective-permute-done | bytes 294944 | tf_op jit(solution)/shard_map/ppermute | solution.py:33
  108.7 1.5 collective-permute-start.18
  110.3 0.0 collective-permute-done.5.k1
  110.3 1.9 %collective-permute-start.19 = (bf16[2,144,512]{2,1,0:T(8,128)(2,1)S(1)}, bf16[2,144,512]{2,1,0:T(8,128)(2,1)S(1)}, u32[]{:S(2)}, u32[]{:S(2)}) collective-permute-start(bf16[2,144,512]{2,1,0:T(8,128)(2,1)S(1)} %get-tuple-element.34), channel_id=1, source_target_pairs={{0,3},{32,35},{1,0},{33,32},{2,1},{34,33},{3,2},{35,34},{4,7},{36,... | collective-permute-start | bytes 884744 | tf_op jit(solution)/shard_map/ppermute | solution.py:33
  112.2 36.5 %collective-permute-done.7.k3 = bf16[8,576,128]{2,1,0:T(8,128)(2,1)S(1)} collective-permute-done((bf16[8,576,128]{2,1,0:T(8,128)(2,1)S(1)}, bf16[8,576,128]{2,1,0:T(8,128)(2,1)S(1)}, u32[]{:S(2)}, u32[]{:S(2)}) %collective-permute-start.7) | collective-permute-done | bytes 1179680 | tf_op jit(solution)/shard_map/ppermute | solution.py:33
  148.7 0.0 collective-permute-done.6.k2
  148.7 6.7 %partials.2 = (bf16[2,144,512]{2,1,0:T(8,128)(2,1)S(1)}, bf16[2,144,512]{2,1,0:T(8,128)(2,1)S(1)}, bf16[2,144,512]{2,1,0:T(8,128)(2,1)S(1)}, bf16[2,144,512]{2,1,0:T(8,128)(2,1)S(1)}) custom-call(s32[6]{0:T(128)S(1)} %stack.33.meta, s32[4,64]{1,0:T(4,128)S(1)} %copy-done.1, s32[4,64]{1,0:T(4,128)S(1)} %copy-done.2, ...), custom_call_target="tpu_custom_call" | custom-call | flops 1140850688 | bytes 4718592 | tf_op jit(solution)/shard_map/partials/pallas_call | solution.py:208
  155.4 2.6 %collective-permute-start.10 = (bf16[2,144,512]{2,1,0:T(8,128)(2,1)S(1)}, bf16[2,144,512]{2,1,0:T(8,128)(2,1)S(1)}, u32[]{:S(2)}, u32[]{:S(2)}) collective-permute-start(bf16[2,144,512]{2,1,0:T(8,128)(2,1)S(1)} %get-tuple-element.27), channel_id=1, source_target_pairs={{0,12},{32,44},{1,13},{33,45},{2,14},{34,46},{3,15},{35,47},{4,0},... | collective-permute-start | bytes 884744 | tf_op jit(solution)/shard_map/ppermute | solution.py:33
  158.0 0.0 collective-permute-start.8
  158.0 0.0 collective-permute-done.17.refs_5_
  158.0 1.5 collective-permute-start.9
  159.6 0.0 collective-permute-done.18.refs_6_
  159.6 2.7 %collective-permute-done.10.refs_3_ = bf16[2,144,512]{2,1,0:T(8,128)(2,1)S(1)} collective-permute-done((bf16[2,144,512]{2,1,0:T(8,128)(2,1)S(1)}, bf16[2,144,512]{2,1,0:T(8,128)(2,1)S(1)}, u32[]{:S(2)}, u32[]{:S(2)}) %collective-permute-start.10) | collective-permute-done | bytes 294944 | tf_op jit(solution)/shard_map/ppermute | solution.py:33
  162.3 6.9 %collective-permute-done.8.refs_1_ = bf16[2,144,512]{2,1,0:T(8,128)(2,1)S(1)} collective-permute-done((bf16[2,144,512]{2,1,0:T(8,128)(2,1)S(1)}, bf16[2,144,512]{2,1,0:T(8,128)(2,1)S(1)}, u32[]{:S(2)}, u32[]{:S(2)}) %collective-permute-start.8) | collective-permute-done | bytes 294944 | tf_op jit(solution)/shard_map/ppermute | solution.py:33
  169.1 0.8 middle.1
  170.0 0.1 collective-permute-start.20
  170.1 3.2 %collective-permute-start.21 = (bf16[2,144,512]{2,1,0:T(8,128)(2,1)S(1)}, bf16[2,144,512]{2,1,0:T(8,128)(2,1)S(1)}, u32[]{:S(2)}, u32[]{:S(2)}) collective-permute-start(bf16[2,144,512]{2,1,0:T(8,128)(2,1)S(1)} %get-tuple-element.36), channel_id=1, source_target_pairs={{0,80},{32,112},{1,81},{33,113},{2,82},{34,114},{3,83},{35,115},{4... | collective-permute-start | bytes 884744 | tf_op jit(solution)/shard_map/ppermute | solution.py:33
  173.3 9.1 %resident_rows.1.base = bf16[4,128,512]{2,1,0:T(8,128)(2,1)} custom-call(s32[2]{0:T(128)S(1)} %bitcast.19, bf16[4,576,128]{2,1,0:T(8,128)(2,1)S(1)} %bitcast.18, bf16[2,576,4096]{2,1,0:T(8,128)(2,1)} %bitcast.26), custom_call_target="tpu_custom_call" | custom-call | flops 2281701376 | bytes 9437184 | tf_op jit(solution)/shard_map/resident_rows/pallas_call | solution.py:117
  182.4 1.0 last.1
  (17 shorter events, 0.1 us)
Async XLA Ops:
  1.0 9.2 %collective-permute-start = (bf16[2,576,128]{2,1,0:T(8,128)(2,1)S(1)}, bf16[2,576,128]{2,1,0:T(8,128)(2,1)S(1)}, u32[]{:S(2)}, u32[]{:S(2)}) collective-permute-start(bf16[2,576,128]{2,1,0:T(8,128)(2,1)S(1)} %slice.20), channel_id=1, source_target_pairs={{0,80},{32,112},{1,81},{33,113},{2,82},{34,114},{3,83},{35,115},{4... | collective-permute-start | bytes 884744 | tf_op jit(solution)/shard_map/ppermute | solution.py:33
  3.9 9.7 %collective-permute-start.1 = (bf16[2,576,128]{2,1,0:T(8,128)(2,1)S(1)}, bf16[2,576,128]{2,1,0:T(8,128)(2,1)S(1)}, u32[]{:S(2)}, u32[]{:S(2)}) collective-permute-start(bf16[2,576,128]{2,1,0:T(8,128)(2,1)S(1)} %slice.20), channel_id=1, source_target_pairs={{0,64},{32,96},{1,65},{33,97},{2,66},{34,98},{3,67},{35,99},{4,68}... | collective-permute-start | bytes 884744 | tf_op jit(solution)/shard_map/ppermute | solution.py:33
  4.0 0.7 copy-start.1
  8.0 83.6 %collective-permute-start.14 = (bf16[8,576,128]{2,1,0:T(8,128)(2,1)S(1)}, bf16[8,576,128]{2,1,0:T(8,128)(2,1)S(1)}, u32[]{:S(2)}, u32[]{:S(2)}) collective-permute-start(bf16[8,576,128]{2,1,0:T(8,128)(2,1)S(1)} %get-tuple-element.28), channel_id=1, source_target_pairs={{0,4},{32,36},{1,5},{33,37},{2,6},{34,38},{3,7},{35,39},{4,8},{36,... | collective-permute-start | bytes 3538952 | tf_op jit(solution)/shard_map/ppermute | solution.py:33
  13.6 45.5 %collective-permute-start.11 = (bf16[2,576,128]{2,1,0:T(8,128)(2,1)S(1)}, bf16[2,576,128]{2,1,0:T(8,128)(2,1)S(1)}, u32[]{:S(2)}, u32[]{:S(2)}) collective-permute-start(bf16[2,576,128]{2,1,0:T(8,128)(2,1)S(1)} %pad_maximum_fusion.1.q0), channel_id=1, source_target_pairs={{0,3},{32,35},{1,0},{33,32},{2,1},{34,33},{3,2},{35,34},{4,7},{36,... | collective-permute-start | bytes 884744 | tf_op jit(solution)/shard_map/ppermute | solution.py:33
  16.7 43.5 %collective-permute-start.12 = (bf16[2,576,128]{2,1,0:T(8,128)(2,1)S(1)}, bf16[2,576,128]{2,1,0:T(8,128)(2,1)S(1)}, u32[]{:S(2)}, u32[]{:S(2)}) collective-permute-start(bf16[2,576,128]{2,1,0:T(8,128)(2,1)S(1)} %pad_maximum_fusion.1.q0), channel_id=1, source_target_pairs={{0,2},{32,34},{1,3},{33,35},{2,0},{34,32},{3,1},{35,33},{4,6},{36,... | collective-permute-start | bytes 884744 | tf_op jit(solution)/shard_map/ppermute | solution.py:33
  17.4 79.8 %copy-start.2 = (s32[4,64]{1,0:T(4,128)S(1)}, s32[4,64]{1,0:T(4,128)}, u32[]{:S(2)}) copy-start(s32[4,64]{1,0:T(4,128)} %lengths.3) | copy-start | bytes 3076
  17.4 76.3 %collective-permute-start.16 = (bf16[8,576,128]{2,1,0:T(8,128)(2,1)S(1)}, bf16[8,576,128]{2,1,0:T(8,128)(2,1)S(1)}, u32[]{:S(2)}, u32[]{:S(2)}) collective-permute-start(bf16[8,576,128]{2,1,0:T(8,128)(2,1)S(1)} %get-tuple-element.30), channel_id=1, source_target_pairs={{0,12},{32,44},{1,13},{33,45},{2,14},{34,46},{3,15},{35,47},{4,0},... | collective-permute-start | bytes 3538952 | tf_op jit(solution)/shard_map/ppermute | solution.py:33
  59.0 35.7 %collective-permute-start.15 = (bf16[8,576,128]{2,1,0:T(8,128)(2,1)}, bf16[8,576,128]{2,1,0:T(8,128)(2,1)S(1)}, u32[]{:S(2)}, u32[]{:S(2)}) collective-permute-start(bf16[8,576,128]{2,1,0:T(8,128)(2,1)} %get-tuple-element.29), channel_id=1, source_target_pairs={{0,8},{32,40},{1,9},{33,41},{2,10},{34,42},{3,11},{35,43},{4,12},{... | collective-permute-start | bytes 3538952 | tf_op jit(solution)/shard_map/ppermute | solution.py:33
  59.1 8.0 %collective-permute-start.13 = (bf16[2,576,128]{2,1,0:T(8,128)(2,1)S(1)}, bf16[2,576,128]{2,1,0:T(8,128)(2,1)S(1)}, u32[]{:S(2)}, u32[]{:S(2)}) collective-permute-start(bf16[2,576,128]{2,1,0:T(8,128)(2,1)S(1)} %pad_maximum_fusion.1.q0), channel_id=1, source_target_pairs={{0,1},{32,33},{1,2},{33,34},{2,3},{34,35},{3,0},{35,32},{4,5},{36,... | collective-permute-start | bytes 884744 | tf_op jit(solution)/shard_map/ppermute | solution.py:33
  60.2 30.4 %collective-permute-start.2 = (bf16[2,576,128]{2,1,0:T(8,128)(2,1)S(1)}, bf16[2,576,128]{2,1,0:T(8,128)(2,1)S(1)}, u32[]{:S(2)}, u32[]{:S(2)}) collective-permute-start(bf16[2,576,128]{2,1,0:T(8,128)(2,1)S(1)} %pad_maximum_fusion.q0), channel_id=1, source_target_pairs={{0,12},{32,44},{1,13},{33,45},{2,14},{34,46},{3,15},{35,47},{4,0},... | collective-permute-start | bytes 884744 | tf_op jit(solution)/shard_map/ppermute | solution.py:33
  67.1 43.2 %collective-permute-start.5 = (bf16[8,576,128]{2,1,0:T(8,128)(2,1)S(1)}, bf16[8,576,128]{2,1,0:T(8,128)(2,1)S(1)}, u32[]{:S(2)}, u32[]{:S(2)}) collective-permute-start(bf16[8,576,128]{2,1,0:T(8,128)(2,1)S(1)} %get-tuple-element.21), channel_id=1, source_target_pairs={{0,1},{32,33},{1,2},{33,34},{2,3},{34,35},{3,0},{35,32},{4,5},{36,... | collective-permute-start | bytes 3538952 | tf_op jit(solution)/shard_map/ppermute | solution.py:33
  90.6 58.1 %collective-permute-start.7 = (bf16[8,576,128]{2,1,0:T(8,128)(2,1)S(1)}, bf16[8,576,128]{2,1,0:T(8,128)(2,1)S(1)}, u32[]{:S(2)}, u32[]{:S(2)}) collective-permute-start(bf16[8,576,128]{2,1,0:T(8,128)(2,1)S(1)} %get-tuple-element.23), channel_id=1, source_target_pairs={{0,3},{32,35},{1,0},{33,32},{2,1},{34,33},{3,2},{35,34},{4,7},{36,... | collective-permute-start | bytes 3538952 | tf_op jit(solution)/shard_map/ppermute | solution.py:33
  91.6 57.1 %collective-permute-start.6 = (bf16[8,576,128]{2,1,0:T(8,128)(2,1)S(1)}, bf16[8,576,128]{2,1,0:T(8,128)(2,1)S(1)}, u32[]{:S(2)}, u32[]{:S(2)}) collective-permute-start(bf16[8,576,128]{2,1,0:T(8,128)(2,1)S(1)} %get-tuple-element.22), channel_id=1, source_target_pairs={{0,2},{32,34},{1,3},{33,35},{2,0},{34,32},{3,1},{35,33},{4,6},{36,... | collective-permute-start | bytes 3538952 | tf_op jit(solution)/shard_map/ppermute | solution.py:33
  93.6 11.5 %collective-permute-start.3 = (bf16[2,576,128]{2,1,0:T(8,128)(2,1)S(1)}, bf16[2,576,128]{2,1,0:T(8,128)(2,1)S(1)}, u32[]{:S(2)}, u32[]{:S(2)}) collective-permute-start(bf16[2,576,128]{2,1,0:T(8,128)(2,1)S(1)} %pad_maximum_fusion.q0), channel_id=1, source_target_pairs={{0,8},{32,40},{1,9},{33,41},{2,10},{34,42},{3,11},{35,43},{4,12},{... | collective-permute-start | bytes 884744 | tf_op jit(solution)/shard_map/ppermute | solution.py:33
  94.7 14.1 %collective-permute-start.4 = (bf16[2,576,128]{2,1,0:T(8,128)(2,1)S(1)}, bf16[2,576,128]{2,1,0:T(8,128)(2,1)S(1)}, u32[]{:S(2)}, u32[]{:S(2)}) collective-permute-start(bf16[2,576,128]{2,1,0:T(8,128)(2,1)S(1)} %pad_maximum_fusion.q0), channel_id=1, source_target_pairs={{0,4},{32,36},{1,5},{33,37},{2,6},{34,38},{3,7},{35,39},{4,8},{36,... | collective-permute-start | bytes 884744 | tf_op jit(solution)/shard_map/ppermute | solution.py:33
  105.1 53.0 %collective-permute-start.17 = (bf16[2,144,512]{2,1,0:T(8,128)(2,1)S(1)}, bf16[2,144,512]{2,1,0:T(8,128)(2,1)S(1)}, u32[]{:S(2)}, u32[]{:S(2)}) collective-permute-start(bf16[2,144,512]{2,1,0:T(8,128)(2,1)S(1)} %get-tuple-element.32), channel_id=1, source_target_pairs={{0,1},{32,33},{1,2},{33,34},{2,3},{34,35},{3,0},{35,32},{4,5},{36,... | collective-permute-start | bytes 884744 | tf_op jit(solution)/shard_map/ppermute | solution.py:33
  108.7 50.8 %collective-permute-start.18 = (bf16[2,144,512]{2,1,0:T(8,128)(2,1)S(1)}, bf16[2,144,512]{2,1,0:T(8,128)(2,1)S(1)}, u32[]{:S(2)}, u32[]{:S(2)}) collective-permute-start(bf16[2,144,512]{2,1,0:T(8,128)(2,1)S(1)} %get-tuple-element.33), channel_id=1, source_target_pairs={{0,2},{32,34},{1,3},{33,35},{2,0},{34,32},{3,1},{35,33},{4,6},{36,... | collective-permute-start | bytes 884744 | tf_op jit(solution)/shard_map/ppermute | solution.py:33
  110.3 49.3 %collective-permute-start.19 = (bf16[2,144,512]{2,1,0:T(8,128)(2,1)S(1)}, bf16[2,144,512]{2,1,0:T(8,128)(2,1)S(1)}, u32[]{:S(2)}, u32[]{:S(2)}) collective-permute-start(bf16[2,144,512]{2,1,0:T(8,128)(2,1)S(1)} %get-tuple-element.34), channel_id=1, source_target_pairs={{0,3},{32,35},{1,0},{33,32},{2,1},{34,33},{3,2},{35,34},{4,7},{36,... | collective-permute-start | bytes 884744 | tf_op jit(solution)/shard_map/ppermute | solution.py:33
  155.4 6.9 %collective-permute-start.10 = (bf16[2,144,512]{2,1,0:T(8,128)(2,1)S(1)}, bf16[2,144,512]{2,1,0:T(8,128)(2,1)S(1)}, u32[]{:S(2)}, u32[]{:S(2)}) collective-permute-start(bf16[2,144,512]{2,1,0:T(8,128)(2,1)S(1)} %get-tuple-element.27), channel_id=1, source_target_pairs={{0,12},{32,44},{1,13},{33,45},{2,14},{34,46},{3,15},{35,47},{4,0},... | collective-permute-start | bytes 884744 | tf_op jit(solution)/shard_map/ppermute | solution.py:33
  158.0 11.1 %collective-permute-start.8 = (bf16[2,144,512]{2,1,0:T(8,128)(2,1)S(1)}, bf16[2,144,512]{2,1,0:T(8,128)(2,1)S(1)}, u32[]{:S(2)}, u32[]{:S(2)}) collective-permute-start(bf16[2,144,512]{2,1,0:T(8,128)(2,1)S(1)} %get-tuple-element.25), channel_id=1, source_target_pairs={{0,4},{32,36},{1,5},{33,37},{2,6},{34,38},{3,7},{35,39},{4,8},{36,... | collective-permute-start | bytes 884744 | tf_op jit(solution)/shard_map/ppermute | solution.py:33
  158.0 11.1 %collective-permute-start.9 = (bf16[2,144,512]{2,1,0:T(8,128)(2,1)S(1)}, bf16[2,144,512]{2,1,0:T(8,128)(2,1)S(1)}, u32[]{:S(2)}, u32[]{:S(2)}) collective-permute-start(bf16[2,144,512]{2,1,0:T(8,128)(2,1)S(1)} %get-tuple-element.26), channel_id=1, source_target_pairs={{0,8},{32,40},{1,9},{33,41},{2,10},{34,42},{3,11},{35,43},{4,12},{... | collective-permute-start | bytes 884744 | tf_op jit(solution)/shard_map/ppermute | solution.py:33
  169.1 4.2 %copy-start = (bf16[1,4,128,576]{2,3,1,0:T(8,128)(2,1)S(1)}, bf16[1,4,128,576]{2,3,1,0:T(8,128)(2,1)}, u32[]{:S(2)}) copy-start(bf16[1,4,128,576]{2,3,1,0:T(8,128)(2,1)} %param.6) | copy-start | bytes 1769476
  169.1 4.2 %copy-start.3 = (s32[1,2]{1,0:T(1,128)S(1)}, s32[1,2]{1,0:T(1,128)}, u32[]{:S(2)}) copy-start(s32[1,2]{1,0:T(1,128)} %param.8) | copy-start | bytes 28
  170.0 12.4 %collective-permute-start.20 = (bf16[2,144,512]{2,1,0:T(8,128)(2,1)S(1)}, bf16[2,144,512]{2,1,0:T(8,128)(2,1)S(1)}, u32[]{:S(2)}, u32[]{:S(2)}) collective-permute-start(bf16[2,144,512]{2,1,0:T(8,128)(2,1)S(1)} %get-tuple-element.35), channel_id=1, source_target_pairs={{0,64},{32,96},{1,65},{33,97},{2,66},{34,98},{3,67},{35,99},{4,68}... | collective-permute-start | bytes 884744 | tf_op jit(solution)/shard_map/ppermute | solution.py:33
  170.1 12.3 %collective-permute-start.21 = (bf16[2,144,512]{2,1,0:T(8,128)(2,1)S(1)}, bf16[2,144,512]{2,1,0:T(8,128)(2,1)S(1)}, u32[]{:S(2)}, u32[]{:S(2)}) collective-permute-start(bf16[2,144,512]{2,1,0:T(8,128)(2,1)S(1)} %get-tuple-element.36), channel_id=1, source_target_pairs={{0,80},{32,112},{1,81},{33,113},{2,82},{34,114},{3,83},{35,115},{4... | collective-permute-start | bytes 884744 | tf_op jit(solution)/shard_map/ppermute | solution.py:33

commit v2 on v1

v2 whole, which is shorter than its diff:
```python
import functools

import jax
import jax.numpy as jnp
from jax import lax
from jax.experimental import pallas as pl
from jax.experimental.pallas import tpu as pltpu
from jax.sharding import PartitionSpec as P

KV_RANK = 512
SCALE = 192.0 ** (-0.5)
DEAD = -1e30
RING = 4
STAT_ROWS = 16
AXES = ("section", "dev")
SMALL_VMEM = 16 * 1024 * 1024
GATHER_VMEM = 48 * 1024 * 1024
LARGE_VMEM = 56 * 1024 * 1024


def place(x, z, y, core):
    section = (x % 2) * 2 + core
    dev = ((x % RING) // 2) * 16 + (z % RING) * 4 + (y % RING)
    return section * 32 + dev


def move(block, dx=0, dz=0, dy=0):
    route = [
        (place(x, z, y, core), place(x + dx, z + dz, y + dy, core))
        for x in range(RING)
        for z in range(RING)
        for y in range(RING)
        for core in range(2)
    ]
    return lax.ppermute(block, AXES, route)


def positions():
    section = lax.axis_index("section")
    dev = lax.axis_index("dev")
    x_hi, z, y = dev // 16, (dev // 4) % 4, dev % 4
    x_lo = section // 2
    hi_plus = jnp.where(x_lo == 0, x_hi, 1 - x_hi)
    return jnp.stack([section, x_hi, z, y, hi_plus, 1 - hi_plus]).astype(jnp.int32)


def request_of(meta, matching, half, side, cache_step, query_step):
    x_hi = meta[4 + side]
    if half == 0:
        z, y = (meta[2] + query_step) % RING, (meta[3] + cache_step) % RING
    else:
        z, y = (meta[2] + cache_step) % RING, (meta[3] + query_step) % RING
    return matching[meta[0], (x_hi * 16 + z * 4 + y) * 2 + half]


def gather_kernel(steps, meta, matching, cache, *rest):
    outs, sems = rest[:-1], rest[-1]
    copies = []
    slot = 0
    for out, (half, step) in zip(outs, steps):
        for query_step in range(RING):
            for side in range(2):
                request = request_of(meta, matching, half, side, step, query_step)
                copy = pltpu.make_async_copy(
                    cache.at[request], out.at[query_step * 2 + side], sems.at[slot]
                )
                copy.start()
                copies.append(copy)
                slot += 1
    for copy in copies:
        copy.wait()


def gather_requests(steps, room, meta, matching, cache):
    width, span = cache.shape[1:]
    shape = (2 * RING + room, width, span)
    size = len(steps) * 2 * RING * width * span * 4
    return pl.pallas_call(
        functools.partial(gather_kernel, steps),
        out_shape=[pltpu.VMEM(shape, cache.dtype)] * len(steps),
        grid_spec=pltpu.PrefetchScalarGridSpec(
            num_scalar_prefetch=2,
            grid=(1,),
            in_specs=[pl.BlockSpec(memory_space=pl.ANY)],
            out_specs=[pl.BlockSpec(memory_space=pltpu.VMEM)] * len(steps),
            scratch_shapes=[pltpu.SemaphoreType.DMA((len(steps) * 2 * RING,))],
        ),
        compiler_params=pltpu.CompilerParams(vmem_limit_bytes=GATHER_VMEM),
        cost_estimate=pl.CostEstimate(flops=0, bytes_accessed=size, transcendentals=0),
        name="gather_requests",
    )(meta, matching, cache)


def own_kernel(plus, minus, qa, qb):
    for half, out in enumerate((qa, qb)):
        out[0] = plus[half]
        out[1] = minus[half]


def own_queries(plus, minus):
    return pl.pallas_call(
        own_kernel,
        out_shape=[jax.ShapeDtypeStruct(plus.shape, plus.dtype)] * 2,
        compiler_params=pltpu.CompilerParams(vmem_limit_bytes=SMALL_VMEM),
        name="own_queries",
    )(plus, minus)


def fill_kernel(halves, *refs):
    count = len(halves)
    queries = refs[count : count + 2]
    for half, out in zip(halves, refs[count + 2 :]):
        out[...] = queries[half][...]


def fill_queries(halves, arrays, qa, qb):
    count = len(arrays)
    whole = pl.BlockSpec(qa.shape, lambda i: (0, 0, 0))
    return pl.pallas_call(
        functools.partial(fill_kernel, halves),
        out_shape=[jax.ShapeDtypeStruct(x.shape, x.dtype) for x in arrays],
        grid=(1,),
        in_specs=[pl.BlockSpec(memory_space=pl.ANY)] * count + [whole] * 2,
        out_specs=[pl.BlockSpec(qa.shape, lambda i: (RING, 0, 0))] * count,
        input_output_aliases={i: i for i in range(count)},
        compiler_params=pltpu.CompilerParams(vmem_limit_bytes=SMALL_VMEM),
        name="fill_queries",
    )(*arrays, qa, qb)


def weigh(blocks):
    scores = [
        jnp.dot(query, keys, preferred_element_type=jnp.float32) * SCALE for query, keys, _ in blocks
    ]
    scores = [jnp.where(live, score, DEAD) for score, (_, _, live) in zip(scores, blocks)]
    tops = [jnp.max(score, axis=1, keepdims=True) for score in scores]
    weights = [jnp.exp(score - top) for score, top in zip(scores, tops)]
    totals = [jnp.sum(weight, axis=1, keepdims=True) for weight in weights]
    mixed = [
        lax.dot_general(
            weight.astype(jnp.bfloat16),
            keys[:KV_RANK],
            (((1,), (1,)), ((), ())),
            preferred_element_type=jnp.float32,
        )
        for weight, (_, keys, _) in zip(weights, blocks)
    ]
    return mixed, tops, totals


def resident_kernel(lengths, query, keys, out):
    item = pl.program_id(0)
    live = lax.broadcasted_iota(jnp.int32, (1, keys.shape[2]), 1) < lengths[item]
    (mixed,), _, (total,) = weigh([(query[0].T, keys[0], live)])
    out[0] = (mixed / total).astype(jnp.bfloat16)


def resident_rows(lengths, queries, cache):
    count, width, span = cache.shape
    heads = queries.shape[2]
    return pl.pallas_call(
        resident_kernel,
        out_shape=jax.ShapeDtypeStruct((queries.shape[0], heads, KV_RANK), jnp.bfloat16),
        grid_spec=pltpu.PrefetchScalarGridSpec(
            num_scalar_prefetch=1,
            grid=(count,),
            in_specs=[
                pl.BlockSpec((1, width, heads), lambda i, lengths: (i, 0, 0)),
                pl.BlockSpec((1, width, span), lambda i, lengths: (i, 0, 0)),
            ],
            out_specs=pl.BlockSpec((1, heads, KV_RANK), lambda i, lengths: (i, 0, 0)),
        ),
        compiler_params=pltpu.CompilerParams(vmem_limit_bytes=LARGE_VMEM),
        cost_estimate=pl.CostEstimate(
            flops=2 * count * heads * span * (width + KV_RANK),
            bytes_accessed=2 * count * width * span,
            transcendentals=count * heads * span,
        ),
        name="resident_rows",
    )(lengths, queries, cache)


def split_stat(row):
    high = row.astype(jnp.bfloat16).astype(jnp.float32)
    rest = row - high
    middle = rest.astype(jnp.bfloat16).astype(jnp.float32)
    return high, middle, rest - middle


def put_stat(out, index, row):
    heads = row.shape[1]
    high, middle, low = split_stat(row)
    rows = lax.broadcasted_iota(jnp.int32, (STAT_ROWS, heads), 0)
    block = jnp.where(rows == 0, high, jnp.where(rows == 1, middle, jnp.where(rows == 2, low, 0.0)))
    out[index, heads:, :heads] = block.astype(jnp.bfloat16)
    out[index, heads:, heads:] = jnp.zeros((STAT_ROWS, KV_RANK - heads), jnp.bfloat16)


def slots_of(meta, half, away, span):
    z, y = meta[2], meta[3]
    if half == 0:
        y = (y + RING - away) % RING
    else:
        z = (z + RING - away) % RING
    return lax.broadcasted_iota(jnp.int32, (1, span), 1) + (meta[1] * 16 + z * 4 + y) * span


def ring_results(step, meta, matching, lengths, a, b, queries):
    span = a[0].shape[2]
    blocks = []
    for half, segments in enumerate((a, b)):
        slots = jnp.concatenate([slots_of(meta, half, away, span) for away in range(RING)], axis=1)
        for side in range(2):
            request = request_of(meta, matching, half, side, 0, step)
            live = slots < lengths[meta[0], request]
            keys = jnp.concatenate([segment[2 * step + side] for segment in segments], axis=1)
            blocks.append((queries[half][side].T, keys, live))
    mixed, tops, totals = weigh(blocks)
    return [(m / t, stat_row(top, t)) for m, top, t in zip(mixed, tops, totals)]


def stat_row(top, total):
    heads = top.shape[0]
    return jnp.broadcast_to(top + jnp.log(total), (heads, heads)).T[:1]


def put_results(outs, results):
    for index, (value, row) in enumerate(results):
        half, side = divmod(index, 2)
        heads = value.shape[0]
        outs[half][side, :heads] = value.astype(jnp.bfloat16)
        put_stat(outs[half], side, row)


def partial_kernel(step, meta, matching, lengths, *refs):
    a, b, qa, qb, outs = refs[:RING], refs[RING : 2 * RING], refs[2 * RING], refs[2 * RING + 1], refs[2 * RING + 2 :]
    if step != 2:
        back = RING - step
        qa, qb = b[back].at[2 * RING :], a[back].at[2 * RING :]
    put_results(outs, ring_results(step, meta, matching, lengths, a, b, (qa, qb)))


def ring_call(kernel, operands, arrays, name):
    meta, matching, lengths = operands
    width, span = arrays[0].shape[1:]
    heads = span
    work = 4 * heads * span * RING
    whole = pl.BlockSpec(memory_space=pltpu.VMEM)
    shape = (2, heads + STAT_ROWS, KV_RANK)
    return pl.pallas_call(
        kernel,
        out_shape=[pltpu.VMEM(shape, jnp.bfloat16)] * 2,
        grid_spec=pltpu.PrefetchScalarGridSpec(
            num_scalar_prefetch=3,
            grid=(1,),
            in_specs=[whole] * len(arrays),
            out_specs=[whole] * 2,
        ),
        compiler_params=pltpu.CompilerParams(vmem_limit_bytes=SMALL_VMEM),
        cost_estimate=pl.CostEstimate(
            flops=2 * work * (width + KV_RANK),
            bytes_accessed=8 * RING * width * span,
            transcendentals=work,
        ),
        name=name,
    )(meta, matching, lengths, *arrays)


def merge(parts):
    heads = parts[0][0].shape[0]
    stats = [stat for _, stat in parts]
    top = functools.reduce(jnp.maximum, stats)
    shares = [jnp.exp(stat - top) for stat in stats]
    total = functools.reduce(jnp.add, shares)
    mixed = 0.0
    for (value, _), share in zip(parts, shares):
        column = jnp.broadcast_to(share / total, (heads, heads)).T[:, :1]
        mixed = mixed + value * column
    return mixed, top + jnp.log(total)


def received(block):
    heads = block.shape[0] - STAT_ROWS
    rows = block[heads:, :heads].astype(jnp.float32)
    return block[:heads].astype(jnp.float32), rows[0:1] + rows[1:2] + rows[2:3]


def middle_kernel(meta, matching, lengths, *refs):
    a, b, queries, ins, outs = refs[:RING], refs[RING : 2 * RING], refs[8:10], refs[10:16], refs[16:]
    near = ring_results(0, meta, matching, lengths, a, b, queries)
    for half in range(2):
        for side in range(2):
            parts = [near[2 * half + side]] + [received(ref[side]) for ref in ins[3 * half : 3 * half + 3]]
            mixed, row = merge(parts)
            outs[side][half, : mixed.shape[0]] = mixed.astype(jnp.bfloat16)
            put_stat(outs[side], half, row)


def last_kernel(base, plus, minus, out):
    del base
    for half in range(2):
        mixed, _ = merge([received(plus[half]), received(minus[half])])
        out[half] = mixed.astype(jnp.bfloat16)


def last(base, plus, minus):
    count, heads, rank = base.shape
    whole = pl.BlockSpec(plus.shape, lambda i: (0, 0, 0))
    return pl.pallas_call(
        last_kernel,
        out_shape=jax.ShapeDtypeStruct(base.shape, base.dtype),
        grid=(1,),
        in_specs=[pl.BlockSpec(memory_space=pl.ANY), whole, whole],
        out_specs=pl.BlockSpec((count // 2, heads, rank), lambda i: (1, 0, 0)),
        input_output_aliases={0: 0},
        compiler_params=pltpu.CompilerParams(vmem_limit_bytes=SMALL_VMEM),
        name="last",
    )(base, plus, minus)


def per_device(queries, res_cache, res_lengths, inc_cache, inc_lengths, matching):
    meta = positions()
    queries = jnp.swapaxes(queries[0], 1, 2)
    res_cache = jnp.swapaxes(res_cache[0], 1, 2)
    inc_cache = jnp.swapaxes(inc_cache[0], 1, 2)

    from_minus = move(queries[2:], dx=1)
    from_plus = move(queries[2:], dx=-1)
    a2, b2 = gather_requests(((0, 2), (1, 2)), 0, meta, matching, inc_cache)
    a2 = move(a2, dy=2)
    b2 = move(b2, dz=2)
    qa, qb = own_queries(from_plus, from_minus)
    qa_far = move(qa, dz=2)
    qb_far = move(qb, dy=2)
    sent = gather_requests(((0, 1), (0, 3), (1, 1), (1, 3)), 2, meta, matching, inc_cache)
    a1, a3, b1, b3 = fill_queries((1, 1, 0, 0), sent, qa, qb)
    base = resident_rows(res_lengths[0], queries, res_cache)
    a1, a3, a2, qb_far, base = lax.optimization_barrier((a1, a3, a2, qb_far, base))
    b1, b3, b2, qa_far = lax.optimization_barrier((b1, b3, b2, qa_far))
    a1 = move(a1, dy=1)
    a3 = move(a3, dy=-1)
    b1 = move(b1, dz=1)
    b3 = move(b3, dz=-1)
    a0, b0 = gather_requests(((0, 0), (1, 0)), 0, meta, matching, inc_cache)

    operands = (meta, matching, inc_lengths)
    segments = (a0, a1, a2, a3, b0, b1, b2, b3)
    pa, pb = [], []
    for step in (2, 1, 3):
        found = ring_call(
            functools.partial(partial_kernel, step), operands, (*segments, qa_far, qb_far), "partials"
        )
        pa.append(move(found[0], dz=step))
        pb.append(move(found[1], dy=step))
    to_plus, to_minus = ring_call(middle_kernel, operands, (*segments, qa, qb, *pa, *pb), "middle")
    plus = move(to_plus, dx=1)
    minus = move(to_minus, dx=-1)
    return last(base, plus, minus)[None]


def solution(mesh):
    placed = (
        P("section", "dev", None, None),
        P("section", "dev", None, None),
        P("section", "dev"),
        P("section", None, "dev", None),
        P(),
        P(),
    )
    return jax.shard_map(
        per_device,
        mesh=mesh,
        in_specs=placed,
        out_specs=P("section", "dev", None, None),
        check_vma=False,
    )
```

time: 185 us -> 114 us (0.62)
  Pallas kernels: 65.3 us -> 30.6 us
  waiting for transfers between devices: 83 us -> 52.7 us
  starting transfers between devices: 33.2 us -> 29.6 us
    pallas_call x5 -> x9, Pallas kernels: 55.1 us -> 20.2 us  [the longest x3 10.7 us: gather_requests(): pl.pallas_call(functools.partial(gather_kernel, steps), out_shape=[pltpu....]
    ppermute x22 -> x18, waiting for transfers between devices: 83 us -> 52.7 us  [move(): return lax.ppermute(block, AXES, route)]
    ppermute x22 -> x18, starting transfers between devices: 33.2 us -> 29.6 us  [move(): return lax.ppermute(block, AXES, route)]
  transfers between devices with their start and end apart: 22 -> 18, of which waited for: 9 -> 9; matrix products, arithmetic and copies ran while one was open for 0% -> 0% of each run, Pallas kernels for 35% -> 18%
where the time goes in v2:
time: 114 us
  waiting for transfers between devices  52.7 us (46%)
  Pallas kernels  30.6 us (27%)
  starting transfers between devices  29.6 us (26%)
    ppermute x18, waiting for transfers between devices, move(): return lax.ppermute(block, AXES, route)  52.7 us
    ppermute x18, starting transfers between devices, move(): return lax.ppermute(block, AXES, route)  29.6 us
    pallas_call x3, Pallas kernels, gather_requests(): pl.pallas_call(functools.partial(gather_kernel, steps), out_shape=[pltpu....  10.7 us
    pallas_call x1, Pallas kernels, resident_rows(): pl.pallas_call(resident_kernel, out_shape=jax.ShapeDtypeStruct((queries.s...  9.32 us
    pallas_call x4, Pallas kernels, ring_call(): pl.pallas_call(kernel, out_shape=[pltpu.VMEM(shape, jnp.bfloat16)] * 2, g...  8.67 us
  transfers between devices with their start and end apart: 18, of which 9 were waited for; matrix products, arithmetic and copies ran while one was open for 0% of the time, Pallas kernels for 18%

profile of v2, /device:TPU:0, one launch (start us, length us, event | category | flops | bytes accessed | tf_op | source)
XLA Modules:
  0.0 113.8 jit_solution(15315927813508241218)
XLA Ops:
  0.0 0.1 stack.27.meta
  0.1 0.7 copy-done
  0.8 3.8 %gather_requests.4 = (bf16[8,576,128]{2,1,0:T(8,128)(2,1)}, bf16[8,576,128]{2,1,0:T(8,128)(2,1)}) custom-call(s32[6]{0:T(128)S(1)} %stack.27.meta, s32[4,64]{1,0:T(4,128)S(1)} %copy-done, bf16[64,576,128]{2,1,0:T(8,128)(2,1)} %bitcast.17), custom_call_target="tpu_custom_call" | custom-call | bytes 4718592 | tf_op jit(solution)/shard_map/gather_requests/pallas_call | solution.py:78
  4.6 4.0 %collective-permute-start.6 = (bf16[8,576,128]{2,1,0:T(8,128)(2,1)}, bf16[8,576,128]{2,1,0:T(8,128)(2,1)S(1)}, u32[]{:S(2)}, u32[]{:S(2)}) collective-permute-start(bf16[8,576,128]{2,1,0:T(8,128)(2,1)} %get-tuple-element.53), channel_id=1, source_target_pairs={{0,8},{32,40},{1,9},{33,41},{2,10},{34,42},{3,11},{35,43},{4,12},{... | collective-permute-start | bytes 3538952 | tf_op jit(solution)/shard_map/ppermute | solution.py:35
  8.6 3.2 %collective-permute-start.2 = (bf16[8,576,128]{2,1,0:T(8,128)(2,1)}, bf16[8,576,128]{2,1,0:T(8,128)(2,1)S(1)}, u32[]{:S(2)}, u32[]{:S(2)}) collective-permute-start(bf16[8,576,128]{2,1,0:T(8,128)(2,1)} %get-tuple-element.44), channel_id=1, source_target_pairs={{0,2},{32,34},{1,3},{33,35},{2,0},{34,32},{3,1},{35,33},{4,6},{36,... | collective-permute-start | bytes 3538952 | tf_op jit(solution)/shard_map/ppermute | solution.py:35
  11.8 2.8 %collective-permute-start = (bf16[2,576,128]{2,1,0:T(8,128)(2,1)S(1)}, bf16[2,576,128]{2,1,0:T(8,128)(2,1)S(1)}, u32[]{:S(2)}, u32[]{:S(2)}) collective-permute-start(bf16[2,576,128]{2,1,0:T(8,128)(2,1)S(1)} %slice.5), channel_id=1, source_target_pairs={{0,80},{32,112},{1,81},{33,113},{2,82},{34,114},{3,83},{35,115},{4... | collective-permute-start | bytes 884744 | tf_op jit(solution)/shard_map/ppermute | solution.py:35
  14.7 0.0 collective-permute-start.1
  14.7 5.7 %collective-permute-done.plus = bf16[2,576,128]{2,1,0:T(8,128)(2,1)S(1)} collective-permute-done((bf16[2,576,128]{2,1,0:T(8,128)(2,1)S(1)}, bf16[2,576,128]{2,1,0:T(8,128)(2,1)S(1)}, u32[]{:S(2)}, u32[]{:S(2)}) %collective-permute-start) | collective-permute-done | bytes 294944 | tf_op jit(solution)/shard_map/ppermute | solution.py:35
  20.4 3.4 %collective-permute-done.1.minus = bf16[2,576,128]{2,1,0:T(8,128)(2,1)S(1)} collective-permute-done((bf16[2,576,128]{2,1,0:T(8,128)(2,1)S(1)}, bf16[2,576,128]{2,1,0:T(8,128)(2,1)S(1)}, u32[]{:S(2)}, u32[]{:S(2)}) %collective-permute-start.1) | collective-permute-done | bytes 294944 | tf_op jit(solution)/shard_map/ppermute | solution.py:35
  23.8 0.5 collective-permute-start.7
  24.3 0.3 collective-permute-start.3
  24.6 4.4 %gather_requests.3 = (bf16[10,576,128]{2,1,0:T(8,128)(2,1)S(1)}, bf16[10,576,128]{2,1,0:T(8,128)(2,1)S(1)}, bf16[10,576,128]{2,1,0:T(8,128)(2,1)S(1)}, bf16[10,576,128]{2,1,0:T(8,128)(2,1)}) custom-call(s32[6]{0:T(128)S(1)} %stack.27.meta, s32[4,64]{1,0:T(4,128)S(1)} %copy-done, bf16[64,576,128]{2,1,0:T(8,128)(2,1)} %bitcast.18), custom_call_target="tpu_custom_call" | custom-call | bytes 9437184 | tf_op jit(solution)/shard_map/gather_requests/pallas_call | solution.py:78
  29.1 9.3 %resident_rows.1.base = bf16[4,128,512]{2,1,0:T(8,128)(2,1)} custom-call(s32[2]{0:T(128)} %bitcast.23, bf16[4,576,128]{2,1,0:T(8,128)(2,1)} %bitcast.21, bf16[2,576,4096]{2,1,0:T(8,128)(2,1)} %bitcast.20), custom_call_target="tpu_custom_call" | custom-call | flops 2281701376 | bytes 9437184 | tf_op jit(solution)/shard_map/resident_rows/pallas_call | solution.py:161
  38.4 0.8 fill_queries.1
  39.2 1.9 %collective-permute-done.7.refs_8_ = bf16[2,576,128]{2,1,0:T(8,128)(2,1)S(1)} collective-permute-done((bf16[2,576,128]{2,1,0:T(8,128)(2,1)S(1)}, bf16[2,576,128]{2,1,0:T(8,128)(2,1)S(1)}, u32[]{:S(2)}, u32[]{:S(2)}) %collective-permute-start.7) | collective-permute-done | bytes 294944 | tf_op jit(solution)/shard_map/ppermute | solution.py:35
  41.1 0.0 collective-permute-done.6.refs_6_
  41.1 1.3 %collective-permute-start.8 = (bf16[10,576,128]{2,1,0:T(8,128)(2,1)S(1)}, bf16[10,576,128]{2,1,0:T(8,128)(2,1)S(1)}, u32[]{:S(2)}, u32[]{:S(2)}) collective-permute-start(bf16[10,576,128]{2,1,0:T(8,128)(2,1)S(1)} %get-tuple-element.54), channel_id=1, source_target_pairs={{0,4},{32,36},{1,5},{33,37},{2,6},{34,38},{3,7},{35,39},{4,8},{36,... | collective-permute-start | bytes 4423688 | tf_op jit(solution)/shard_map/ppermute | solution.py:35
  42.4 2.1 %collective-permute-start.9 = (bf16[10,576,128]{2,1,0:T(8,128)(2,1)}, bf16[10,576,128]{2,1,0:T(8,128)(2,1)S(1)}, u32[]{:S(2)}, u32[]{:S(2)}) collective-permute-start(bf16[10,576,128]{2,1,0:T(8,128)(2,1)} %get-tuple-element.56), channel_id=1, source_target_pairs={{0,12},{32,44},{1,13},{33,45},{2,14},{34,46},{3,15},{35,47},{4,0},... | collective-permute-start | bytes 4423688 | tf_op jit(solution)/shard_map/ppermute | solution.py:35
  44.5 0.0 collective-permute-done.3.refs_9_
  44.5 0.0 collective-permute-done.2.refs_2_
  44.6 1.6 %collective-permute-start.4 = (bf16[10,576,128]{2,1,0:T(8,128)(2,1)S(1)}, bf16[10,576,128]{2,1,0:T(8,128)(2,1)S(1)}, u32[]{:S(2)}, u32[]{:S(2)}) collective-permute-start(bf16[10,576,128]{2,1,0:T(8,128)(2,1)S(1)} %get-tuple-element.47), channel_id=1, source_target_pairs={{0,1},{32,33},{1,2},{33,34},{2,3},{34,35},{3,0},{35,32},{4,5},{36,... | collective-permute-start | bytes 4423688 | tf_op jit(solution)/shard_map/ppermute | solution.py:35
  46.2 1.7 %collective-permute-start.5 = (bf16[10,576,128]{2,1,0:T(8,128)(2,1)S(1)}, bf16[10,576,128]{2,1,0:T(8,128)(2,1)S(1)}, u32[]{:S(2)}, u32[]{:S(2)}) collective-permute-start(bf16[10,576,128]{2,1,0:T(8,128)(2,1)S(1)} %get-tuple-element.49), channel_id=1, source_target_pairs={{0,3},{32,35},{1,0},{33,32},{2,1},{34,33},{3,2},{35,34},{4,7},{36,... | collective-permute-start | bytes 4423688 | tf_op jit(solution)/shard_map/ppermute | solution.py:35
  47.9 2.4 %gather_requests.5 = (bf16[8,576,128]{2,1,0:T(8,128)(2,1)S(1)}, bf16[8,576,128]{2,1,0:T(8,128)(2,1)S(1)}) custom-call(s32[6]{0:T(128)S(1)} %stack.27.meta, s32[4,64]{1,0:T(4,128)S(1)} %copy-done.1, bf16[64,576,128]{2,1,0:T(8,128)(2,1)} %bitcast.19), custom_call_target="tpu_custom_call" | custom-call | bytes 4718592 | tf_op jit(solution)/shard_map/gather_requests/pallas_call | solution.py:78
  50.3 25.7 %collective-permute-done.8.refs_5_ = bf16[10,576,128]{2,1,0:T(8,128)(2,1)S(1)} collective-permute-done((bf16[10,576,128]{2,1,0:T(8,128)(2,1)S(1)}, bf16[10,576,128]{2,1,0:T(8,128)(2,1)S(1)}, u32[]{:S(2)}, u32[]{:S(2)}) %collective-permute-start.8) | collective-permute-done | bytes 1474592 | tf_op jit(solution)/shard_map/ppermute | solution.py:35
  76.0 0.0 collective-permute-done.9.refs_7_
  76.0 2.8 %collective-permute-done.4.refs_1_ = bf16[10,576,128]{2,1,0:T(8,128)(2,1)S(1)} collective-permute-done((bf16[10,576,128]{2,1,0:T(8,128)(2,1)S(1)}, bf16[10,576,128]{2,1,0:T(8,128)(2,1)S(1)}, u32[]{:S(2)}, u32[]{:S(2)}) %collective-permute-start.4) | collective-permute-done | bytes 1474592 | tf_op jit(solution)/shard_map/ppermute | solution.py:35
  78.8 0.0 collective-permute-done.5.refs_3_
  78.8 2.0 %partials.5 = (bf16[2,144,512]{2,1,0:T(8,128)(2,1)S(1)}, bf16[2,144,512]{2,1,0:T(8,128)(2,1)S(1)}) custom-call(s32[6]{0:T(128)S(1)} %stack.27.meta, s32[4,64]{1,0:T(4,128)S(1)} %copy-done.1, s32[4,64]{1,0:T(4,128)S(1)} %copy-done.2, bf16[8,576,128]{2,1,0:T(8,128)(2,1)S(1)} %get-tuple-element.46.refs_0_, ...), custom_call_target="tpu_custom_call" | custom-call | flops 570425344 | bytes 2359296 | tf_op jit(solution)/shard_map/partials/pallas_call | solution.py:250
  80.8 1.8 %collective-permute-start.12 = (bf16[2,144,512]{2,1,0:T(8,128)(2,1)S(1)}, bf16[2,144,512]{2,1,0:T(8,128)(2,1)S(1)}, u32[]{:S(2)}, u32[]{:S(2)}) collective-permute-start(bf16[2,144,512]{2,1,0:T(8,128)(2,1)S(1)} %get-tuple-element.61), channel_id=1, source_target_pairs={{0,12},{32,44},{1,13},{33,45},{2,14},{34,46},{3,15},{35,47},{4,0},... | collective-permute-start | bytes 884744 | tf_op jit(solution)/shard_map/ppermute | solution.py:35
  82.6 3.0 %collective-permute-start.15 = (bf16[2,144,512]{2,1,0:T(8,128)(2,1)S(1)}, bf16[2,144,512]{2,1,0:T(8,128)(2,1)S(1)}, u32[]{:S(2)}, u32[]{:S(2)}) collective-permute-start(bf16[2,144,512]{2,1,0:T(8,128)(2,1)S(1)} %get-tuple-element.64), channel_id=1, source_target_pairs={{0,3},{32,35},{1,0},{33,32},{2,1},{34,33},{3,2},{35,34},{4,7},{36,... | collective-permute-start | bytes 884744 | tf_op jit(solution)/shard_map/ppermute | solution.py:35
  85.6 2.0 %partials.4 = (bf16[2,144,512]{2,1,0:T(8,128)(2,1)S(1)}, bf16[2,144,512]{2,1,0:T(8,128)(2,1)S(1)}) custom-call(s32[6]{0:T(128)S(1)} %stack.27.meta, s32[4,64]{1,0:T(4,128)S(1)} %copy-done.1, s32[4,64]{1,0:T(4,128)S(1)} %copy-done.2, bf16[8,576,128]{2,1,0:T(8,128)(2,1)S(1)} %get-tuple-element.46.refs_0_, ...), custom_call_target="tpu_custom_call" | custom-call | flops 570425344 | bytes 2359296 | tf_op jit(solution)/shard_map/partials/pallas_call | solution.py:250
  87.6 0.4 collective-permute-start.11
  88.0 0.0 collective-permute-start.14
  88.0 2.0 %partials.3 = (bf16[2,144,512]{2,1,0:T(8,128)(2,1)S(1)}, bf16[2,144,512]{2,1,0:T(8,128)(2,1)S(1)}) custom-call(s32[6]{0:T(128)S(1)} %stack.27.meta, s32[4,64]{1,0:T(4,128)S(1)} %copy-done.1, s32[4,64]{1,0:T(4,128)S(1)} %copy-done.2, bf16[8,576,128]{2,1,0:T(8,128)(2,1)S(1)} %get-tuple-element.46.refs_0_, ...), custom_call_target="tpu_custom_call" | custom-call | flops 570425344 | bytes 2359296 | tf_op jit(solution)/shard_map/partials/pallas_call | solution.py:250
  90.0 1.7 %collective-permute-start.10 = (bf16[2,144,512]{2,1,0:T(8,128)(2,1)S(1)}, bf16[2,144,512]{2,1,0:T(8,128)(2,1)S(1)}, u32[]{:S(2)}, u32[]{:S(2)}) collective-permute-start(bf16[2,144,512]{2,1,0:T(8,128)(2,1)S(1)} %get-tuple-element.59), channel_id=1, source_target_pairs={{0,8},{32,40},{1,9},{33,41},{2,10},{34,42},{3,11},{35,43},{4,12},{... | collective-permute-start | bytes 884744 | tf_op jit(solution)/shard_map/ppermute | solution.py:35
  91.6 0.0 collective-permute-done.12.refs_12_
  91.6 1.9 %collective-permute-start.13 = (bf16[2,144,512]{2,1,0:T(8,128)(2,1)S(1)}, bf16[2,144,512]{2,1,0:T(8,128)(2,1)S(1)}, u32[]{:S(2)}, u32[]{:S(2)}) collective-permute-start(bf16[2,144,512]{2,1,0:T(8,128)(2,1)S(1)} %get-tuple-element.62), channel_id=1, source_target_pairs={{0,2},{32,34},{1,3},{33,35},{2,0},{34,32},{3,1},{35,33},{4,6},{36,... | collective-permute-start | bytes 884744 | tf_op jit(solution)/shard_map/ppermute | solution.py:35
  93.5 0.0 collective-permute-done.15.refs_15_
  93.5 7.5 %collective-permute-done.11.refs_11_ = bf16[2,144,512]{2,1,0:T(8,128)(2,1)S(1)} collective-permute-done((bf16[2,144,512]{2,1,0:T(8,128)(2,1)S(1)}, bf16[2,144,512]{2,1,0:T(8,128)(2,1)S(1)}, u32[]{:S(2)}, u32[]{:S(2)}) %collective-permute-start.11) | collective-permute-done | bytes 294944 | tf_op jit(solution)/shard_map/ppermute | solution.py:35
  101.1 0.7 collective-permute-done.14.refs_14_
  101.8 0.0 collective-permute-done.10.refs_10_
  101.8 0.0 collective-permute-done.13.refs_13_
  101.8 2.7 %middle.1 = (bf16[2,144,512]{2,1,0:T(8,128)(2,1)S(1)}, bf16[2,144,512]{2,1,0:T(8,128)(2,1)S(1)}) custom-call(s32[6]{0:T(128)S(1)} %stack.27.meta, s32[4,64]{1,0:T(4,128)S(1)} %copy-done.1, s32[4,64]{1,0:T(4,128)S(1)} %copy-done.2, bf16[8,576,128]{2,1,0:T(8,128)(2,1)S(1)} %get-tuple-element.46.refs_0_, ...), custom_call_target="tpu_custom_call" | custom-call | flops 570425344 | bytes 2359296 | tf_op jit(solution)/shard_map/middle/pallas_call | solution.py:250
  104.5 1.5 %collective-permute-start.16 = (bf16[2,144,512]{2,1,0:T(8,128)(2,1)S(1)}, bf16[2,144,512]{2,1,0:T(8,128)(2,1)S(1)}, u32[]{:S(2)}, u32[]{:S(2)}) collective-permute-start(bf16[2,144,512]{2,1,0:T(8,128)(2,1)S(1)} %get-tuple-element.65), channel_id=1, source_target_pairs={{0,64},{32,96},{1,65},{33,97},{2,66},{34,98},{3,67},{35,99},{4,68}... | collective-permute-start | bytes 884744 | tf_op jit(solution)/shard_map/ppermute | solution.py:35
  106.0 1.8 %collective-permute-start.17 = (bf16[2,144,512]{2,1,0:T(8,128)(2,1)S(1)}, bf16[2,144,512]{2,1,0:T(8,128)(2,1)S(1)}, u32[]{:S(2)}, u32[]{:S(2)}) collective-permute-start(bf16[2,144,512]{2,1,0:T(8,128)(2,1)S(1)} %get-tuple-element.66), channel_id=1, source_target_pairs={{0,80},{32,112},{1,81},{33,113},{2,82},{34,114},{3,83},{35,115},{4... | collective-permute-start | bytes 884744 | tf_op jit(solution)/shard_map/ppermute | solution.py:35
  107.8 4.7 %collective-permute-done.16.plus = bf16[2,144,512]{2,1,0:T(8,128)(2,1)S(1)} collective-permute-done((bf16[2,144,512]{2,1,0:T(8,128)(2,1)S(1)}, bf16[2,144,512]{2,1,0:T(8,128)(2,1)S(1)}, u32[]{:S(2)}, u32[]{:S(2)}) %collective-permute-start.16) | collective-permute-done | bytes 294944 | tf_op jit(solution)/shard_map/ppermute | solution.py:35
  112.5 0.2 collective-permute-done.17.minus
  112.8 1.0 last.1
  (9 shorter events, 0.1 us)
Async XLA Ops:
  0.1 0.7 copy-start
  0.8 11.1 %copy-start.3 = (bf16[1,4,128,576]{2,3,1,0:T(8,128)(2,1)S(1)}, bf16[1,4,128,576]{2,3,1,0:T(8,128)(2,1)}, u32[]{:S(2)}) copy-start(bf16[1,4,128,576]{2,3,1,0:T(8,128)(2,1)} %param.6) | copy-start | bytes 1769476
  4.6 36.5 %collective-permute-start.6 = (bf16[8,576,128]{2,1,0:T(8,128)(2,1)}, bf16[8,576,128]{2,1,0:T(8,128)(2,1)S(1)}, u32[]{:S(2)}, u32[]{:S(2)}) collective-permute-start(bf16[8,576,128]{2,1,0:T(8,128)(2,1)} %get-tuple-element.53), channel_id=1, source_target_pairs={{0,8},{32,40},{1,9},{33,41},{2,10},{34,42},{3,11},{35,43},{4,12},{... | collective-permute-start | bytes 3538952 | tf_op jit(solution)/shard_map/ppermute | solution.py:35
  8.6 35.9 %collective-permute-start.2 = (bf16[8,576,128]{2,1,0:T(8,128)(2,1)}, bf16[8,576,128]{2,1,0:T(8,128)(2,1)S(1)}, u32[]{:S(2)}, u32[]{:S(2)}) collective-permute-start(bf16[8,576,128]{2,1,0:T(8,128)(2,1)} %get-tuple-element.44), channel_id=1, source_target_pairs={{0,2},{32,34},{1,3},{33,35},{2,0},{34,32},{3,1},{35,33},{4,6},{36,... | collective-permute-start | bytes 3538952 | tf_op jit(solution)/shard_map/ppermute | solution.py:35
  11.8 8.5 %collective-permute-start = (bf16[2,576,128]{2,1,0:T(8,128)(2,1)S(1)}, bf16[2,576,128]{2,1,0:T(8,128)(2,1)S(1)}, u32[]{:S(2)}, u32[]{:S(2)}) collective-permute-start(bf16[2,576,128]{2,1,0:T(8,128)(2,1)S(1)} %slice.5), channel_id=1, source_target_pairs={{0,80},{32,112},{1,81},{33,113},{2,82},{34,114},{3,83},{35,115},{4... | collective-permute-start | bytes 884744 | tf_op jit(solution)/shard_map/ppermute | solution.py:35
  14.7 9.1 %collective-permute-start.1 = (bf16[2,576,128]{2,1,0:T(8,128)(2,1)S(1)}, bf16[2,576,128]{2,1,0:T(8,128)(2,1)S(1)}, u32[]{:S(2)}, u32[]{:S(2)}) collective-permute-start(bf16[2,576,128]{2,1,0:T(8,128)(2,1)S(1)} %slice.5), channel_id=1, source_target_pairs={{0,64},{32,96},{1,65},{33,97},{2,66},{34,98},{3,67},{35,99},{4,68}... | collective-permute-start | bytes 884744 | tf_op jit(solution)/shard_map/ppermute | solution.py:35
  23.8 17.3 %collective-permute-start.7 = (bf16[2,576,128]{2,1,0:T(8,128)(2,1)S(1)}, bf16[2,576,128]{2,1,0:T(8,128)(2,1)S(1)}, u32[]{:S(2)}, u32[]{:S(2)}) collective-permute-start(bf16[2,576,128]{2,1,0:T(8,128)(2,1)S(1)} %get-tuple-element.40.refs_4_.refs_8_), channel_id=1, source_target_pairs={{0,8},{32,40},{1,9},{33,41},{2,10},{34,42},{3,11},{35,43},{4,12},{... | collective-permute-start | bytes 884744 | tf_op jit(solution)/shard_map/ppermute | solution.py:35
  24.3 20.3 %collective-permute-start.3 = (bf16[2,576,128]{2,1,0:T(8,128)(2,1)S(1)}, bf16[2,576,128]{2,1,0:T(8,128)(2,1)S(1)}, u32[]{:S(2)}, u32[]{:S(2)}) collective-permute-start(bf16[2,576,128]{2,1,0:T(8,128)(2,1)S(1)} %get-tuple-element.41.refs_5_.refs_9_), channel_id=1, source_target_pairs={{0,2},{32,34},{1,3},{33,35},{2,0},{34,32},{3,1},{35,33},{4,6},{36,... | collective-permute-start | bytes 884744 | tf_op jit(solution)/shard_map/ppermute | solution.py:35
  38.4 9.5 %copy-start.1 = (s32[4,64]{1,0:T(4,128)S(1)}, s32[4,64]{1,0:T(4,128)}, u32[]{:S(2)}) copy-start(s32[4,64]{1,0:T(4,128)} %matching.13) | copy-start | bytes 3076
  41.1 34.8 %collective-permute-start.8 = (bf16[10,576,128]{2,1,0:T(8,128)(2,1)S(1)}, bf16[10,576,128]{2,1,0:T(8,128)(2,1)S(1)}, u32[]{:S(2)}, u32[]{:S(2)}) collective-permute-start(bf16[10,576,128]{2,1,0:T(8,128)(2,1)S(1)} %get-tuple-element.54), channel_id=1, source_target_pairs={{0,4},{32,36},{1,5},{33,37},{2,6},{34,38},{3,7},{35,39},{4,8},{36,... | collective-permute-start | bytes 4423688 | tf_op jit(solution)/shard_map/ppermute | solution.py:35
  42.4 33.5 %collective-permute-start.9 = (bf16[10,576,128]{2,1,0:T(8,128)(2,1)}, bf16[10,576,128]{2,1,0:T(8,128)(2,1)S(1)}, u32[]{:S(2)}, u32[]{:S(2)}) collective-permute-start(bf16[10,576,128]{2,1,0:T(8,128)(2,1)} %get-tuple-element.56), channel_id=1, source_target_pairs={{0,12},{32,44},{1,13},{33,45},{2,14},{34,46},{3,15},{35,47},{4,0},... | collective-permute-start | bytes 4423688 | tf_op jit(solution)/shard_map/ppermute | solution.py:35
  44.5 34.2 %copy-start.2 = (s32[4,64]{1,0:T(4,128)S(1)}, s32[4,64]{1,0:T(4,128)}, u32[]{:S(2)}) copy-start(s32[4,64]{1,0:T(4,128)} %lengths.7) | copy-start | bytes 3076
  44.6 34.2 %collective-permute-start.4 = (bf16[10,576,128]{2,1,0:T(8,128)(2,1)S(1)}, bf16[10,576,128]{2,1,0:T(8,128)(2,1)S(1)}, u32[]{:S(2)}, u32[]{:S(2)}) collective-permute-start(bf16[10,576,128]{2,1,0:T(8,128)(2,1)S(1)} %get-tuple-element.47), channel_id=1, source_target_pairs={{0,1},{32,33},{1,2},{33,34},{2,3},{34,35},{3,0},{35,32},{4,5},{36,... | collective-permute-start | bytes 4423688 | tf_op jit(solution)/shard_map/ppermute | solution.py:35
  46.2 32.6 %collective-permute-start.5 = (bf16[10,576,128]{2,1,0:T(8,128)(2,1)S(1)}, bf16[10,576,128]{2,1,0:T(8,128)(2,1)S(1)}, u32[]{:S(2)}, u32[]{:S(2)}) collective-permute-start(bf16[10,576,128]{2,1,0:T(8,128)(2,1)S(1)} %get-tuple-element.49), channel_id=1, source_target_pairs={{0,3},{32,35},{1,0},{33,32},{2,1},{34,33},{3,2},{35,34},{4,7},{36,... | collective-permute-start | bytes 4423688 | tf_op jit(solution)/shard_map/ppermute | solution.py:35
  80.8 10.8 %collective-permute-start.12 = (bf16[2,144,512]{2,1,0:T(8,128)(2,1)S(1)}, bf16[2,144,512]{2,1,0:T(8,128)(2,1)S(1)}, u32[]{:S(2)}, u32[]{:S(2)}) collective-permute-start(bf16[2,144,512]{2,1,0:T(8,128)(2,1)S(1)} %get-tuple-element.61), channel_id=1, source_target_pairs={{0,12},{32,44},{1,13},{33,45},{2,14},{34,46},{3,15},{35,47},{4,0},... | collective-permute-start | bytes 884744 | tf_op jit(solution)/shard_map/ppermute | solution.py:35
  82.6 11.0 %collective-permute-start.15 = (bf16[2,144,512]{2,1,0:T(8,128)(2,1)S(1)}, bf16[2,144,512]{2,1,0:T(8,128)(2,1)S(1)}, u32[]{:S(2)}, u32[]{:S(2)}) collective-permute-start(bf16[2,144,512]{2,1,0:T(8,128)(2,1)S(1)} %get-tuple-element.64), channel_id=1, source_target_pairs={{0,3},{32,35},{1,0},{33,32},{2,1},{34,33},{3,2},{35,34},{4,7},{36,... | collective-permute-start | bytes 884744 | tf_op jit(solution)/shard_map/ppermute | solution.py:35
  87.6 13.5 %collective-permute-start.11 = (bf16[2,144,512]{2,1,0:T(8,128)(2,1)S(1)}, bf16[2,144,512]{2,1,0:T(8,128)(2,1)S(1)}, u32[]{:S(2)}, u32[]{:S(2)}) collective-permute-start(bf16[2,144,512]{2,1,0:T(8,128)(2,1)S(1)} %get-tuple-element.60), channel_id=1, source_target_pairs={{0,4},{32,36},{1,5},{33,37},{2,6},{34,38},{3,7},{35,39},{4,8},{36,... | collective-permute-start | bytes 884744 | tf_op jit(solution)/shard_map/ppermute | solution.py:35
  88.0 13.8 %collective-permute-start.14 = (bf16[2,144,512]{2,1,0:T(8,128)(2,1)S(1)}, bf16[2,144,512]{2,1,0:T(8,128)(2,1)S(1)}, u32[]{:S(2)}, u32[]{:S(2)}) collective-permute-start(bf16[2,144,512]{2,1,0:T(8,128)(2,1)S(1)} %get-tuple-element.63), channel_id=1, source_target_pairs={{0,1},{32,33},{1,2},{33,34},{2,3},{34,35},{3,0},{35,32},{4,5},{36,... | collective-permute-start | bytes 884744 | tf_op jit(solution)/shard_map/ppermute | solution.py:35
  90.0 11.8 %collective-permute-start.10 = (bf16[2,144,512]{2,1,0:T(8,128)(2,1)S(1)}, bf16[2,144,512]{2,1,0:T(8,128)(2,1)S(1)}, u32[]{:S(2)}, u32[]{:S(2)}) collective-permute-start(bf16[2,144,512]{2,1,0:T(8,128)(2,1)S(1)} %get-tuple-element.59), channel_id=1, source_target_pairs={{0,8},{32,40},{1,9},{33,41},{2,10},{34,42},{3,11},{35,43},{4,12},{... | collective-permute-start | bytes 884744 | tf_op jit(solution)/shard_map/ppermute | solution.py:35
  91.6 10.2 %collective-permute-start.13 = (bf16[2,144,512]{2,1,0:T(8,128)(2,1)S(1)}, bf16[2,144,512]{2,1,0:T(8,128)(2,1)S(1)}, u32[]{:S(2)}, u32[]{:S(2)}) collective-permute-start(bf16[2,144,512]{2,1,0:T(8,128)(2,1)S(1)} %get-tuple-element.62), channel_id=1, source_target_pairs={{0,2},{32,34},{1,3},{33,35},{2,0},{34,32},{3,1},{35,33},{4,6},{36,... | collective-permute-start | bytes 884744 | tf_op jit(solution)/shard_map/ppermute | solution.py:35
  104.5 8.0 %collective-permute-start.16 = (bf16[2,144,512]{2,1,0:T(8,128)(2,1)S(1)}, bf16[2,144,512]{2,1,0:T(8,128)(2,1)S(1)}, u32[]{:S(2)}, u32[]{:S(2)}) collective-permute-start(bf16[2,144,512]{2,1,0:T(8,128)(2,1)S(1)} %get-tuple-element.65), channel_id=1, source_target_pairs={{0,64},{32,96},{1,65},{33,97},{2,66},{34,98},{3,67},{35,99},{4,68}... | collective-permute-start | bytes 884744 | tf_op jit(solution)/shard_map/ppermute | solution.py:35
  106.0 6.7 %collective-permute-start.17 = (bf16[2,144,512]{2,1,0:T(8,128)(2,1)S(1)}, bf16[2,144,512]{2,1,0:T(8,128)(2,1)S(1)}, u32[]{:S(2)}, u32[]{:S(2)}) collective-permute-start(bf16[2,144,512]{2,1,0:T(8,128)(2,1)S(1)} %get-tuple-element.66), channel_id=1, source_target_pairs={{0,80},{32,112},{1,81},{33,113},{2,82},{34,114},{3,83},{35,115},{4... | collective-permute-start | bytes 884744 | tf_op jit(solution)/shard_map/ppermute | solution.py:35

commit v3 on v2

--- a/solution.py
+++ b/solution.py
@@ -15,7 +15,7 @@
 AXES = ("section", "dev")
 SMALL_VMEM = 16 * 1024 * 1024
 GATHER_VMEM = 48 * 1024 * 1024
-LARGE_VMEM = 56 * 1024 * 1024
+LARGE_VMEM = 46 * 1024 * 1024
 
 
 def place(x, z, y, core):
@@ -91,41 +91,48 @@
     )(meta, matching, cache)
 
 
-def own_kernel(plus, minus, qa, qb):
-    for half, out in enumerate((qa, qb)):
+def pack_kernel(own, far_a, far_b, out):
+    out[:2] = own[...]
+    out[2] = far_a[0]
+    out[3] = far_b[0]
+
+
+def pack_queries(queries, far_a, far_b):
+    shape = queries.shape[1:]
+    single = pl.BlockSpec((1,) + shape, lambda i: (0, 0, 0))
+    return pl.pallas_call(
+        pack_kernel,
+        out_shape=jax.ShapeDtypeStruct((4,) + shape, queries.dtype),
+        grid=(1,),
+        in_specs=[pl.BlockSpec((2,) + shape, lambda i: (1, 0, 0)), single, single],
+        out_specs=pl.BlockSpec((4,) + shape, lambda i: (0, 0, 0)),
+        compiler_params=pltpu.CompilerParams(vmem_limit_bytes=SMALL_VMEM),
+        name="pack_queries",
+    )(queries, far_a, far_b)
+
+
+def fill_kernel(halves, *refs):
+    count = len(halves)
+    plus, minus = refs[count : count + 2]
+    for half, out in zip(halves, refs[count + 2 :]):
         out[0] = plus[half]
         out[1] = minus[half]
 
 
-def own_queries(plus, minus):
-    return pl.pallas_call(
-        own_kernel,
-        out_shape=[jax.ShapeDtypeStruct(plus.shape, plus.dtype)] * 2,
-        compiler_params=pltpu.CompilerParams(vmem_limit_bytes=SMALL_VMEM),
-        name="own_queries",
-    )(plus, minus)
-
-
-def fill_kernel(halves, *refs):
-    count = len(halves)
-    queries = refs[count : count + 2]
-    for half, out in zip(halves, refs[count + 2 :]):
-        out[...] = queries[half][...]
-
-
-def fill_queries(halves, arrays, qa, qb):
+def fill_queries(halves, arrays, plus, minus):
     count = len(arrays)
-    whole = pl.BlockSpec(qa.shape, lambda i: (0, 0, 0))
+    shape = arrays[0].shape[1:]
+    own = pl.BlockSpec((2,) + shape, lambda i: (0, 0, 0))
     return pl.pallas_call(
         functools.partial(fill_kernel, halves),
         out_shape=[jax.ShapeDtypeStruct(x.shape, x.dtype) for x in arrays],
         grid=(1,),
-        in_specs=[pl.BlockSpec(memory_space=pl.ANY)] * count + [whole] * 2,
-        out_specs=[pl.BlockSpec(qa.shape, lambda i: (RING, 0, 0))] * count,
+        in_specs=[pl.BlockSpec(memory_space=pl.ANY)] * count + [own] * 2,
+        out_specs=[pl.BlockSpec((2,) + shape, lambda i: (RING, 0, 0))] * count,
         input_output_aliases={i: i for i in range(count)},
         compiler_params=pltpu.CompilerParams(vmem_limit_bytes=SMALL_VMEM),
         name="fill_queries",
-    )(*arrays, qa, qb)
+    )(*arrays, plus, minus)
 
 
 def weigh(blocks):
@@ -192,8 +199,8 @@
     high, middle, low = split_stat(row)
     rows = lax.broadcasted_iota(jnp.int32, (STAT_ROWS, heads), 0)
     block = jnp.where(rows == 0, high, jnp.where(rows == 1, middle, jnp.where(rows == 2, low, 0.0)))
-    out[index, heads:, :heads] = block.astype(jnp.bfloat16)
-    out[index, heads:, heads:] = jnp.zeros((STAT_ROWS, KV_RANK - heads), jnp.bfloat16)
+    out[index, heads:, :heads] = block.astype(out.dtype)
+    out[index, heads:, heads:] = jnp.zeros((STAT_ROWS, KV_RANK - heads), out.dtype)
 
 
 def slots_of(meta, half, away, span):
@@ -214,7 +221,7 @@
             request = request_of(meta, matching, half, side, 0, step)
             live = slots < lengths[meta[0], request]
             keys = jnp.concatenate([segment[2 * step + side] for segment in segments], axis=1)
-            blocks.append((queries[half][side].T, keys, live))
+            blocks.append((queries[half][side][...].T, keys, live))
     mixed, tops, totals = weigh(blocks)
     return [(m / t, stat_row(top, t)) for m, top, t in zip(mixed, tops, totals)]
 
@@ -228,28 +235,29 @@
     for index, (value, row) in enumerate(results):
         half, side = divmod(index, 2)
         heads = value.shape[0]
-        outs[half][side, :heads] = value.astype(jnp.bfloat16)
+        outs[half][side, :heads] = value.astype(outs[half].dtype)
         put_stat(outs[half], side, row)
 
 
 def partial_kernel(step, meta, matching, lengths, *refs):
-    a, b, qa, qb, outs = refs[:RING], refs[RING : 2 * RING], refs[2 * RING], refs[2 * RING + 1], refs[2 * RING + 2 :]
-    if step != 2:
-        back = RING - step
-        qa, qb = b[back].at[2 * RING :], a[back].at[2 * RING :]
-    put_results(outs, ring_results(step, meta, matching, lengths, a, b, (qa, qb)))
-
-
-def ring_call(kernel, operands, arrays, name):
-    meta, matching, lengths = operands
+    a, b, plus, minus, outs = refs[:RING], refs[RING : 2 * RING], refs[8], refs[9], refs[10:]
+    if step % 2:
+        queries = [[ref.at[2 * RING + side] for side in range(2)] for ref in (b[RING - step], a[RING - step])]
+    else:
+        queries = [[plus.at[step + half], minus.at[step + half]] for half in range(2)]
+    put_results(outs, ring_results(step, meta, matching, lengths, a, b, queries))
+
+
+def partials(step, meta, matching, lengths, arrays):
     width, span = arrays[0].shape[1:]
     heads = span
     work = 4 * heads * span * RING
     whole = pl.BlockSpec(memory_space=pltpu.VMEM)
     shape = (2, heads + STAT_ROWS, KV_RANK)
-    return pl.pallas_call(
-        kernel,
-        out_shape=[pltpu.VMEM(shape, jnp.bfloat16)] * 2,
+    dtype = jnp.bfloat16 if step else jnp.float32
+    return pl.pallas_call(
+        functools.partial(partial_kernel, step),
+        out_shape=[pltpu.VMEM(shape, dtype)] * 2,
         grid_spec=pltpu.PrefetchScalarGridSpec(
             num_scalar_prefetch=3,
             grid=(1,),
@@ -262,7 +270,7 @@
             bytes_accessed=8 * RING * width * span,
             transcendentals=work,
         ),
-        name=name,
+        name="partials",
     )(meta, matching, lengths, *arrays)
 
 
@@ -285,15 +293,25 @@
     return block[:heads].astype(jnp.float32), rows[0:1] + rows[1:2] + rows[2:3]
 
 
-def middle_kernel(meta, matching, lengths, *refs):
-    a, b, queries, ins, outs = refs[:RING], refs[RING : 2 * RING], refs[8:10], refs[10:16], refs[16:]
-    near = ring_results(0, meta, matching, lengths, a, b, queries)
+def middle_kernel(*refs):
+    ins, outs = refs[: 2 * RING], refs[2 * RING :]
     for half in range(2):
         for side in range(2):
-            parts = [near[2 * half + side]] + [received(ref[side]) for ref in ins[3 * half : 3 * half + 3]]
-            mixed, row = merge(parts)
+            mixed, row = merge([received(ref[side]) for ref in ins[half * RING : (half + 1) * RING]])
             outs[side][half, : mixed.shape[0]] = mixed.astype(jnp.bfloat16)
             put_stat(outs[side], half, row)
+
+
+def middle(parts):
+    whole = pl.BlockSpec(memory_space=pltpu.VMEM)
+    return pl.pallas_call(
+        middle_kernel,
+        out_shape=[pltpu.VMEM(parts[-1].shape, jnp.bfloat16)] * 2,
+        in_specs=[whole] * (2 * RING),
+        out_specs=[whole] * 2,
+        compiler_params=pltpu.CompilerParams(vmem_limit_bytes=SMALL_VMEM),
+        name="middle",
+    )(*parts)
 
 
 def last_kernel(base, plus, minus, out):
@@ -324,35 +342,35 @@
     res_cache = jnp.swapaxes(res_cache[0], 1, 2)
     inc_cache = jnp.swapaxes(inc_cache[0], 1, 2)
 
-    from_minus = move(queries[2:], dx=1)
-    from_plus = move(queries[2:], dx=-1)
+    far_a = move(queries[2:3], dz=2)
+    far_b = move(queries[3:4], dy=2)
     a2, b2 = gather_requests(((0, 2), (1, 2)), 0, meta, matching, inc_cache)
+    a2, b2, far_a, far_b = lax.optimization_barrier((a2, b2, far_a, far_b))
     a2 = move(a2, dy=2)
     b2 = move(b2, dz=2)
-    qa, qb = own_queries(from_plus, from_minus)
-    qa_far = move(qa, dz=2)
-    qb_far = move(qb, dy=2)
+    packed = pack_queries(queries, far_a, far_b)
+    from_minus = move(packed, dx=1)
+    from_plus = move(packed, dx=-1)
     sent = gather_requests(((0, 1), (0, 3), (1, 1), (1, 3)), 2, meta, matching, inc_cache)
-    a1, a3, b1, b3 = fill_queries((1, 1, 0, 0), sent, qa, qb)
-    base = resident_rows(res_lengths[0], queries, res_cache)
-    a1, a3, a2, qb_far, base = lax.optimization_barrier((a1, a3, a2, qb_far, base))
-    b1, b3, b2, qa_far = lax.optimization_barrier((b1, b3, b2, qa_far))
+    a1, a3, b1, b3 = fill_queries((1, 1, 0, 0), sent, from_plus, from_minus)
     a1 = move(a1, dy=1)
+    b1 = move(b1, dz=1)
     a3 = move(a3, dy=-1)
-    b1 = move(b1, dz=1)
+    b3, a2, b2, lengths = lax.optimization_barrier((b3, a2, b2, res_lengths[0]))
     b3 = move(b3, dz=-1)
-    a0, b0 = gather_requests(((0, 0), (1, 0)), 0, meta, matching, inc_cache)
-
-    operands = (meta, matching, inc_lengths)
-    segments = (a0, a1, a2, a3, b0, b1, b2, b3)
+    base = resident_rows(lengths, queries, res_cache)
+    later, base = lax.optimization_barrier((meta, base))
+    a0, b0 = gather_requests(((0, 0), (1, 0)), 0, later, matching, inc_cache)
+
+    arrays = (a0, a1, a2, a3, b0, b1, b2, b3, from_plus, from_minus)
     pa, pb = [], []
-    for step in (2, 1, 3):
-        found = ring_call(
-            functools.partial(partial_kernel, step), operands, (*segments, qa_far, qb_far), "partials"
-        )
-        pa.append(move(found[0], dz=step))
-        pb.append(move(found[1], dy=step))
-    to_plus, to_minus = ring_call(middle_kernel, operands, (*segments, qa, qb, *pa, *pb), "middle")
+    order = meta
+    for step in (2, 1, 3, 0):
+        for_a, for_b = partials(step, order, matching, inc_lengths, arrays)
+        order, for_a, for_b = lax.optimization_barrier((order, for_a, for_b))
+        pa.append(move(for_a, dz=step) if step else for_a)
+        pb.append(move(for_b, dy=step) if step else for_b)
+    to_plus, to_minus = middle(pa + pb)
     plus = move(to_plus, dx=1)
     minus = move(to_minus, dx=-1)
     return last(base, plus, minus)[None]

time: 114 us -> 107 us (0.939)
  waiting for transfers between devices: 52.7 us -> 37.8 us
  starting transfers between devices: 29.6 us -> 36.4 us
    ppermute x18, waiting for transfers between devices: 52.7 us -> 37.8 us  [move(): return lax.ppermute(block, AXES, route)]
    ppermute x18, starting transfers between devices: 29.6 us -> 36.4 us  [move(): return lax.ppermute(block, AXES, route)]
    pallas_call x5 -> x6, Pallas kernels: 8.71 us -> 8.87 us  [the longest x4 7.98 us: partials(): pl.pallas_call(functools.partial(partial_kernel, step), out_shape=[pltpu....]
  transfers between devices with their start and end apart: 18 -> 18, of which waited for: 9 -> 12; matrix products, arithmetic and copies ran while one was open for 0% -> 0% of each run, Pallas kernels for 18% -> 24%
where the time goes in v3:
time: 107 us; the launch traced here: 106 us
  waiting for transfers between devices  37.8 us (35%)
  starting transfers between devices  36.4 us (34%)
  Pallas kernels  29.7 us (28%)
  local copies, waits for them, and re-layouts  1.78 us (2%)
    ppermute x18, waiting for transfers between devices, move(): return lax.ppermute(block, AXES, route)  37.8 us
    ppermute x18, starting transfers between devices, move(): return lax.ppermute(block, AXES, route)  36.4 us
    pallas_call x3, Pallas kernels, gather_requests(): pl.pallas_call(functools.partial(gather_kernel, steps), out_shape=[pltpu....  9.74 us
    pallas_call x1, Pallas kernels, resident_rows(): pl.pallas_call(resident_kernel, out_shape=jax.ShapeDtypeStruct((queries.s...  9.11 us
    pallas_call x4, Pallas kernels, partials(): pl.pallas_call(functools.partial(partial_kernel, step), out_shape=[pltpu....  7.98 us
  transfers between devices with their start and end apart: 18, of which 12 were waited for; matrix products, arithmetic and copies ran while one was open for 0% of the time, Pallas kernels for 24%

profile of v3, /device:TPU:0, one launch (start us, length us, event | category | flops | bytes accessed | tf_op | source)
XLA Modules:
  0.0 105.9 jit_solution(8209502073717768179)
XLA Ops:
  0.0 1.0 fusion
  1.0 3.4 %collective-permute-start.1 = (bf16[1,576,128]{2,1,0:T(8,128)(2,1)S(1)}, bf16[1,576,128]{2,1,0:T(8,128)(2,1)S(1)}, u32[]{:S(2)}, u32[]{:S(2)}) collective-permute-start(bf16[1,576,128]{2,1,0:T(8,128)(2,1)S(1)} %get-tuple-element.91), channel_id=1, source_target_pairs={{0,2},{32,34},{1,3},{33,35},{2,0},{34,32},{3,1},{35,33},{4,6},{36,... | collective-permute-start | bytes 442376 | tf_op jit(solution)/shard_map/ppermute | solution.py:35
  4.4 3.9 %collective-permute-start = (bf16[1,576,128]{2,1,0:T(8,128)(2,1)S(1)}, bf16[1,576,128]{2,1,0:T(8,128)(2,1)S(1)}, u32[]{:S(2)}, u32[]{:S(2)}) collective-permute-start(bf16[1,576,128]{2,1,0:T(8,128)(2,1)S(1)} %get-tuple-element.92), channel_id=1, source_target_pairs={{0,8},{32,40},{1,9},{33,41},{2,10},{34,42},{3,11},{35,43},{4,12},{... | collective-permute-start | bytes 442376 | tf_op jit(solution)/shard_map/ppermute | solution.py:35
  8.2 0.1 stack.27.meta
  8.3 0.7 copy-done.1
  9.0 2.4 %gather_requests.4 = (bf16[8,576,128]{2,1,0:T(8,128)(2,1)S(1)}, bf16[8,576,128]{2,1,0:T(8,128)(2,1)S(1)}) custom-call(s32[6]{0:T(128)S(1)} %stack.27.meta, s32[4,64]{1,0:T(4,128)S(1)} %copy-done.1, bf16[64,576,128]{2,1,0:T(8,128)(2,1)} %bitcast.21), custom_call_target="tpu_custom_call" | custom-call | bytes 4718592 | tf_op jit(solution)/shard_map/gather_requests/pallas_call | solution.py:78
  11.4 0.0 collective-permute-done.1.far_b
  11.5 0.3 collective-permute-done.far_a
  11.8 0.4 collective-permute-start.4
  12.2 3.2 %collective-permute-start.5 = (bf16[8,576,128]{2,1,0:T(8,128)(2,1)S(1)}, bf16[8,576,128]{2,1,0:T(8,128)(2,1)S(1)}, u32[]{:S(2)}, u32[]{:S(2)}) collective-permute-start(bf16[8,576,128]{2,1,0:T(8,128)(2,1)S(1)} %get-tuple-element.58), channel_id=1, source_target_pairs={{0,8},{32,40},{1,9},{33,41},{2,10},{34,42},{3,11},{35,43},{4,12},{... | collective-permute-start | bytes 3538952 | tf_op jit(solution)/shard_map/ppermute | solution.py:35
  15.5 1.6 %collective-permute-start.3 = (bf16[4,576,128]{2,1,0:T(8,128)(2,1)S(1)}, bf16[4,576,128]{2,1,0:T(8,128)(2,1)S(1)}, u32[]{:S(2)}, u32[]{:S(2)}) collective-permute-start(bf16[4,576,128]{2,1,0:T(8,128)(2,1)S(1)} %pack_queries.1), channel_id=1, source_target_pairs={{0,64},{32,96},{1,65},{33,97},{2,66},{34,98},{3,67},{35,99},{4,68}... | collective-permute-start | bytes 1769480 | tf_op jit(solution)/shard_map/ppermute | solution.py:35
  17.0 1.7 %collective-permute-start.2 = (bf16[4,576,128]{2,1,0:T(8,128)(2,1)S(1)}, bf16[4,576,128]{2,1,0:T(8,128)(2,1)S(1)}, u32[]{:S(2)}, u32[]{:S(2)}) collective-permute-start(bf16[4,576,128]{2,1,0:T(8,128)(2,1)S(1)} %pack_queries.1), channel_id=1, source_target_pairs={{0,80},{32,112},{1,81},{33,113},{2,82},{34,114},{3,83},{35,115},{4... | collective-permute-start | bytes 1769480 | tf_op jit(solution)/shard_map/ppermute | solution.py:35
  18.8 4.9 %gather_requests.3 = (bf16[10,576,128]{2,1,0:T(8,128)(2,1)S(1)}, bf16[10,576,128]{2,1,0:T(8,128)(2,1)S(1)}, bf16[10,576,128]{2,1,0:T(8,128)(2,1)}, bf16[10,576,128]{2,1,0:T(8,128)(2,1)}) custom-call(s32[6]{0:T(128)S(1)} %stack.27.meta, s32[4,64]{1,0:T(4,128)S(1)} %copy-done.1, bf16[64,576,128]{2,1,0:T(8,128)(2,1)} %bitcast.22), custom_call_target="tpu_custom_call" | custom-call | bytes 9437184 | tf_op jit(solution)/shard_map/gather_requests/pallas_call | solution.py:78
  23.7 6.6 %collective-permute-done.3.refs_5_.refs_9_ = bf16[4,576,128]{2,1,0:T(8,128)(2,1)S(1)} collective-permute-done((bf16[4,576,128]{2,1,0:T(8,128)(2,1)S(1)}, bf16[4,576,128]{2,1,0:T(8,128)(2,1)S(1)}, u32[]{:S(2)}, u32[]{:S(2)}) %collective-permute-start.3) | collective-permute-done | bytes 589856 | tf_op jit(solution)/shard_map/ppermute | solution.py:35
  30.3 0.0 collective-permute-done.2.refs_4_.refs_8_
  30.3 1.0 fill_queries.1
  31.3 1.3 %collective-permute-start.6 = (bf16[10,576,128]{2,1,0:T(8,128)(2,1)S(1)}, bf16[10,576,128]{2,1,0:T(8,128)(2,1)S(1)}, u32[]{:S(2)}, u32[]{:S(2)}) collective-permute-start(bf16[10,576,128]{2,1,0:T(8,128)(2,1)S(1)} %get-tuple-element.63), channel_id=1, source_target_pairs={{0,1},{32,33},{1,2},{33,34},{2,3},{34,35},{3,0},{35,32},{4,5},{36,... | collective-permute-start | bytes 4423688 | tf_op jit(solution)/shard_map/ppermute | solution.py:35
  32.6 1.9 %collective-permute-start.7 = (bf16[10,576,128]{2,1,0:T(8,128)(2,1)S(1)}, bf16[10,576,128]{2,1,0:T(8,128)(2,1)S(1)}, u32[]{:S(2)}, u32[]{:S(2)}) collective-permute-start(bf16[10,576,128]{2,1,0:T(8,128)(2,1)S(1)} %get-tuple-element.65), channel_id=1, source_target_pairs={{0,3},{32,35},{1,0},{33,32},{2,1},{34,33},{3,2},{35,34},{4,7},{36,... | collective-permute-start | bytes 4423688 | tf_op jit(solution)/shard_map/ppermute | solution.py:35
  34.5 1.0 collective-permute-start.8
  35.5 6.7 %collective-permute-done.4.refs_2_ = bf16[8,576,128]{2,1,0:T(8,128)(2,1)S(1)} collective-permute-done((bf16[8,576,128]{2,1,0:T(8,128)(2,1)S(1)}, bf16[8,576,128]{2,1,0:T(8,128)(2,1)S(1)}, u32[]{:S(2)}, u32[]{:S(2)}) %collective-permute-start.4) | collective-permute-done | bytes 1179680 | tf_op jit(solution)/shard_map/ppermute | solution.py:35
  42.3 0.4 collective-permute-done.5.refs_6_
  42.6 3.0 %collective-permute-start.9 = (bf16[10,576,128]{2,1,0:T(8,128)(2,1)}, bf16[10,576,128]{2,1,0:T(8,128)(2,1)S(1)}, u32[]{:S(2)}, u32[]{:S(2)}) collective-permute-start(bf16[10,576,128]{2,1,0:T(8,128)(2,1)} %get-tuple-element.69), channel_id=1, source_target_pairs={{0,12},{32,44},{1,13},{33,45},{2,14},{34,46},{3,15},{35,47},{4,0},... | collective-permute-start | bytes 4423688 | tf_op jit(solution)/shard_map/ppermute | solution.py:35
  45.7 9.1 %resident_rows.1.base = bf16[4,128,512]{2,1,0:T(8,128)(2,1)} custom-call(s32[2]{0:T(128)S(1)} %bitcast.20, bf16[4,576,128]{2,1,0:T(8,128)(2,1)S(1)} %bitcast.19, bf16[2,576,4096]{2,1,0:T(8,128)(2,1)} %bitcast.24), custom_call_target="tpu_custom_call" | custom-call | flops 2281701376 | bytes 9437184 | tf_op jit(solution)/shard_map/resident_rows/pallas_call | solution.py:168
  54.8 2.4 %gather_requests.5 = (bf16[8,576,128]{2,1,0:T(8,128)(2,1)S(1)}, bf16[8,576,128]{2,1,0:T(8,128)(2,1)S(1)}) custom-call(s32[6]{0:T(128)S(1)} %stack.27.meta, s32[4,64]{1,0:T(4,128)S(1)} %copy-done.1, bf16[64,576,128]{2,1,0:T(8,128)(2,1)} %bitcast.23), custom_call_target="tpu_custom_call" | custom-call | bytes 4718592 | tf_op jit(solution)/shard_map/gather_requests/pallas_call | solution.py:78
  57.2 14.6 %collective-permute-done.6.refs_1_ = bf16[10,576,128]{2,1,0:T(8,128)(2,1)S(1)} collective-permute-done((bf16[10,576,128]{2,1,0:T(8,128)(2,1)S(1)}, bf16[10,576,128]{2,1,0:T(8,128)(2,1)S(1)}, u32[]{:S(2)}, u32[]{:S(2)}) %collective-permute-start.6) | collective-permute-done | bytes 1474592 | tf_op jit(solution)/shard_map/ppermute | solution.py:35
  71.8 0.0 collective-permute-done.7.refs_3_
  71.8 0.1 collective-permute-done.8.refs_5_
  71.9 1.4 %collective-permute-done.9.refs_7_ = bf16[10,576,128]{2,1,0:T(8,128)(2,1)S(1)} collective-permute-done((bf16[10,576,128]{2,1,0:T(8,128)(2,1)}, bf16[10,576,128]{2,1,0:T(8,128)(2,1)S(1)}, u32[]{:S(2)}, u32[]{:S(2)}) %collective-permute-start.9) | collective-permute-done | bytes 1474592 | tf_op jit(solution)/shard_map/ppermute | solution.py:35
  73.3 2.0 %partials.4 = (bf16[2,144,512]{2,1,0:T(8,128)(2,1)S(1)}, bf16[2,144,512]{2,1,0:T(8,128)(2,1)S(1)}) custom-call(s32[6]{0:T(128)S(1)} %stack.27.meta, s32[4,64]{1,0:T(4,128)S(1)} %copy-done.1, s32[4,64]{1,0:T(4,128)S(1)} %copy-done.2, bf16[8,576,128]{2,1,0:T(8,128)(2,1)S(1)} %get-tuple-element.62.refs_0_, ...), custom_call_target="tpu_custom_call" | custom-call | flops 570425344 | bytes 2359296 | tf_op jit(solution)/shard_map/partials/pallas_call | solution.py:258
  75.2 2.3 %collective-permute-start.10 = (bf16[2,144,512]{2,1,0:T(8,128)(2,1)S(1)}, bf16[2,144,512]{2,1,0:T(8,128)(2,1)S(1)}, u32[]{:S(2)}, u32[]{:S(2)}) collective-permute-start(bf16[2,144,512]{2,1,0:T(8,128)(2,1)S(1)} %get-tuple-element.72), channel_id=1, source_target_pairs={{0,8},{32,40},{1,9},{33,41},{2,10},{34,42},{3,11},{35,43},{4,12},{... | collective-permute-start | bytes 884744 | tf_op jit(solution)/shard_map/ppermute | solution.py:35
  77.6 2.7 %collective-permute-start.13 = (bf16[2,144,512]{2,1,0:T(8,128)(2,1)S(1)}, bf16[2,144,512]{2,1,0:T(8,128)(2,1)S(1)}, u32[]{:S(2)}, u32[]{:S(2)}) collective-permute-start(bf16[2,144,512]{2,1,0:T(8,128)(2,1)S(1)} %get-tuple-element.85), channel_id=1, source_target_pairs={{0,2},{32,34},{1,3},{33,35},{2,0},{34,32},{3,1},{35,33},{4,6},{36,... | collective-permute-start | bytes 884744 | tf_op jit(solution)/shard_map/ppermute | solution.py:35
  80.3 2.0 %partials.5 = (bf16[2,144,512]{2,1,0:T(8,128)(2,1)S(1)}, bf16[2,144,512]{2,1,0:T(8,128)(2,1)S(1)}) custom-call(s32[6]{0:T(128)S(1)} %stack.27.meta, s32[4,64]{1,0:T(4,128)S(1)} %copy-done.1, s32[4,64]{1,0:T(4,128)S(1)} %copy-done.2, bf16[8,576,128]{2,1,0:T(8,128)(2,1)S(1)} %get-tuple-element.62.refs_0_, ...), custom_call_target="tpu_custom_call" | custom-call | flops 570425344 | bytes 2359296 | tf_op jit(solution)/shard_map/partials/pallas_call | solution.py:258
  82.3 2.3 %collective-permute-start.11 = (bf16[2,144,512]{2,1,0:T(8,128)(2,1)S(1)}, bf16[2,144,512]{2,1,0:T(8,128)(2,1)S(1)}, u32[]{:S(2)}, u32[]{:S(2)}) collective-permute-start(bf16[2,144,512]{2,1,0:T(8,128)(2,1)S(1)} %get-tuple-element.76), channel_id=1, source_target_pairs={{0,4},{32,36},{1,5},{33,37},{2,6},{34,38},{3,7},{35,39},{4,8},{36,... | collective-permute-start | bytes 884744 | tf_op jit(solution)/shard_map/ppermute | solution.py:35
  84.6 0.7 collective-permute-start.14
  85.2 2.0 %partials.6 = (bf16[2,144,512]{2,1,0:T(8,128)(2,1)S(1)}, bf16[2,144,512]{2,1,0:T(8,128)(2,1)S(1)}) custom-call(s32[6]{0:T(128)S(1)} %stack.27.meta, s32[4,64]{1,0:T(4,128)S(1)} %copy-done.1, s32[4,64]{1,0:T(4,128)S(1)} %copy-done.2, bf16[8,576,128]{2,1,0:T(8,128)(2,1)S(1)} %get-tuple-element.62.refs_0_, ...), custom_call_target="tpu_custom_call" | custom-call | flops 570425344 | bytes 2359296 | tf_op jit(solution)/shard_map/partials/pallas_call | solution.py:258
  87.2 1.1 %collective-permute-start.12 = (bf16[2,144,512]{2,1,0:T(8,128)(2,1)S(1)}, bf16[2,144,512]{2,1,0:T(8,128)(2,1)S(1)}, u32[]{:S(2)}, u32[]{:S(2)}) collective-permute-start(bf16[2,144,512]{2,1,0:T(8,128)(2,1)S(1)} %get-tuple-element.80), channel_id=1, source_target_pairs={{0,12},{32,44},{1,13},{33,45},{2,14},{34,46},{3,15},{35,47},{4,0},... | collective-permute-start | bytes 884744 | tf_op jit(solution)/shard_map/ppermute | solution.py:35
  88.4 2.6 %collective-permute-start.15 = (bf16[2,144,512]{2,1,0:T(8,128)(2,1)S(1)}, bf16[2,144,512]{2,1,0:T(8,128)(2,1)S(1)}, u32[]{:S(2)}, u32[]{:S(2)}) collective-permute-start(bf16[2,144,512]{2,1,0:T(8,128)(2,1)S(1)} %get-tuple-element.87), channel_id=1, source_target_pairs={{0,3},{32,35},{1,0},{33,32},{2,1},{34,33},{3,2},{35,34},{4,7},{36,... | collective-permute-start | bytes 884744 | tf_op jit(solution)/shard_map/ppermute | solution.py:35
  90.9 2.0 %partials.7 = (f32[2,144,512]{2,1,0:T(8,128)S(1)}, f32[2,144,512]{2,1,0:T(8,128)S(1)}) custom-call(s32[6]{0:T(128)S(1)} %stack.27.meta, s32[4,64]{1,0:T(4,128)S(1)} %copy-done.1, s32[4,64]{1,0:T(4,128)S(1)} %copy-done.2, bf16[8,576,128]{2,1,0:T(8,128)(2,1)S(1)} %get-tuple-element.62.refs_0_, bf16[10,576,128]{2,1,0:T(8,128)(2,1)S(1)} %collective-permute-done.6.refs_1_, ...), custom_call_target="tpu_custom_call" | custom-call | flops 570425344 | bytes 2359296 | tf_op jit(solution)/shard_map/partials/pallas_call | solution.py:258
  92.9 0.0 collective-permute-done.11.refs_1_
  92.9 0.6 collective-permute-done.14.refs_5_
  93.6 0.5 collective-permute-done.12.refs_2_
  94.0 1.7 %collective-permute-done.15.refs_6_ = bf16[2,144,512]{2,1,0:T(8,128)(2,1)S(1)} collective-permute-done((bf16[2,144,512]{2,1,0:T(8,128)(2,1)S(1)}, bf16[2,144,512]{2,1,0:T(8,128)(2,1)S(1)}, u32[]{:S(2)}, u32[]{:S(2)}) %collective-permute-start.15) | collective-permute-done | bytes 294944 | tf_op jit(solution)/shard_map/ppermute | solution.py:35
  95.7 0.9 middle.1
  96.5 1.6 %collective-permute-start.16 = (bf16[2,144,512]{2,1,0:T(8,128)(2,1)S(1)}, bf16[2,144,512]{2,1,0:T(8,128)(2,1)S(1)}, u32[]{:S(2)}, u32[]{:S(2)}) collective-permute-start(bf16[2,144,512]{2,1,0:T(8,128)(2,1)S(1)} %get-tuple-element.89), channel_id=1, source_target_pairs={{0,64},{32,96},{1,65},{33,97},{2,66},{34,98},{3,67},{35,99},{4,68}... | collective-permute-start | bytes 884744 | tf_op jit(solution)/shard_map/ppermute | solution.py:35
  98.1 1.7 %collective-permute-start.17 = (bf16[2,144,512]{2,1,0:T(8,128)(2,1)S(1)}, bf16[2,144,512]{2,1,0:T(8,128)(2,1)S(1)}, u32[]{:S(2)}, u32[]{:S(2)}) collective-permute-start(bf16[2,144,512]{2,1,0:T(8,128)(2,1)S(1)} %get-tuple-element.90), channel_id=1, source_target_pairs={{0,80},{32,112},{1,81},{33,113},{2,82},{34,114},{3,83},{35,115},{4... | collective-permute-start | bytes 884744 | tf_op jit(solution)/shard_map/ppermute | solution.py:35
  99.8 4.7 %collective-permute-done.16.plus = bf16[2,144,512]{2,1,0:T(8,128)(2,1)S(1)} collective-permute-done((bf16[2,144,512]{2,1,0:T(8,128)(2,1)S(1)}, bf16[2,144,512]{2,1,0:T(8,128)(2,1)S(1)}, u32[]{:S(2)}, u32[]{:S(2)}) %collective-permute-start.16) | collective-permute-done | bytes 294944 | tf_op jit(solution)/shard_map/ppermute | solution.py:35
  104.5 0.3 collective-permute-done.17.minus
  104.8 1.0 last.1
  (10 shorter events, 0.1 us)
Async XLA Ops:
  1.0 10.4 %collective-permute-start.1 = (bf16[1,576,128]{2,1,0:T(8,128)(2,1)S(1)}, bf16[1,576,128]{2,1,0:T(8,128)(2,1)S(1)}, u32[]{:S(2)}, u32[]{:S(2)}) collective-permute-start(bf16[1,576,128]{2,1,0:T(8,128)(2,1)S(1)} %get-tuple-element.91), channel_id=1, source_target_pairs={{0,2},{32,34},{1,3},{33,35},{2,0},{34,32},{3,1},{35,33},{4,6},{36,... | collective-permute-start | bytes 442376 | tf_op jit(solution)/shard_map/ppermute | solution.py:35
  4.4 7.4 %collective-permute-start = (bf16[1,576,128]{2,1,0:T(8,128)(2,1)S(1)}, bf16[1,576,128]{2,1,0:T(8,128)(2,1)S(1)}, u32[]{:S(2)}, u32[]{:S(2)}) collective-permute-start(bf16[1,576,128]{2,1,0:T(8,128)(2,1)S(1)} %get-tuple-element.92), channel_id=1, source_target_pairs={{0,8},{32,40},{1,9},{33,41},{2,10},{34,42},{3,11},{35,43},{4,12},{... | collective-permute-start | bytes 442376 | tf_op jit(solution)/shard_map/ppermute | solution.py:35
  8.3 0.7 copy-start.1
  9.0 6.4 %copy-start = (bf16[1,4,128,576]{2,3,1,0:T(8,128)(2,1)S(1)}, bf16[1,4,128,576]{2,3,1,0:T(8,128)(2,1)}, u32[]{:S(2)}) copy-start(bf16[1,4,128,576]{2,3,1,0:T(8,128)(2,1)} %param.6) | copy-start | bytes 1769476
  11.8 30.5 %collective-permute-start.4 = (bf16[8,576,128]{2,1,0:T(8,128)(2,1)S(1)}, bf16[8,576,128]{2,1,0:T(8,128)(2,1)S(1)}, u32[]{:S(2)}, u32[]{:S(2)}) collective-permute-start(bf16[8,576,128]{2,1,0:T(8,128)(2,1)S(1)} %get-tuple-element.57), channel_id=1, source_target_pairs={{0,2},{32,34},{1,3},{33,35},{2,0},{34,32},{3,1},{35,33},{4,6},{36,... | collective-permute-start | bytes 3538952 | tf_op jit(solution)/shard_map/ppermute | solution.py:35
  12.2 30.5 %collective-permute-start.5 = (bf16[8,576,128]{2,1,0:T(8,128)(2,1)S(1)}, bf16[8,576,128]{2,1,0:T(8,128)(2,1)S(1)}, u32[]{:S(2)}, u32[]{:S(2)}) collective-permute-start(bf16[8,576,128]{2,1,0:T(8,128)(2,1)S(1)} %get-tuple-element.58), channel_id=1, source_target_pairs={{0,8},{32,40},{1,9},{33,41},{2,10},{34,42},{3,11},{35,43},{4,12},{... | collective-permute-start | bytes 3538952 | tf_op jit(solution)/shard_map/ppermute | solution.py:35
  15.5 14.8 %collective-permute-start.3 = (bf16[4,576,128]{2,1,0:T(8,128)(2,1)S(1)}, bf16[4,576,128]{2,1,0:T(8,128)(2,1)S(1)}, u32[]{:S(2)}, u32[]{:S(2)}) collective-permute-start(bf16[4,576,128]{2,1,0:T(8,128)(2,1)S(1)} %pack_queries.1), channel_id=1, source_target_pairs={{0,64},{32,96},{1,65},{33,97},{2,66},{34,98},{3,67},{35,99},{4,68}... | collective-permute-start | bytes 1769480 | tf_op jit(solution)/shard_map/ppermute | solution.py:35
  17.0 13.3 %collective-permute-start.2 = (bf16[4,576,128]{2,1,0:T(8,128)(2,1)S(1)}, bf16[4,576,128]{2,1,0:T(8,128)(2,1)S(1)}, u32[]{:S(2)}, u32[]{:S(2)}) collective-permute-start(bf16[4,576,128]{2,1,0:T(8,128)(2,1)S(1)} %pack_queries.1), channel_id=1, source_target_pairs={{0,80},{32,112},{1,81},{33,113},{2,82},{34,114},{3,83},{35,115},{4... | collective-permute-start | bytes 1769480 | tf_op jit(solution)/shard_map/ppermute | solution.py:35
  30.3 15.4 %copy-start.3 = (s32[1,2]{1,0:T(1,128)S(1)}, s32[1,2]{1,0:T(1,128)}, u32[]{:S(2)}) copy-start(s32[1,2]{1,0:T(1,128)} %param.8) | copy-start | bytes 28
  31.3 40.5 %collective-permute-start.6 = (bf16[10,576,128]{2,1,0:T(8,128)(2,1)S(1)}, bf16[10,576,128]{2,1,0:T(8,128)(2,1)S(1)}, u32[]{:S(2)}, u32[]{:S(2)}) collective-permute-start(bf16[10,576,128]{2,1,0:T(8,128)(2,1)S(1)} %get-tuple-element.63), channel_id=1, source_target_pairs={{0,1},{32,33},{1,2},{33,34},{2,3},{34,35},{3,0},{35,32},{4,5},{36,... | collective-permute-start | bytes 4423688 | tf_op jit(solution)/shard_map/ppermute | solution.py:35
  32.6 39.2 %collective-permute-start.7 = (bf16[10,576,128]{2,1,0:T(8,128)(2,1)S(1)}, bf16[10,576,128]{2,1,0:T(8,128)(2,1)S(1)}, u32[]{:S(2)}, u32[]{:S(2)}) collective-permute-start(bf16[10,576,128]{2,1,0:T(8,128)(2,1)S(1)} %get-tuple-element.65), channel_id=1, source_target_pairs={{0,3},{32,35},{1,0},{33,32},{2,1},{34,33},{3,2},{35,34},{4,7},{36,... | collective-permute-start | bytes 4423688 | tf_op jit(solution)/shard_map/ppermute | solution.py:35
  34.5 37.4 %collective-permute-start.8 = (bf16[10,576,128]{2,1,0:T(8,128)(2,1)}, bf16[10,576,128]{2,1,0:T(8,128)(2,1)S(1)}, u32[]{:S(2)}, u32[]{:S(2)}) collective-permute-start(bf16[10,576,128]{2,1,0:T(8,128)(2,1)} %get-tuple-element.67), channel_id=1, source_target_pairs={{0,4},{32,36},{1,5},{33,37},{2,6},{34,38},{3,7},{35,39},{4,8},{36,... | collective-permute-start | bytes 4423688 | tf_op jit(solution)/shard_map/ppermute | solution.py:35
  42.6 30.6 %collective-permute-start.9 = (bf16[10,576,128]{2,1,0:T(8,128)(2,1)}, bf16[10,576,128]{2,1,0:T(8,128)(2,1)S(1)}, u32[]{:S(2)}, u32[]{:S(2)}) collective-permute-start(bf16[10,576,128]{2,1,0:T(8,128)(2,1)} %get-tuple-element.69), channel_id=1, source_target_pairs={{0,12},{32,44},{1,13},{33,45},{2,14},{34,46},{3,15},{35,47},{4,0},... | collective-permute-start | bytes 4423688 | tf_op jit(solution)/shard_map/ppermute | solution.py:35
  54.8 18.5 %copy-start.2 = (s32[4,64]{1,0:T(4,128)S(1)}, s32[4,64]{1,0:T(4,128)}, u32[]{:S(2)}) copy-start(s32[4,64]{1,0:T(4,128)} %lengths.7) | copy-start | bytes 3076
  75.2 13.1 %collective-permute-start.10 = (bf16[2,144,512]{2,1,0:T(8,128)(2,1)S(1)}, bf16[2,144,512]{2,1,0:T(8,128)(2,1)S(1)}, u32[]{:S(2)}, u32[]{:S(2)}) collective-permute-start(bf16[2,144,512]{2,1,0:T(8,128)(2,1)S(1)} %get-tuple-element.72), channel_id=1, source_target_pairs={{0,8},{32,40},{1,9},{33,41},{2,10},{34,42},{3,11},{35,43},{4,12},{... | collective-permute-start | bytes 884744 | tf_op jit(solution)/shard_map/ppermute | solution.py:35
  77.6 15.3 %collective-permute-start.13 = (bf16[2,144,512]{2,1,0:T(8,128)(2,1)S(1)}, bf16[2,144,512]{2,1,0:T(8,128)(2,1)S(1)}, u32[]{:S(2)}, u32[]{:S(2)}) collective-permute-start(bf16[2,144,512]{2,1,0:T(8,128)(2,1)S(1)} %get-tuple-element.85), channel_id=1, source_target_pairs={{0,2},{32,34},{1,3},{33,35},{2,0},{34,32},{3,1},{35,33},{4,6},{36,... | collective-permute-start | bytes 884744 | tf_op jit(solution)/shard_map/ppermute | solution.py:35
  82.3 10.6 %collective-permute-start.11 = (bf16[2,144,512]{2,1,0:T(8,128)(2,1)S(1)}, bf16[2,144,512]{2,1,0:T(8,128)(2,1)S(1)}, u32[]{:S(2)}, u32[]{:S(2)}) collective-permute-start(bf16[2,144,512]{2,1,0:T(8,128)(2,1)S(1)} %get-tuple-element.76), channel_id=1, source_target_pairs={{0,4},{32,36},{1,5},{33,37},{2,6},{34,38},{3,7},{35,39},{4,8},{36,... | collective-permute-start | bytes 884744 | tf_op jit(solution)/shard_map/ppermute | solution.py:35
  84.6 9.0 %collective-permute-start.14 = (bf16[2,144,512]{2,1,0:T(8,128)(2,1)S(1)}, bf16[2,144,512]{2,1,0:T(8,128)(2,1)S(1)}, u32[]{:S(2)}, u32[]{:S(2)}) collective-permute-start(bf16[2,144,512]{2,1,0:T(8,128)(2,1)S(1)} %get-tuple-element.86), channel_id=1, source_target_pairs={{0,1},{32,33},{1,2},{33,34},{2,3},{34,35},{3,0},{35,32},{4,5},{36,... | collective-permute-start | bytes 884744 | tf_op jit(solution)/shard_map/ppermute | solution.py:35
  87.2 6.8 %collective-permute-start.12 = (bf16[2,144,512]{2,1,0:T(8,128)(2,1)S(1)}, bf16[2,144,512]{2,1,0:T(8,128)(2,1)S(1)}, u32[]{:S(2)}, u32[]{:S(2)}) collective-permute-start(bf16[2,144,512]{2,1,0:T(8,128)(2,1)S(1)} %get-tuple-element.80), channel_id=1, source_target_pairs={{0,12},{32,44},{1,13},{33,45},{2,14},{34,46},{3,15},{35,47},{4,0},... | collective-permute-start | bytes 884744 | tf_op jit(solution)/shard_map/ppermute | solution.py:35
  88.4 7.3 %collective-permute-start.15 = (bf16[2,144,512]{2,1,0:T(8,128)(2,1)S(1)}, bf16[2,144,512]{2,1,0:T(8,128)(2,1)S(1)}, u32[]{:S(2)}, u32[]{:S(2)}) collective-permute-start(bf16[2,144,512]{2,1,0:T(8,128)(2,1)S(1)} %get-tuple-element.87), channel_id=1, source_target_pairs={{0,3},{32,35},{1,0},{33,32},{2,1},{34,33},{3,2},{35,34},{4,7},{36,... | collective-permute-start | bytes 884744 | tf_op jit(solution)/shard_map/ppermute | solution.py:35
  96.5 8.0 %collective-permute-start.16 = (bf16[2,144,512]{2,1,0:T(8,128)(2,1)S(1)}, bf16[2,144,512]{2,1,0:T(8,128)(2,1)S(1)}, u32[]{:S(2)}, u32[]{:S(2)}) collective-permute-start(bf16[2,144,512]{2,1,0:T(8,128)(2,1)S(1)} %get-tuple-element.89), channel_id=1, source_target_pairs={{0,64},{32,96},{1,65},{33,97},{2,66},{34,98},{3,67},{35,99},{4,68}... | collective-permute-start | bytes 884744 | tf_op jit(solution)/shard_map/ppermute | solution.py:35
  98.1 6.7 %collective-permute-start.17 = (bf16[2,144,512]{2,1,0:T(8,128)(2,1)S(1)}, bf16[2,144,512]{2,1,0:T(8,128)(2,1)S(1)}, u32[]{:S(2)}, u32[]{:S(2)}) collective-permute-start(bf16[2,144,512]{2,1,0:T(8,128)(2,1)S(1)} %get-tuple-element.90), channel_id=1, source_target_pairs={{0,80},{32,112},{1,81},{33,113},{2,82},{34,114},{3,83},{35,115},{4... | collective-permute-start | bytes 884744 | tf_op jit(solution)/shard_map/ppermute | solution.py:35

commit v4 on v3

--- a/solution.py
+++ b/solution.py
@@ -11,6 +11,7 @@
 SCALE = 192.0 ** (-0.5)
 DEAD = -1e30
 RING = 4
+LAST = RING - 1
 STAT_ROWS = 16
 AXES = ("section", "dev")
 SMALL_VMEM = 16 * 1024 * 1024
@@ -47,9 +48,9 @@
 def request_of(meta, matching, half, side, cache_step, query_step):
     x_hi = meta[4 + side]
     if half == 0:
-        z, y = (meta[2] + query_step) % RING, (meta[3] + cache_step) % RING
+        z, y = (meta[2] + query_step) & LAST, (meta[3] + cache_step) & LAST
     else:
-        z, y = (meta[2] + cache_step) % RING, (meta[3] + query_step) % RING
+        z, y = (meta[2] + cache_step) & LAST, (meta[3] + query_step) & LAST
     return matching[meta[0], (x_hi * 16 + z * 4 + y) * 2 + half]
 
 
@@ -137,9 +138,8 @@
 
 def weigh(blocks):
     scores = [
-        jnp.dot(query, keys, preferred_element_type=jnp.float32) * SCALE for query, keys, _ in blocks
+        jnp.dot(query, keys, preferred_element_type=jnp.float32) * SCALE + bias for query, keys, bias in blocks
     ]
-    scores = [jnp.where(live, score, DEAD) for score, (_, _, live) in zip(scores, blocks)]
     tops = [jnp.max(score, axis=1, keepdims=True) for score in scores]
     weights = [jnp.exp(score - top) for score, top in zip(scores, tops)]
     totals = [jnp.sum(weight, axis=1, keepdims=True) for weight in weights]
@@ -158,7 +158,8 @@
 def resident_kernel(lengths, query, keys, out):
     item = pl.program_id(0)
     live = lax.broadcasted_iota(jnp.int32, (1, keys.shape[2]), 1) < lengths[item]
-    (mixed,), _, (total,) = weigh([(query[0].T, keys[0], live)])
+    bias = jnp.where(live, 0.0, DEAD)
+    (mixed,), _, (total,) = weigh([(query[0].T, keys[0], bias)])
     out[0] = (mixed / total).astype(jnp.bfloat16)
 
 
@@ -203,27 +204,52 @@
     out[index, heads:, heads:] = jnp.zeros((STAT_ROWS, KV_RANK - heads), out.dtype)
 
 
-def slots_of(meta, half, away, span):
-    z, y = meta[2], meta[3]
-    if half == 0:
-        y = (y + RING - away) % RING
-    else:
-        z = (z + RING - away) % RING
-    return lax.broadcasted_iota(jnp.int32, (1, span), 1) + (meta[1] * 16 + z * 4 + y) * span
-
-
-def ring_results(step, meta, matching, lengths, a, b, queries):
-    span = a[0].shape[2]
+def bias_kernel(span, meta, matching, lengths, bias):
+    lane = lax.broadcasted_iota(jnp.int32, (1, span), 1)
+    for half in range(2):
+        slots = []
+        for away in range(RING):
+            z, y = meta[2], meta[3]
+            if half == 0:
+                y = (y + RING - away) & LAST
+            else:
+                z = (z + RING - away) & LAST
+            slots.append(lane + (meta[1] * 16 + z * 4 + y) * span)
+        slots = jnp.concatenate(slots, axis=1)
+        for step in range(RING):
+            for side in range(2):
+                request = request_of(meta, matching, half, side, 0, step)
+                live = slots < lengths[meta[0], request]
+                row = (half * RING + step) * 2 + side
+                bias[row : row + 1, :] = jnp.where(live, 0.0, DEAD)
+
+
+def attention_bias(span, meta, matching, lengths):
+    scalars = pl.BlockSpec(memory_space=pltpu.SMEM)
+    return pl.pallas_call(
+        functools.partial(bias_kernel, span),
+        out_shape=pltpu.VMEM((4 * RING, RING * span), jnp.float32),
+        in_specs=[scalars] * 3,
+        out_specs=pl.BlockSpec(memory_space=pltpu.VMEM),
+        compiler_params=pltpu.CompilerParams(vmem_limit_bytes=SMALL_VMEM),
+        name="attention_bias",
+    )(meta, matching, lengths)
+
+
+def attend_ring(step, bias, a, b, queries, outs):
     blocks = []
     for half, segments in enumerate((a, b)):
-        slots = jnp.concatenate([slots_of(meta, half, away, span) for away in range(RING)], axis=1)
         for side in range(2):
-            request = request_of(meta, matching, half, side, 0, step)
-            live = slots < lengths[meta[0], request]
+            row = (half * RING + step) * 2 + side
             keys = jnp.concatenate([segment[2 * step + side] for segment in segments], axis=1)
-            blocks.append((queries[half][side][...].T, keys, live))
+            blocks.append((queries[half][side][...].T, keys, bias[row : row + 1, :]))
     mixed, tops, totals = weigh(blocks)
-    return [(m / t, stat_row(top, t)) for m, top, t in zip(mixed, tops, totals)]
+    for index in range(4):
+        half, side = divmod(index, 2)
+        out = outs[half]
+        heads = mixed[index].shape[0]
+        out[side, :heads] = (mixed[index] / totals[index]).astype(out.dtype)
+        put_stat(out, side, stat_row(tops[index], totals[index]))
 
 
 def stat_row(top, total):
@@ -231,24 +257,16 @@
     return jnp.broadcast_to(top + jnp.log(total), (heads, heads)).T[:1]
 
 
-def put_results(outs, results):
-    for index, (value, row) in enumerate(results):
-        half, side = divmod(index, 2)
-        heads = value.shape[0]
-        outs[half][side, :heads] = value.astype(outs[half].dtype)
-        put_stat(outs[half], side, row)
-
-
-def partial_kernel(step, meta, matching, lengths, *refs):
+def partial_kernel(step, bias, *refs):
     a, b, plus, minus, outs = refs[:RING], refs[RING : 2 * RING], refs[8], refs[9], refs[10:]
     if step % 2:
         queries = [[ref.at[2 * RING + side] for side in range(2)] for ref in (b[RING - step], a[RING - step])]
     else:
         queries = [[plus.at[step + half], minus.at[step + half]] for half in range(2)]
-    put_results(outs, ring_results(step, meta, matching, lengths, a, b, queries))
-
-
-def partials(step, meta, matching, lengths, arrays):
+    attend_ring(step, bias, a, b, queries, outs)
+
+
+def partials(step, bias, arrays):
     width, span = arrays[0].shape[1:]
     heads = span
     work = 4 * heads * span * RING
@@ -258,12 +276,8 @@
     return pl.pallas_call(
         functools.partial(partial_kernel, step),
         out_shape=[pltpu.VMEM(shape, dtype)] * 2,
-        grid_spec=pltpu.PrefetchScalarGridSpec(
-            num_scalar_prefetch=3,
-            grid=(1,),
-            in_specs=[whole] * len(arrays),
-            out_specs=[whole] * 2,
-        ),
+        in_specs=[whole] * (1 + len(arrays)),
+        out_specs=[whole] * 2,
         compiler_params=pltpu.CompilerParams(vmem_limit_bytes=SMALL_VMEM),
         cost_estimate=pl.CostEstimate(
             flops=2 * work * (width + KV_RANK),
@@ -271,7 +285,7 @@
             transcendentals=work,
         ),
         name="partials",
-    )(meta, matching, lengths, *arrays)
+    )(bias, *arrays)
 
 
 def merge(parts):
@@ -364,9 +378,9 @@
 
     arrays = (a0, a1, a2, a3, b0, b1, b2, b3, from_plus, from_minus)
     pa, pb = [], []
-    order = meta
+    order = attention_bias(inc_cache.shape[2], later, matching, inc_lengths)
     for step in (2, 1, 3, 0):
-        for_a, for_b = partials(step, order, matching, inc_lengths, arrays)
+        for_a, for_b = partials(step, order, arrays)
         order, for_a, for_b = lax.optimization_barrier((order, for_a, for_b))
         pa.append(move(for_a, dz=step) if step else for_a)
         pb.append(move(for_b, dy=step) if step else for_b)

time: 107 us -> 105 us (0.981)
  Pallas kernels: 29.7 us -> 27.6 us
    pallas_call x4, Pallas kernels: 7.98 us -> 5.35 us  [partials(): pl.pallas_call(functools.partial(partial_kernel, step), out_shape=[pltpu....]
  transfers between devices with their start and end apart: 18 -> 18, of which waited for: 12 -> 12; matrix products, arithmetic and copies ran while one was open for 0% -> 0% of each run, Pallas kernels for 24% -> 23%
where the time goes in v4:
time: 105 us; the launch traced here: 104 us
  waiting for transfers between devices  38 us (36%)
  starting transfers between devices  36.4 us (35%)
  Pallas kernels  27.6 us (26%)
  local copies, waits for them, and re-layouts  1.78 us (2%)
    ppermute x18, waiting for transfers between devices, move(): return lax.ppermute(block, AXES, route)  38 us
    ppermute x18, starting transfers between devices, move(): return lax.ppermute(block, AXES, route)  36.4 us
    pallas_call x3, Pallas kernels, gather_requests(): pl.pallas_call(functools.partial(gather_kernel, steps), out_shape=[pltpu....  9.71 us
    pallas_call x1, Pallas kernels, resident_rows(): pl.pallas_call(resident_kernel, out_shape=jax.ShapeDtypeStruct((queries.s...  8.96 us
    pallas_call x4, Pallas kernels, partials(): pl.pallas_call(functools.partial(partial_kernel, step), out_shape=[pltpu....  5.35 us
  transfers between devices with their start and end apart: 18, of which 12 were waited for; matrix products, arithmetic and copies ran while one was open for 0% of the time, Pallas kernels for 23%

profile of v4, /device:TPU:0, one launch (start us, length us, event | category | flops | bytes accessed | tf_op | source)
XLA Modules:
  0.0 103.9 jit_solution(2234623542142914992)
XLA Ops:
  0.0 1.0 fusion
  1.0 3.4 %collective-permute-start.1 = (bf16[1,576,128]{2,1,0:T(8,128)(2,1)S(1)}, bf16[1,576,128]{2,1,0:T(8,128)(2,1)S(1)}, u32[]{:S(2)}, u32[]{:S(2)}) collective-permute-start(bf16[1,576,128]{2,1,0:T(8,128)(2,1)S(1)} %get-tuple-element.91), channel_id=1, source_target_pairs={{0,2},{32,34},{1,3},{33,35},{2,0},{34,32},{3,1},{35,33},{4,6},{36,... | collective-permute-start | bytes 442376 | tf_op jit(solution)/shard_map/ppermute | solution.py:36
  4.4 3.9 %collective-permute-start = (bf16[1,576,128]{2,1,0:T(8,128)(2,1)S(1)}, bf16[1,576,128]{2,1,0:T(8,128)(2,1)S(1)}, u32[]{:S(2)}, u32[]{:S(2)}) collective-permute-start(bf16[1,576,128]{2,1,0:T(8,128)(2,1)S(1)} %get-tuple-element.92), channel_id=1, source_target_pairs={{0,8},{32,40},{1,9},{33,41},{2,10},{34,42},{3,11},{35,43},{4,12},{... | collective-permute-start | bytes 442376 | tf_op jit(solution)/shard_map/ppermute | solution.py:36
  8.2 0.1 stack.27.meta
  8.3 0.7 copy-done.1
  9.0 2.4 %gather_requests.4 = (bf16[8,576,128]{2,1,0:T(8,128)(2,1)S(1)}, bf16[8,576,128]{2,1,0:T(8,128)(2,1)S(1)}) custom-call(s32[6]{0:T(128)S(1)} %stack.27.meta, s32[4,64]{1,0:T(4,128)S(1)} %copy-done.1, bf16[64,576,128]{2,1,0:T(8,128)(2,1)} %bitcast.21), custom_call_target="tpu_custom_call" | custom-call | bytes 4718592 | tf_op jit(solution)/shard_map/gather_requests/pallas_call | solution.py:79
  11.4 0.0 collective-permute-done.1.far_b
  11.4 0.4 collective-permute-done.far_a
  11.8 0.4 collective-permute-start.4
  12.2 3.2 %collective-permute-start.5 = (bf16[8,576,128]{2,1,0:T(8,128)(2,1)S(1)}, bf16[8,576,128]{2,1,0:T(8,128)(2,1)S(1)}, u32[]{:S(2)}, u32[]{:S(2)}) collective-permute-start(bf16[8,576,128]{2,1,0:T(8,128)(2,1)S(1)} %get-tuple-element.58), channel_id=1, source_target_pairs={{0,8},{32,40},{1,9},{33,41},{2,10},{34,42},{3,11},{35,43},{4,12},{... | collective-permute-start | bytes 3538952 | tf_op jit(solution)/shard_map/ppermute | solution.py:36
  15.5 1.6 %collective-permute-start.3 = (bf16[4,576,128]{2,1,0:T(8,128)(2,1)S(1)}, bf16[4,576,128]{2,1,0:T(8,128)(2,1)S(1)}, u32[]{:S(2)}, u32[]{:S(2)}) collective-permute-start(bf16[4,576,128]{2,1,0:T(8,128)(2,1)S(1)} %pack_queries.1), channel_id=1, source_target_pairs={{0,64},{32,96},{1,65},{33,97},{2,66},{34,98},{3,67},{35,99},{4,68}... | collective-permute-start | bytes 1769480 | tf_op jit(solution)/shard_map/ppermute | solution.py:36
  17.0 1.7 %collective-permute-start.2 = (bf16[4,576,128]{2,1,0:T(8,128)(2,1)S(1)}, bf16[4,576,128]{2,1,0:T(8,128)(2,1)S(1)}, u32[]{:S(2)}, u32[]{:S(2)}) collective-permute-start(bf16[4,576,128]{2,1,0:T(8,128)(2,1)S(1)} %pack_queries.1), channel_id=1, source_target_pairs={{0,80},{32,112},{1,81},{33,113},{2,82},{34,114},{3,83},{35,115},{4... | collective-permute-start | bytes 1769480 | tf_op jit(solution)/shard_map/ppermute | solution.py:36
  18.8 4.9 %gather_requests.3 = (bf16[10,576,128]{2,1,0:T(8,128)(2,1)S(1)}, bf16[10,576,128]{2,1,0:T(8,128)(2,1)S(1)}, bf16[10,576,128]{2,1,0:T(8,128)(2,1)}, bf16[10,576,128]{2,1,0:T(8,128)(2,1)}) custom-call(s32[6]{0:T(128)S(1)} %stack.27.meta, s32[4,64]{1,0:T(4,128)S(1)} %copy-done.1, bf16[64,576,128]{2,1,0:T(8,128)(2,1)} %bitcast.22), custom_call_target="tpu_custom_call" | custom-call | bytes 9437184 | tf_op jit(solution)/shard_map/gather_requests/pallas_call | solution.py:79
  23.7 6.6 %collective-permute-done.3.refs_5_.refs_9_ = bf16[4,576,128]{2,1,0:T(8,128)(2,1)S(1)} collective-permute-done((bf16[4,576,128]{2,1,0:T(8,128)(2,1)S(1)}, bf16[4,576,128]{2,1,0:T(8,128)(2,1)S(1)}, u32[]{:S(2)}, u32[]{:S(2)}) %collective-permute-start.3) | collective-permute-done | bytes 589856 | tf_op jit(solution)/shard_map/ppermute | solution.py:36
  30.3 0.0 collective-permute-done.2.refs_4_.refs_8_
  30.3 1.0 fill_queries.1
  31.3 1.3 %collective-permute-start.6 = (bf16[10,576,128]{2,1,0:T(8,128)(2,1)S(1)}, bf16[10,576,128]{2,1,0:T(8,128)(2,1)S(1)}, u32[]{:S(2)}, u32[]{:S(2)}) collective-permute-start(bf16[10,576,128]{2,1,0:T(8,128)(2,1)S(1)} %get-tuple-element.63), channel_id=1, source_target_pairs={{0,1},{32,33},{1,2},{33,34},{2,3},{34,35},{3,0},{35,32},{4,5},{36,... | collective-permute-start | bytes 4423688 | tf_op jit(solution)/shard_map/ppermute | solution.py:36
  32.6 1.9 %collective-permute-start.7 = (bf16[10,576,128]{2,1,0:T(8,128)(2,1)S(1)}, bf16[10,576,128]{2,1,0:T(8,128)(2,1)S(1)}, u32[]{:S(2)}, u32[]{:S(2)}) collective-permute-start(bf16[10,576,128]{2,1,0:T(8,128)(2,1)S(1)} %get-tuple-element.65), channel_id=1, source_target_pairs={{0,3},{32,35},{1,0},{33,32},{2,1},{34,33},{3,2},{35,34},{4,7},{36,... | collective-permute-start | bytes 4423688 | tf_op jit(solution)/shard_map/ppermute | solution.py:36
  34.5 1.0 collective-permute-start.8
  35.5 6.7 %collective-permute-done.4.refs_2_ = bf16[8,576,128]{2,1,0:T(8,128)(2,1)S(1)} collective-permute-done((bf16[8,576,128]{2,1,0:T(8,128)(2,1)S(1)}, bf16[8,576,128]{2,1,0:T(8,128)(2,1)S(1)}, u32[]{:S(2)}, u32[]{:S(2)}) %collective-permute-start.4) | collective-permute-done | bytes 1179680 | tf_op jit(solution)/shard_map/ppermute | solution.py:36
  42.3 0.4 collective-permute-done.5.refs_6_
  42.6 3.0 %collective-permute-start.9 = (bf16[10,576,128]{2,1,0:T(8,128)(2,1)}, bf16[10,576,128]{2,1,0:T(8,128)(2,1)S(1)}, u32[]{:S(2)}, u32[]{:S(2)}) collective-permute-start(bf16[10,576,128]{2,1,0:T(8,128)(2,1)} %get-tuple-element.69), channel_id=1, source_target_pairs={{0,12},{32,44},{1,13},{33,45},{2,14},{34,46},{3,15},{35,47},{4,0},... | collective-permute-start | bytes 4423688 | tf_op jit(solution)/shard_map/ppermute | solution.py:36
  45.7 9.0 %resident_rows.1.base = bf16[4,128,512]{2,1,0:T(8,128)(2,1)} custom-call(s32[2]{0:T(128)S(1)} %bitcast.20, bf16[4,576,128]{2,1,0:T(8,128)(2,1)S(1)} %bitcast.19, bf16[2,576,4096]{2,1,0:T(8,128)(2,1)} %bitcast.24), custom_call_target="tpu_custom_call" | custom-call | flops 2281701376 | bytes 9437184 | tf_op jit(solution)/shard_map/resident_rows/pallas_call | solution.py:169
  54.6 2.4 %gather_requests.5 = (bf16[8,576,128]{2,1,0:T(8,128)(2,1)S(1)}, bf16[8,576,128]{2,1,0:T(8,128)(2,1)S(1)}) custom-call(s32[6]{0:T(128)S(1)} %stack.27.meta, s32[4,64]{1,0:T(4,128)S(1)} %copy-done.1, bf16[64,576,128]{2,1,0:T(8,128)(2,1)} %bitcast.23), custom_call_target="tpu_custom_call" | custom-call | bytes 4718592 | tf_op jit(solution)/shard_map/gather_requests/pallas_call | solution.py:79
  57.1 0.7 attention_bias.1.bias
  57.8 14.0 %collective-permute-done.6.refs_1_ = bf16[10,576,128]{2,1,0:T(8,128)(2,1)S(1)} collective-permute-done((bf16[10,576,128]{2,1,0:T(8,128)(2,1)S(1)}, bf16[10,576,128]{2,1,0:T(8,128)(2,1)S(1)}, u32[]{:S(2)}, u32[]{:S(2)}) %collective-permute-start.6) | collective-permute-done | bytes 1474592 | tf_op jit(solution)/shard_map/ppermute | solution.py:36
  71.8 0.1 collective-permute-done.8.refs_5_
  71.9 1.4 %collective-permute-done.9.refs_7_ = bf16[10,576,128]{2,1,0:T(8,128)(2,1)S(1)} collective-permute-done((bf16[10,576,128]{2,1,0:T(8,128)(2,1)}, bf16[10,576,128]{2,1,0:T(8,128)(2,1)S(1)}, u32[]{:S(2)}, u32[]{:S(2)}) %collective-permute-start.9) | collective-permute-done | bytes 1474592 | tf_op jit(solution)/shard_map/ppermute | solution.py:36
  73.3 1.3 %partials.4 = (bf16[2,144,512]{2,1,0:T(8,128)(2,1)S(1)}, bf16[2,144,512]{2,1,0:T(8,128)(2,1)S(1)}) custom-call(f32[16,512]{1,0:T(8,128)S(1)} %attention_bias.1.bias, bf16[8,576,128]{2,1,0:T(8,128)(2,1)S(1)} %get-tuple-element.62.refs_0_, bf16[10,576,128]{2,1,0:T(8,128)(2,1)S(1)} %collective-permute-done.6.refs_1_, ...), custom_call_target="tpu_custom_call" | custom-call | flops 570425344 | bytes 2359296 | tf_op jit(solution)/shard_map/partials/pallas_call | solution.py:276
  74.6 2.3 %collective-permute-start.10 = (bf16[2,144,512]{2,1,0:T(8,128)(2,1)S(1)}, bf16[2,144,512]{2,1,0:T(8,128)(2,1)S(1)}, u32[]{:S(2)}, u32[]{:S(2)}) collective-permute-start(bf16[2,144,512]{2,1,0:T(8,128)(2,1)S(1)} %get-tuple-element.72), channel_id=1, source_target_pairs={{0,8},{32,40},{1,9},{33,41},{2,10},{34,42},{3,11},{35,43},{4,12},{... | collective-permute-start | bytes 884744 | tf_op jit(solution)/shard_map/ppermute | solution.py:36
  76.9 2.7 %collective-permute-start.13 = (bf16[2,144,512]{2,1,0:T(8,128)(2,1)S(1)}, bf16[2,144,512]{2,1,0:T(8,128)(2,1)S(1)}, u32[]{:S(2)}, u32[]{:S(2)}) collective-permute-start(bf16[2,144,512]{2,1,0:T(8,128)(2,1)S(1)} %get-tuple-element.85), channel_id=1, source_target_pairs={{0,2},{32,34},{1,3},{33,35},{2,0},{34,32},{3,1},{35,33},{4,6},{36,... | collective-permute-start | bytes 884744 | tf_op jit(solution)/shard_map/ppermute | solution.py:36
  79.6 1.3 %partials.5 = (bf16[2,144,512]{2,1,0:T(8,128)(2,1)S(1)}, bf16[2,144,512]{2,1,0:T(8,128)(2,1)S(1)}) custom-call(f32[16,512]{1,0:T(8,128)S(1)} %attention_bias.1.bias, bf16[8,576,128]{2,1,0:T(8,128)(2,1)S(1)} %get-tuple-element.62.refs_0_, bf16[10,576,128]{2,1,0:T(8,128)(2,1)S(1)} %collective-permute-done.6.refs_1_, ...), custom_call_target="tpu_custom_call" | custom-call | flops 570425344 | bytes 2359296 | tf_op jit(solution)/shard_map/partials/pallas_call | solution.py:276
  81.0 2.3 %collective-permute-start.11 = (bf16[2,144,512]{2,1,0:T(8,128)(2,1)S(1)}, bf16[2,144,512]{2,1,0:T(8,128)(2,1)S(1)}, u32[]{:S(2)}, u32[]{:S(2)}) collective-permute-start(bf16[2,144,512]{2,1,0:T(8,128)(2,1)S(1)} %get-tuple-element.76), channel_id=1, source_target_pairs={{0,4},{32,36},{1,5},{33,37},{2,6},{34,38},{3,7},{35,39},{4,8},{36,... | collective-permute-start | bytes 884744 | tf_op jit(solution)/shard_map/ppermute | solution.py:36
  83.3 0.7 collective-permute-start.14
  83.9 1.3 %partials.6 = (bf16[2,144,512]{2,1,0:T(8,128)(2,1)S(1)}, bf16[2,144,512]{2,1,0:T(8,128)(2,1)S(1)}) custom-call(f32[16,512]{1,0:T(8,128)S(1)} %attention_bias.1.bias, bf16[8,576,128]{2,1,0:T(8,128)(2,1)S(1)} %get-tuple-element.62.refs_0_, bf16[10,576,128]{2,1,0:T(8,128)(2,1)S(1)} %collective-permute-done.6.refs_1_, ...), custom_call_target="tpu_custom_call" | custom-call | flops 570425344 | bytes 2359296 | tf_op jit(solution)/shard_map/partials/pallas_call | solution.py:276
  85.3 1.1 %collective-permute-start.12 = (bf16[2,144,512]{2,1,0:T(8,128)(2,1)S(1)}, bf16[2,144,512]{2,1,0:T(8,128)(2,1)S(1)}, u32[]{:S(2)}, u32[]{:S(2)}) collective-permute-start(bf16[2,144,512]{2,1,0:T(8,128)(2,1)S(1)} %get-tuple-element.80), channel_id=1, source_target_pairs={{0,12},{32,44},{1,13},{33,45},{2,14},{34,46},{3,15},{35,47},{4,0},... | collective-permute-start | bytes 884744 | tf_op jit(solution)/shard_map/ppermute | solution.py:36
  86.4 0.0 collective-permute-done.10.refs_0_
  86.4 2.5 %collective-permute-start.15 = (bf16[2,144,512]{2,1,0:T(8,128)(2,1)S(1)}, bf16[2,144,512]{2,1,0:T(8,128)(2,1)S(1)}, u32[]{:S(2)}, u32[]{:S(2)}) collective-permute-start(bf16[2,144,512]{2,1,0:T(8,128)(2,1)S(1)} %get-tuple-element.87), channel_id=1, source_target_pairs={{0,3},{32,35},{1,0},{33,32},{2,1},{34,33},{3,2},{35,34},{4,7},{36,... | collective-permute-start | bytes 884744 | tf_op jit(solution)/shard_map/ppermute | solution.py:36
  89.0 1.3 %partials.7 = (f32[2,144,512]{2,1,0:T(8,128)S(1)}, f32[2,144,512]{2,1,0:T(8,128)S(1)}) custom-call(f32[16,512]{1,0:T(8,128)S(1)} %attention_bias.1.bias, bf16[8,576,128]{2,1,0:T(8,128)(2,1)S(1)} %get-tuple-element.62.refs_0_, bf16[10,576,128]{2,1,0:T(8,128)(2,1)S(1)} %collective-permute-done.6.refs_1_, ...), custom_call_target="tpu_custom_call" | custom-call | flops 570425344 | bytes 2359296 | tf_op jit(solution)/shard_map/partials/pallas_call | solution.py:276
  90.3 0.4 collective-permute-done.11.refs_1_
  90.7 2.2 %collective-permute-done.14.refs_5_ = bf16[2,144,512]{2,1,0:T(8,128)(2,1)S(1)} collective-permute-done((bf16[2,144,512]{2,1,0:T(8,128)(2,1)S(1)}, bf16[2,144,512]{2,1,0:T(8,128)(2,1)S(1)}, u32[]{:S(2)}, u32[]{:S(2)}) %collective-permute-start.14) | collective-permute-done | bytes 294944 | tf_op jit(solution)/shard_map/ppermute | solution.py:36
  92.9 0.8 collective-permute-done.15.refs_6_
  93.7 0.8 middle.1
  94.5 1.6 %collective-permute-start.16 = (bf16[2,144,512]{2,1,0:T(8,128)(2,1)S(1)}, bf16[2,144,512]{2,1,0:T(8,128)(2,1)S(1)}, u32[]{:S(2)}, u32[]{:S(2)}) collective-permute-start(bf16[2,144,512]{2,1,0:T(8,128)(2,1)S(1)} %get-tuple-element.89), channel_id=1, source_target_pairs={{0,64},{32,96},{1,65},{33,97},{2,66},{34,98},{3,67},{35,99},{4,68}... | collective-permute-start | bytes 884744 | tf_op jit(solution)/shard_map/ppermute | solution.py:36
  96.1 1.7 %collective-permute-start.17 = (bf16[2,144,512]{2,1,0:T(8,128)(2,1)S(1)}, bf16[2,144,512]{2,1,0:T(8,128)(2,1)S(1)}, u32[]{:S(2)}, u32[]{:S(2)}) collective-permute-start(bf16[2,144,512]{2,1,0:T(8,128)(2,1)S(1)} %get-tuple-element.90), channel_id=1, source_target_pairs={{0,80},{32,112},{1,81},{33,113},{2,82},{34,114},{3,83},{35,115},{4... | collective-permute-start | bytes 884744 | tf_op jit(solution)/shard_map/ppermute | solution.py:36
  97.8 4.7 %collective-permute-done.16.plus = bf16[2,144,512]{2,1,0:T(8,128)(2,1)S(1)} collective-permute-done((bf16[2,144,512]{2,1,0:T(8,128)(2,1)S(1)}, bf16[2,144,512]{2,1,0:T(8,128)(2,1)S(1)}, u32[]{:S(2)}, u32[]{:S(2)}) %collective-permute-start.16) | collective-permute-done | bytes 294944 | tf_op jit(solution)/shard_map/ppermute | solution.py:36
  102.5 0.3 collective-permute-done.17.minus
  102.8 1.0 last.1
  (11 shorter events, 0.1 us)
Async XLA Ops:
  1.0 10.4 %collective-permute-start.1 = (bf16[1,576,128]{2,1,0:T(8,128)(2,1)S(1)}, bf16[1,576,128]{2,1,0:T(8,128)(2,1)S(1)}, u32[]{:S(2)}, u32[]{:S(2)}) collective-permute-start(bf16[1,576,128]{2,1,0:T(8,128)(2,1)S(1)} %get-tuple-element.91), channel_id=1, source_target_pairs={{0,2},{32,34},{1,3},{33,35},{2,0},{34,32},{3,1},{35,33},{4,6},{36,... | collective-permute-start | bytes 442376 | tf_op jit(solution)/shard_map/ppermute | solution.py:36
  4.4 7.4 %collective-permute-start = (bf16[1,576,128]{2,1,0:T(8,128)(2,1)S(1)}, bf16[1,576,128]{2,1,0:T(8,128)(2,1)S(1)}, u32[]{:S(2)}, u32[]{:S(2)}) collective-permute-start(bf16[1,576,128]{2,1,0:T(8,128)(2,1)S(1)} %get-tuple-element.92), channel_id=1, source_target_pairs={{0,8},{32,40},{1,9},{33,41},{2,10},{34,42},{3,11},{35,43},{4,12},{... | collective-permute-start | bytes 442376 | tf_op jit(solution)/shard_map/ppermute | solution.py:36
  8.3 0.7 copy-start.1
  9.0 6.4 %copy-start = (bf16[1,4,128,576]{2,3,1,0:T(8,128)(2,1)S(1)}, bf16[1,4,128,576]{2,3,1,0:T(8,128)(2,1)}, u32[]{:S(2)}) copy-start(bf16[1,4,128,576]{2,3,1,0:T(8,128)(2,1)} %param.6) | copy-start | bytes 1769476
  11.8 30.5 %collective-permute-start.4 = (bf16[8,576,128]{2,1,0:T(8,128)(2,1)S(1)}, bf16[8,576,128]{2,1,0:T(8,128)(2,1)S(1)}, u32[]{:S(2)}, u32[]{:S(2)}) collective-permute-start(bf16[8,576,128]{2,1,0:T(8,128)(2,1)S(1)} %get-tuple-element.57), channel_id=1, source_target_pairs={{0,2},{32,34},{1,3},{33,35},{2,0},{34,32},{3,1},{35,33},{4,6},{36,... | collective-permute-start | bytes 3538952 | tf_op jit(solution)/shard_map/ppermute | solution.py:36
  12.2 30.5 %collective-permute-start.5 = (bf16[8,576,128]{2,1,0:T(8,128)(2,1)S(1)}, bf16[8,576,128]{2,1,0:T(8,128)(2,1)S(1)}, u32[]{:S(2)}, u32[]{:S(2)}) collective-permute-start(bf16[8,576,128]{2,1,0:T(8,128)(2,1)S(1)} %get-tuple-element.58), channel_id=1, source_target_pairs={{0,8},{32,40},{1,9},{33,41},{2,10},{34,42},{3,11},{35,43},{4,12},{... | collective-permute-start | bytes 3538952 | tf_op jit(solution)/shard_map/ppermute | solution.py:36
  15.5 14.8 %collective-permute-start.3 = (bf16[4,576,128]{2,1,0:T(8,128)(2,1)S(1)}, bf16[4,576,128]{2,1,0:T(8,128)(2,1)S(1)}, u32[]{:S(2)}, u32[]{:S(2)}) collective-permute-start(bf16[4,576,128]{2,1,0:T(8,128)(2,1)S(1)} %pack_queries.1), channel_id=1, source_target_pairs={{0,64},{32,96},{1,65},{33,97},{2,66},{34,98},{3,67},{35,99},{4,68}... | collective-permute-start | bytes 1769480 | tf_op jit(solution)/shard_map/ppermute | solution.py:36
  17.0 13.3 %collective-permute-start.2 = (bf16[4,576,128]{2,1,0:T(8,128)(2,1)S(1)}, bf16[4,576,128]{2,1,0:T(8,128)(2,1)S(1)}, u32[]{:S(2)}, u32[]{:S(2)}) collective-permute-start(bf16[4,576,128]{2,1,0:T(8,128)(2,1)S(1)} %pack_queries.1), channel_id=1, source_target_pairs={{0,80},{32,112},{1,81},{33,113},{2,82},{34,114},{3,83},{35,115},{4... | collective-permute-start | bytes 1769480 | tf_op jit(solution)/shard_map/ppermute | solution.py:36
  30.3 15.4 %copy-start.3 = (s32[1,2]{1,0:T(1,128)S(1)}, s32[1,2]{1,0:T(1,128)}, u32[]{:S(2)}) copy-start(s32[1,2]{1,0:T(1,128)} %param.8) | copy-start | bytes 28
  31.3 40.5 %collective-permute-start.6 = (bf16[10,576,128]{2,1,0:T(8,128)(2,1)S(1)}, bf16[10,576,128]{2,1,0:T(8,128)(2,1)S(1)}, u32[]{:S(2)}, u32[]{:S(2)}) collective-permute-start(bf16[10,576,128]{2,1,0:T(8,128)(2,1)S(1)} %get-tuple-element.63), channel_id=1, source_target_pairs={{0,1},{32,33},{1,2},{33,34},{2,3},{34,35},{3,0},{35,32},{4,5},{36,... | collective-permute-start | bytes 4423688 | tf_op jit(solution)/shard_map/ppermute | solution.py:36
  32.6 39.2 %collective-permute-start.7 = (bf16[10,576,128]{2,1,0:T(8,128)(2,1)S(1)}, bf16[10,576,128]{2,1,0:T(8,128)(2,1)S(1)}, u32[]{:S(2)}, u32[]{:S(2)}) collective-permute-start(bf16[10,576,128]{2,1,0:T(8,128)(2,1)S(1)} %get-tuple-element.65), channel_id=1, source_target_pairs={{0,3},{32,35},{1,0},{33,32},{2,1},{34,33},{3,2},{35,34},{4,7},{36,... | collective-permute-start | bytes 4423688 | tf_op jit(solution)/shard_map/ppermute | solution.py:36
  34.5 37.4 %collective-permute-start.8 = (bf16[10,576,128]{2,1,0:T(8,128)(2,1)}, bf16[10,576,128]{2,1,0:T(8,128)(2,1)S(1)}, u32[]{:S(2)}, u32[]{:S(2)}) collective-permute-start(bf16[10,576,128]{2,1,0:T(8,128)(2,1)} %get-tuple-element.67), channel_id=1, source_target_pairs={{0,4},{32,36},{1,5},{33,37},{2,6},{34,38},{3,7},{35,39},{4,8},{36,... | collective-permute-start | bytes 4423688 | tf_op jit(solution)/shard_map/ppermute | solution.py:36
  42.6 30.6 %collective-permute-start.9 = (bf16[10,576,128]{2,1,0:T(8,128)(2,1)}, bf16[10,576,128]{2,1,0:T(8,128)(2,1)S(1)}, u32[]{:S(2)}, u32[]{:S(2)}) collective-permute-start(bf16[10,576,128]{2,1,0:T(8,128)(2,1)} %get-tuple-element.69), channel_id=1, source_target_pairs={{0,12},{32,44},{1,13},{33,45},{2,14},{34,46},{3,15},{35,47},{4,0},... | collective-permute-start | bytes 4423688 | tf_op jit(solution)/shard_map/ppermute | solution.py:36
  54.6 2.4 %copy-start.2 = (s32[4,64]{1,0:T(4,128)S(1)}, s32[4,64]{1,0:T(4,128)}, u32[]{:S(2)}) copy-start(s32[4,64]{1,0:T(4,128)} %lengths.1) | copy-start | bytes 3076
  74.6 11.8 %collective-permute-start.10 = (bf16[2,144,512]{2,1,0:T(8,128)(2,1)S(1)}, bf16[2,144,512]{2,1,0:T(8,128)(2,1)S(1)}, u32[]{:S(2)}, u32[]{:S(2)}) collective-permute-start(bf16[2,144,512]{2,1,0:T(8,128)(2,1)S(1)} %get-tuple-element.72), channel_id=1, source_target_pairs={{0,8},{32,40},{1,9},{33,41},{2,10},{34,42},{3,11},{35,43},{4,12},{... | collective-permute-start | bytes 884744 | tf_op jit(solution)/shard_map/ppermute | solution.py:36
  76.9 13.4 %collective-permute-start.13 = (bf16[2,144,512]{2,1,0:T(8,128)(2,1)S(1)}, bf16[2,144,512]{2,1,0:T(8,128)(2,1)S(1)}, u32[]{:S(2)}, u32[]{:S(2)}) collective-permute-start(bf16[2,144,512]{2,1,0:T(8,128)(2,1)S(1)} %get-tuple-element.85), channel_id=1, source_target_pairs={{0,2},{32,34},{1,3},{33,35},{2,0},{34,32},{3,1},{35,33},{4,6},{36,... | collective-permute-start | bytes 884744 | tf_op jit(solution)/shard_map/ppermute | solution.py:36
  81.0 9.7 %collective-permute-start.11 = (bf16[2,144,512]{2,1,0:T(8,128)(2,1)S(1)}, bf16[2,144,512]{2,1,0:T(8,128)(2,1)S(1)}, u32[]{:S(2)}, u32[]{:S(2)}) collective-permute-start(bf16[2,144,512]{2,1,0:T(8,128)(2,1)S(1)} %get-tuple-element.76), channel_id=1, source_target_pairs={{0,4},{32,36},{1,5},{33,37},{2,6},{34,38},{3,7},{35,39},{4,8},{36,... | collective-permute-start | bytes 884744 | tf_op jit(solution)/shard_map/ppermute | solution.py:36
  83.3 9.7 %collective-permute-start.14 = (bf16[2,144,512]{2,1,0:T(8,128)(2,1)S(1)}, bf16[2,144,512]{2,1,0:T(8,128)(2,1)S(1)}, u32[]{:S(2)}, u32[]{:S(2)}) collective-permute-start(bf16[2,144,512]{2,1,0:T(8,128)(2,1)S(1)} %get-tuple-element.86), channel_id=1, source_target_pairs={{0,1},{32,33},{1,2},{33,34},{2,3},{34,35},{3,0},{35,32},{4,5},{36,... | collective-permute-start | bytes 884744 | tf_op jit(solution)/shard_map/ppermute | solution.py:36
  85.3 7.6 %collective-permute-start.12 = (bf16[2,144,512]{2,1,0:T(8,128)(2,1)S(1)}, bf16[2,144,512]{2,1,0:T(8,128)(2,1)S(1)}, u32[]{:S(2)}, u32[]{:S(2)}) collective-permute-start(bf16[2,144,512]{2,1,0:T(8,128)(2,1)S(1)} %get-tuple-element.80), channel_id=1, source_target_pairs={{0,12},{32,44},{1,13},{33,45},{2,14},{34,46},{3,15},{35,47},{4,0},... | collective-permute-start | bytes 884744 | tf_op jit(solution)/shard_map/ppermute | solution.py:36
  86.4 7.3 %collective-permute-start.15 = (bf16[2,144,512]{2,1,0:T(8,128)(2,1)S(1)}, bf16[2,144,512]{2,1,0:T(8,128)(2,1)S(1)}, u32[]{:S(2)}, u32[]{:S(2)}) collective-permute-start(bf16[2,144,512]{2,1,0:T(8,128)(2,1)S(1)} %get-tuple-element.87), channel_id=1, source_target_pairs={{0,3},{32,35},{1,0},{33,32},{2,1},{34,33},{3,2},{35,34},{4,7},{36,... | collective-permute-start | bytes 884744 | tf_op jit(solution)/shard_map/ppermute | solution.py:36
  94.5 8.0 %collective-permute-start.16 = (bf16[2,144,512]{2,1,0:T(8,128)(2,1)S(1)}, bf16[2,144,512]{2,1,0:T(8,128)(2,1)S(1)}, u32[]{:S(2)}, u32[]{:S(2)}) collective-permute-start(bf16[2,144,512]{2,1,0:T(8,128)(2,1)S(1)} %get-tuple-element.89), channel_id=1, source_target_pairs={{0,64},{32,96},{1,65},{33,97},{2,66},{34,98},{3,67},{35,99},{4,68}... | collective-permute-start | bytes 884744 | tf_op jit(solution)/shard_map/ppermute | solution.py:36
  96.1 6.7 %collective-permute-start.17 = (bf16[2,144,512]{2,1,0:T(8,128)(2,1)S(1)}, bf16[2,144,512]{2,1,0:T(8,128)(2,1)S(1)}, u32[]{:S(2)}, u32[]{:S(2)}) collective-permute-start(bf16[2,144,512]{2,1,0:T(8,128)(2,1)S(1)} %get-tuple-element.90), channel_id=1, source_target_pairs={{0,80},{32,112},{1,81},{33,113},{2,82},{34,114},{3,83},{35,115},{4... | collective-permute-start | bytes 884744 | tf_op jit(solution)/shard_map/ppermute | solution.py:36

commit v5 on v4

--- a/solution.py
+++ b/solution.py
@@ -195,13 +195,16 @@
     return high, middle, rest - middle
 
 
-def put_stat(out, index, row):
-    heads = row.shape[1]
-    high, middle, low = split_stat(row)
-    rows = lax.broadcasted_iota(jnp.int32, (STAT_ROWS, heads), 0)
-    block = jnp.where(rows == 0, high, jnp.where(rows == 1, middle, jnp.where(rows == 2, low, 0.0)))
-    out[index, heads:, :heads] = block.astype(out.dtype)
-    out[index, heads:, heads:] = jnp.zeros((STAT_ROWS, KV_RANK - heads), out.dtype)
+def put_pair(out, values, rows):
+    heads = rows[0].shape[1]
+    line = lax.broadcasted_iota(jnp.int32, (STAT_ROWS, heads), 0)
+    block = jnp.zeros((STAT_ROWS, heads), jnp.float32)
+    for index in range(2):
+        out[index * heads : (index + 1) * heads] = values[index].astype(out.dtype)
+        for place, part in enumerate(split_stat(rows[index])):
+            block = jnp.where(line == 3 * index + place, part, block)
+    out[2 * heads :, :heads] = block.astype(out.dtype)
+    out[2 * heads :, heads:] = jnp.zeros((STAT_ROWS, KV_RANK - heads), out.dtype)
 
 
 def bias_kernel(span, meta, matching, lengths, bias):
@@ -244,12 +247,13 @@
             keys = jnp.concatenate([segment[2 * step + side] for segment in segments], axis=1)
             blocks.append((queries[half][side][...].T, keys, bias[row : row + 1, :]))
     mixed, tops, totals = weigh(blocks)
-    for index in range(4):
-        half, side = divmod(index, 2)
-        out = outs[half]
-        heads = mixed[index].shape[0]
-        out[side, :heads] = (mixed[index] / totals[index]).astype(out.dtype)
-        put_stat(out, side, stat_row(tops[index], totals[index]))
+    for half in range(2):
+        pair = range(2 * half, 2 * half + 2)
+        put_pair(
+            outs[half],
+            [mixed[index] / totals[index] for index in pair],
+            [stat_row(tops[index], totals[index]) for index in pair],
+        )
 
 
 def stat_row(top, total):
@@ -271,7 +275,7 @@
     heads = span
     work = 4 * heads * span * RING
     whole = pl.BlockSpec(memory_space=pltpu.VMEM)
-    shape = (2, heads + STAT_ROWS, KV_RANK)
+    shape = (2 * heads + STAT_ROWS, KV_RANK)
     dtype = jnp.bfloat16 if step else jnp.float32
     return pl.pallas_call(
         functools.partial(partial_kernel, step),
@@ -301,19 +305,19 @@
     return mixed, top + jnp.log(total)
 
 
-def received(block):
-    heads = block.shape[0] - STAT_ROWS
-    rows = block[heads:, :heads].astype(jnp.float32)
-    return block[:heads].astype(jnp.float32), rows[0:1] + rows[1:2] + rows[2:3]
+def received(pair, index):
+    heads = (pair.shape[0] - STAT_ROWS) // 2
+    rows = pair[2 * heads :, :heads].astype(jnp.float32)
+    values = pair[index * heads : (index + 1) * heads].astype(jnp.float32)
+    first = 3 * index
+    return values, rows[first : first + 1] + rows[first + 1 : first + 2] + rows[first + 2 : first + 3]
 
 
 def middle_kernel(*refs):
     ins, outs = refs[: 2 * RING], refs[2 * RING :]
-    for half in range(2):
-        for side in range(2):
-            mixed, row = merge([received(ref[side]) for ref in ins[half * RING : (half + 1) * RING]])
-            outs[side][half, : mixed.shape[0]] = mixed.astype(jnp.bfloat16)
-            put_stat(outs[side], half, row)
+    for side in range(2):
+        merged = [merge([received(ref, side) for ref in ins[half * RING : (half + 1) * RING]]) for half in range(2)]
+        put_pair(outs[side], [mixed for mixed, _ in merged], [row for _, row in merged])
 
 
 def middle(parts):
@@ -331,13 +335,13 @@
 def last_kernel(base, plus, minus, out):
     del base
     for half in range(2):
-        mixed, _ = merge([received(plus[half]), received(minus[half])])
+        mixed, _ = merge([received(plus, half), received(minus, half)])
         out[half] = mixed.astype(jnp.bfloat16)
 
 
 def last(base, plus, minus):
     count, heads, rank = base.shape
-    whole = pl.BlockSpec(plus.shape, lambda i: (0, 0, 0))
+    whole = pl.BlockSpec(memory_space=pltpu.VMEM)
     return pl.pallas_call(
         last_kernel,
         out_shape=jax.ShapeDtypeStruct(base.shape, base.dtype),
@@ -379,7 +383,7 @@
     arrays = (a0, a1, a2, a3, b0, b1, b2, b3, from_plus, from_minus)
     pa, pb = [], []
     order = attention_bias(inc_cache.shape[2], later, matching, inc_lengths)
-    for step in (2, 1, 3, 0):
+    for step in (2, 3, 1, 0):
         for_a, for_b = partials(step, order, arrays)
         order, for_a, for_b = lax.optimization_barrier((order, for_a, for_b))
         pa.append(move(for_a, dz=step) if step else for_a)

time: 105 us -> 104 us (level)
  starting transfers between devices: 36.4 us -> 34.2 us
  waiting for transfers between devices: 38 us -> 39.9 us
    ppermute x18, starting transfers between devices: 36.4 us -> 34.2 us  [move(): return lax.ppermute(block, AXES, route)]
    ppermute x18, waiting for transfers between devices: 38 us -> 39.9 us  [move(): return lax.ppermute(block, AXES, route)]
  transfers between devices with their start and end apart: 18 -> 18, of which waited for: 12 -> 13; matrix products, arithmetic and copies ran while one was open for 0% -> 0% of each run, Pallas kernels for 23% -> 24%
where the time goes in v5:
time: 104 us
  waiting for transfers between devices  39.9 us (38%)
  starting transfers between devices  34.2 us (33%)
  Pallas kernels  27.6 us (27%)
  local copies, waits for them, and re-layouts  1.78 us (2%)
    ppermute x18, waiting for transfers between devices, move(): return lax.ppermute(block, AXES, route)  39.9 us
    ppermute x18, starting transfers between devices, move(): return lax.ppermute(block, AXES, route)  34.2 us
    pallas_call x3, Pallas kernels, gather_requests(): pl.pallas_call(functools.partial(gather_kernel, steps), out_shape=[pltpu....  9.71 us
    pallas_call x1, Pallas kernels, resident_rows(): pl.pallas_call(resident_kernel, out_shape=jax.ShapeDtypeStruct((queries.s...  8.96 us
    pallas_call x4, Pallas kernels, partials(): pl.pallas_call(functools.partial(partial_kernel, step), out_shape=[pltpu....  5.38 us
  transfers between devices with their start and end apart: 18, of which 13 were waited for; matrix products, arithmetic and copies ran while one was open for 0% of the time, Pallas kernels for 24%

profile of v5, /device:TPU:0, one launch (start us, length us, event | category | flops | bytes accessed | tf_op | source)
XLA Modules:
  0.0 103.7 jit_solution(4712489425276532771)
XLA Ops:
  0.0 1.0 fusion
  1.0 3.4 %collective-permute-start.1 = (bf16[1,576,128]{2,1,0:T(8,128)(2,1)S(1)}, bf16[1,576,128]{2,1,0:T(8,128)(2,1)S(1)}, u32[]{:S(2)}, u32[]{:S(2)}) collective-permute-start(bf16[1,576,128]{2,1,0:T(8,128)(2,1)S(1)} %get-tuple-element.91), channel_id=1, source_target_pairs={{0,2},{32,34},{1,3},{33,35},{2,0},{34,32},{3,1},{35,33},{4,6},{36,... | collective-permute-start | bytes 442376 | tf_op jit(solution)/shard_map/ppermute | solution.py:36
  4.4 3.9 %collective-permute-start = (bf16[1,576,128]{2,1,0:T(8,128)(2,1)S(1)}, bf16[1,576,128]{2,1,0:T(8,128)(2,1)S(1)}, u32[]{:S(2)}, u32[]{:S(2)}) collective-permute-start(bf16[1,576,128]{2,1,0:T(8,128)(2,1)S(1)} %get-tuple-element.92), channel_id=1, source_target_pairs={{0,8},{32,40},{1,9},{33,41},{2,10},{34,42},{3,11},{35,43},{4,12},{... | collective-permute-start | bytes 442376 | tf_op jit(solution)/shard_map/ppermute | solution.py:36
  8.2 0.1 stack.27.meta
  8.3 0.7 copy-done.1
  9.0 2.4 %gather_requests.4 = (bf16[8,576,128]{2,1,0:T(8,128)(2,1)S(1)}, bf16[8,576,128]{2,1,0:T(8,128)(2,1)S(1)}) custom-call(s32[6]{0:T(128)S(1)} %stack.27.meta, s32[4,64]{1,0:T(4,128)S(1)} %copy-done.1, bf16[64,576,128]{2,1,0:T(8,128)(2,1)} %bitcast.21), custom_call_target="tpu_custom_call" | custom-call | bytes 4718592 | tf_op jit(solution)/shard_map/gather_requests/pallas_call | solution.py:79
  11.4 0.4 collective-permute-done.far_a
  11.8 0.4 collective-permute-start.4
  12.2 3.2 %collective-permute-start.5 = (bf16[8,576,128]{2,1,0:T(8,128)(2,1)S(1)}, bf16[8,576,128]{2,1,0:T(8,128)(2,1)S(1)}, u32[]{:S(2)}, u32[]{:S(2)}) collective-permute-start(bf16[8,576,128]{2,1,0:T(8,128)(2,1)S(1)} %get-tuple-element.58), channel_id=1, source_target_pairs={{0,8},{32,40},{1,9},{33,41},{2,10},{34,42},{3,11},{35,43},{4,12},{... | collective-permute-start | bytes 3538952 | tf_op jit(solution)/shard_map/ppermute | solution.py:36
  15.5 1.6 %collective-permute-start.3 = (bf16[4,576,128]{2,1,0:T(8,128)(2,1)S(1)}, bf16[4,576,128]{2,1,0:T(8,128)(2,1)S(1)}, u32[]{:S(2)}, u32[]{:S(2)}) collective-permute-start(bf16[4,576,128]{2,1,0:T(8,128)(2,1)S(1)} %pack_queries.1), channel_id=1, source_target_pairs={{0,64},{32,96},{1,65},{33,97},{2,66},{34,98},{3,67},{35,99},{4,68}... | collective-permute-start | bytes 1769480 | tf_op jit(solution)/shard_map/ppermute | solution.py:36
  17.0 1.7 %collective-permute-start.2 = (bf16[4,576,128]{2,1,0:T(8,128)(2,1)S(1)}, bf16[4,576,128]{2,1,0:T(8,128)(2,1)S(1)}, u32[]{:S(2)}, u32[]{:S(2)}) collective-permute-start(bf16[4,576,128]{2,1,0:T(8,128)(2,1)S(1)} %pack_queries.1), channel_id=1, source_target_pairs={{0,80},{32,112},{1,81},{33,113},{2,82},{34,114},{3,83},{35,115},{4... | collective-permute-start | bytes 1769480 | tf_op jit(solution)/shard_map/ppermute | solution.py:36
  18.8 4.9 %gather_requests.3 = (bf16[10,576,128]{2,1,0:T(8,128)(2,1)S(1)}, bf16[10,576,128]{2,1,0:T(8,128)(2,1)S(1)}, bf16[10,576,128]{2,1,0:T(8,128)(2,1)}, bf16[10,576,128]{2,1,0:T(8,128)(2,1)}) custom-call(s32[6]{0:T(128)S(1)} %stack.27.meta, s32[4,64]{1,0:T(4,128)S(1)} %copy-done.1, bf16[64,576,128]{2,1,0:T(8,128)(2,1)} %bitcast.22), custom_call_target="tpu_custom_call" | custom-call | bytes 9437184 | tf_op jit(solution)/shard_map/gather_requests/pallas_call | solution.py:79
  23.7 6.6 %collective-permute-done.3.refs_5_.refs_9_ = bf16[4,576,128]{2,1,0:T(8,128)(2,1)S(1)} collective-permute-done((bf16[4,576,128]{2,1,0:T(8,128)(2,1)S(1)}, bf16[4,576,128]{2,1,0:T(8,128)(2,1)S(1)}, u32[]{:S(2)}, u32[]{:S(2)}) %collective-permute-start.3) | collective-permute-done | bytes 589856 | tf_op jit(solution)/shard_map/ppermute | solution.py:36
  30.3 0.0 collective-permute-done.2.refs_4_.refs_8_
  30.3 1.0 fill_queries.1
  31.3 1.3 %collective-permute-start.6 = (bf16[10,576,128]{2,1,0:T(8,128)(2,1)S(1)}, bf16[10,576,128]{2,1,0:T(8,128)(2,1)S(1)}, u32[]{:S(2)}, u32[]{:S(2)}) collective-permute-start(bf16[10,576,128]{2,1,0:T(8,128)(2,1)S(1)} %get-tuple-element.63), channel_id=1, source_target_pairs={{0,1},{32,33},{1,2},{33,34},{2,3},{34,35},{3,0},{35,32},{4,5},{36,... | collective-permute-start | bytes 4423688 | tf_op jit(solution)/shard_map/ppermute | solution.py:36
  32.6 1.9 %collective-permute-start.7 = (bf16[10,576,128]{2,1,0:T(8,128)(2,1)S(1)}, bf16[10,576,128]{2,1,0:T(8,128)(2,1)S(1)}, u32[]{:S(2)}, u32[]{:S(2)}) collective-permute-start(bf16[10,576,128]{2,1,0:T(8,128)(2,1)S(1)} %get-tuple-element.65), channel_id=1, source_target_pairs={{0,3},{32,35},{1,0},{33,32},{2,1},{34,33},{3,2},{35,34},{4,7},{36,... | collective-permute-start | bytes 4423688 | tf_op jit(solution)/shard_map/ppermute | solution.py:36
  34.5 1.0 collective-permute-start.8
  35.5 6.7 %collective-permute-done.4.refs_2_ = bf16[8,576,128]{2,1,0:T(8,128)(2,1)S(1)} collective-permute-done((bf16[8,576,128]{2,1,0:T(8,128)(2,1)S(1)}, bf16[8,576,128]{2,1,0:T(8,128)(2,1)S(1)}, u32[]{:S(2)}, u32[]{:S(2)}) %collective-permute-start.4) | collective-permute-done | bytes 1179680 | tf_op jit(solution)/shard_map/ppermute | solution.py:36
  42.3 0.4 collective-permute-done.5.refs_6_
  42.6 3.0 %collective-permute-start.9 = (bf16[10,576,128]{2,1,0:T(8,128)(2,1)}, bf16[10,576,128]{2,1,0:T(8,128)(2,1)S(1)}, u32[]{:S(2)}, u32[]{:S(2)}) collective-permute-start(bf16[10,576,128]{2,1,0:T(8,128)(2,1)} %get-tuple-element.69), channel_id=1, source_target_pairs={{0,12},{32,44},{1,13},{33,45},{2,14},{34,46},{3,15},{35,47},{4,0},... | collective-permute-start | bytes 4423688 | tf_op jit(solution)/shard_map/ppermute | solution.py:36
  45.7 9.0 %resident_rows.1.base = bf16[4,128,512]{2,1,0:T(8,128)(2,1)} custom-call(s32[2]{0:T(128)S(1)} %bitcast.20, bf16[4,576,128]{2,1,0:T(8,128)(2,1)S(1)} %bitcast.19, bf16[2,576,4096]{2,1,0:T(8,128)(2,1)} %bitcast.24), custom_call_target="tpu_custom_call" | custom-call | flops 2281701376 | bytes 9437184 | tf_op jit(solution)/shard_map/resident_rows/pallas_call | solution.py:169
  54.6 2.4 %gather_requests.5 = (bf16[8,576,128]{2,1,0:T(8,128)(2,1)S(1)}, bf16[8,576,128]{2,1,0:T(8,128)(2,1)S(1)}) custom-call(s32[6]{0:T(128)S(1)} %stack.27.meta, s32[4,64]{1,0:T(4,128)S(1)} %copy-done.1, bf16[64,576,128]{2,1,0:T(8,128)(2,1)} %bitcast.23), custom_call_target="tpu_custom_call" | custom-call | bytes 4718592 | tf_op jit(solution)/shard_map/gather_requests/pallas_call | solution.py:79
  57.1 0.7 attention_bias.1.bias
  57.8 14.0 %collective-permute-done.6.refs_1_ = bf16[10,576,128]{2,1,0:T(8,128)(2,1)S(1)} collective-permute-done((bf16[10,576,128]{2,1,0:T(8,128)(2,1)S(1)}, bf16[10,576,128]{2,1,0:T(8,128)(2,1)S(1)}, u32[]{:S(2)}, u32[]{:S(2)}) %collective-permute-start.6) | collective-permute-done | bytes 1474592 | tf_op jit(solution)/shard_map/ppermute | solution.py:36
  71.8 0.0 collective-permute-done.7.refs_3_
  71.8 0.1 collective-permute-done.8.refs_5_
  71.9 1.4 %collective-permute-done.9.refs_7_ = bf16[10,576,128]{2,1,0:T(8,128)(2,1)S(1)} collective-permute-done((bf16[10,576,128]{2,1,0:T(8,128)(2,1)}, bf16[10,576,128]{2,1,0:T(8,128)(2,1)S(1)}, u32[]{:S(2)}, u32[]{:S(2)}) %collective-permute-start.9) | collective-permute-done | bytes 1474592 | tf_op jit(solution)/shard_map/ppermute | solution.py:36
  73.3 1.3 %partials.4 = (bf16[272,512]{1,0:T(8,128)(2,1)S(1)}, bf16[272,512]{1,0:T(8,128)(2,1)S(1)}) custom-call(f32[16,512]{1,0:T(8,128)S(1)} %attention_bias.1.bias, bf16[8,576,128]{2,1,0:T(8,128)(2,1)S(1)} %get-tuple-element.62.refs_0_, bf16[10,576,128]{2,1,0:T(8,128)(2,1)S(1)} %collective-permute-done.6.refs_1_, ...), custom_call_target="tpu_custom_call" | custom-call | flops 570425344 | bytes 2359296 | tf_op jit(solution)/shard_map/partials/pallas_call | solution.py:280
  74.6 2.3 %collective-permute-start.10 = (bf16[272,512]{1,0:T(8,128)(2,1)S(1)}, bf16[272,512]{1,0:T(8,128)(2,1)S(1)}, u32[]{:S(2)}, u32[]{:S(2)}) collective-permute-start(bf16[272,512]{1,0:T(8,128)(2,1)S(1)} %get-tuple-element.72), channel_id=1, source_target_pairs={{0,8},{32,40},{1,9},{33,41},{2,10},{34,42},{3,11},{35,43},{4,12},{... | collective-permute-start | bytes 835592 | tf_op jit(solution)/shard_map/ppermute | solution.py:36
  76.9 2.7 %collective-permute-start.13 = (bf16[272,512]{1,0:T(8,128)(2,1)S(1)}, bf16[272,512]{1,0:T(8,128)(2,1)S(1)}, u32[]{:S(2)}, u32[]{:S(2)}) collective-permute-start(bf16[272,512]{1,0:T(8,128)(2,1)S(1)} %get-tuple-element.85), channel_id=1, source_target_pairs={{0,2},{32,34},{1,3},{33,35},{2,0},{34,32},{3,1},{35,33},{4,6},{36,... | collective-permute-start | bytes 835592 | tf_op jit(solution)/shard_map/ppermute | solution.py:36
  79.7 1.3 %partials.5 = (bf16[272,512]{1,0:T(8,128)(2,1)S(1)}, bf16[272,512]{1,0:T(8,128)(2,1)S(1)}) custom-call(f32[16,512]{1,0:T(8,128)S(1)} %attention_bias.1.bias, bf16[8,576,128]{2,1,0:T(8,128)(2,1)S(1)} %get-tuple-element.62.refs_0_, bf16[10,576,128]{2,1,0:T(8,128)(2,1)S(1)} %collective-permute-done.6.refs_1_, ...), custom_call_target="tpu_custom_call" | custom-call | flops 570425344 | bytes 2359296 | tf_op jit(solution)/shard_map/partials/pallas_call | solution.py:280
  81.0 1.5 %collective-permute-start.11 = (bf16[272,512]{1,0:T(8,128)(2,1)S(1)}, bf16[272,512]{1,0:T(8,128)(2,1)S(1)}, u32[]{:S(2)}, u32[]{:S(2)}) collective-permute-start(bf16[272,512]{1,0:T(8,128)(2,1)S(1)} %get-tuple-element.76), channel_id=1, source_target_pairs={{0,12},{32,44},{1,13},{33,45},{2,14},{34,46},{3,15},{35,47},{4,0},... | collective-permute-start | bytes 835592 | tf_op jit(solution)/shard_map/ppermute | solution.py:36
  82.5 1.1 %collective-permute-start.14 = (bf16[272,512]{1,0:T(8,128)(2,1)S(1)}, bf16[272,512]{1,0:T(8,128)(2,1)S(1)}, u32[]{:S(2)}, u32[]{:S(2)}) collective-permute-start(bf16[272,512]{1,0:T(8,128)(2,1)S(1)} %get-tuple-element.86), channel_id=1, source_target_pairs={{0,3},{32,35},{1,0},{33,32},{2,1},{34,33},{3,2},{35,34},{4,7},{36,... | collective-permute-start | bytes 835592 | tf_op jit(solution)/shard_map/ppermute | solution.py:36
  83.5 1.3 %partials.6 = (bf16[272,512]{1,0:T(8,128)(2,1)S(1)}, bf16[272,512]{1,0:T(8,128)(2,1)S(1)}) custom-call(f32[16,512]{1,0:T(8,128)S(1)} %attention_bias.1.bias, bf16[8,576,128]{2,1,0:T(8,128)(2,1)S(1)} %get-tuple-element.62.refs_0_, bf16[10,576,128]{2,1,0:T(8,128)(2,1)S(1)} %collective-permute-done.6.refs_1_, ...), custom_call_target="tpu_custom_call" | custom-call | flops 570425344 | bytes 2359296 | tf_op jit(solution)/shard_map/partials/pallas_call | solution.py:280
  84.9 0.9 collective-permute-start.12
  85.8 1.0 collective-permute-start.15
  86.8 1.3 %partials.7 = (f32[272,512]{1,0:T(8,128)S(1)}, f32[272,512]{1,0:T(8,128)S(1)}) custom-call(f32[16,512]{1,0:T(8,128)S(1)} %attention_bias.1.bias, bf16[8,576,128]{2,1,0:T(8,128)(2,1)S(1)} %get-tuple-element.62.refs_0_, bf16[10,576,128]{2,1,0:T(8,128)(2,1)S(1)} %collective-permute-done.6.refs_1_, bf16[8,576,128]{2,1,0:T(8,128)(2,1)S(1)} %collective-permute-done.4.refs_2_, ...), custom_call_target="tpu_custom_call" | custom-call | flops 570425344 | bytes 2359296 | tf_op jit(solution)/shard_map/partials/pallas_call | solution.py:280
  88.1 1.5 %collective-permute-done.11.refs_1_ = bf16[272,512]{1,0:T(8,128)(2,1)S(1)} collective-permute-done((bf16[272,512]{1,0:T(8,128)(2,1)S(1)}, bf16[272,512]{1,0:T(8,128)(2,1)S(1)}, u32[]{:S(2)}, u32[]{:S(2)}) %collective-permute-start.11) | collective-permute-done | bytes 278560 | tf_op jit(solution)/shard_map/ppermute | solution.py:36
  89.7 2.7 %collective-permute-done.14.refs_5_ = bf16[272,512]{1,0:T(8,128)(2,1)S(1)} collective-permute-done((bf16[272,512]{1,0:T(8,128)(2,1)S(1)}, bf16[272,512]{1,0:T(8,128)(2,1)S(1)}, u32[]{:S(2)}, u32[]{:S(2)}) %collective-permute-start.14) | collective-permute-done | bytes 278560 | tf_op jit(solution)/shard_map/ppermute | solution.py:36
  92.3 0.4 collective-permute-done.12.refs_2_
  92.7 0.9 collective-permute-done.15.refs_6_
  93.7 0.8 middle.1
  94.5 1.6 %collective-permute-start.16 = (bf16[272,512]{1,0:T(8,128)(2,1)S(1)}, bf16[272,512]{1,0:T(8,128)(2,1)S(1)}, u32[]{:S(2)}, u32[]{:S(2)}) collective-permute-start(bf16[272,512]{1,0:T(8,128)(2,1)S(1)} %get-tuple-element.89), channel_id=1, source_target_pairs={{0,64},{32,96},{1,65},{33,97},{2,66},{34,98},{3,67},{35,99},{4,68}... | collective-permute-start | bytes 835592 | tf_op jit(solution)/shard_map/ppermute | solution.py:36
  96.1 1.7 %collective-permute-start.17 = (bf16[272,512]{1,0:T(8,128)(2,1)S(1)}, bf16[272,512]{1,0:T(8,128)(2,1)S(1)}, u32[]{:S(2)}, u32[]{:S(2)}) collective-permute-start(bf16[272,512]{1,0:T(8,128)(2,1)S(1)} %get-tuple-element.90), channel_id=1, source_target_pairs={{0,80},{32,112},{1,81},{33,113},{2,82},{34,114},{3,83},{35,115},{4... | collective-permute-start | bytes 835592 | tf_op jit(solution)/shard_map/ppermute | solution.py:36
  97.8 4.5 %collective-permute-done.16.plus = bf16[272,512]{1,0:T(8,128)(2,1)S(1)} collective-permute-done((bf16[272,512]{1,0:T(8,128)(2,1)S(1)}, bf16[272,512]{1,0:T(8,128)(2,1)S(1)}, u32[]{:S(2)}, u32[]{:S(2)}) %collective-permute-start.16) | collective-permute-done | bytes 278560 | tf_op jit(solution)/shard_map/ppermute | solution.py:36
  102.3 0.3 collective-permute-done.17.minus
  102.6 1.0 %last.1 = bf16[4,128,512]{2,1,0:T(8,128)(2,1)} custom-call(bf16[4,128,512]{2,1,0:T(8,128)(2,1)} %resident_rows.1.base, bf16[272,512]{1,0:T(8,128)(2,1)S(1)} %collective-permute-done.16.plus, bf16[272,512]{1,0:T(8,128)(2,1)S(1)} %collective-permute-done.17.minus), custom_call_target="tpu_custom_call", output_to_operand_aliasing={{}: (0, {})} | custom-call | tf_op jit(solution)/shard_map/last/pallas_call | solution.py:345
  (11 shorter events, 0.1 us)
Async XLA Ops:
  1.0 10.4 %collective-permute-start.1 = (bf16[1,576,128]{2,1,0:T(8,128)(2,1)S(1)}, bf16[1,576,128]{2,1,0:T(8,128)(2,1)S(1)}, u32[]{:S(2)}, u32[]{:S(2)}) collective-permute-start(bf16[1,576,128]{2,1,0:T(8,128)(2,1)S(1)} %get-tuple-element.91), channel_id=1, source_target_pairs={{0,2},{32,34},{1,3},{33,35},{2,0},{34,32},{3,1},{35,33},{4,6},{36,... | collective-permute-start | bytes 442376 | tf_op jit(solution)/shard_map/ppermute | solution.py:36
  4.4 7.4 %collective-permute-start = (bf16[1,576,128]{2,1,0:T(8,128)(2,1)S(1)}, bf16[1,576,128]{2,1,0:T(8,128)(2,1)S(1)}, u32[]{:S(2)}, u32[]{:S(2)}) collective-permute-start(bf16[1,576,128]{2,1,0:T(8,128)(2,1)S(1)} %get-tuple-element.92), channel_id=1, source_target_pairs={{0,8},{32,40},{1,9},{33,41},{2,10},{34,42},{3,11},{35,43},{4,12},{... | collective-permute-start | bytes 442376 | tf_op jit(solution)/shard_map/ppermute | solution.py:36
  8.3 0.7 copy-start.1
  9.0 6.4 %copy-start = (bf16[1,4,128,576]{2,3,1,0:T(8,128)(2,1)S(1)}, bf16[1,4,128,576]{2,3,1,0:T(8,128)(2,1)}, u32[]{:S(2)}) copy-start(bf16[1,4,128,576]{2,3,1,0:T(8,128)(2,1)} %param.6) | copy-start | bytes 1769476
  11.8 30.5 %collective-permute-start.4 = (bf16[8,576,128]{2,1,0:T(8,128)(2,1)S(1)}, bf16[8,576,128]{2,1,0:T(8,128)(2,1)S(1)}, u32[]{:S(2)}, u32[]{:S(2)}) collective-permute-start(bf16[8,576,128]{2,1,0:T(8,128)(2,1)S(1)} %get-tuple-element.57), channel_id=1, source_target_pairs={{0,2},{32,34},{1,3},{33,35},{2,0},{34,32},{3,1},{35,33},{4,6},{36,... | collective-permute-start | bytes 3538952 | tf_op jit(solution)/shard_map/ppermute | solution.py:36
  12.2 30.5 %collective-permute-start.5 = (bf16[8,576,128]{2,1,0:T(8,128)(2,1)S(1)}, bf16[8,576,128]{2,1,0:T(8,128)(2,1)S(1)}, u32[]{:S(2)}, u32[]{:S(2)}) collective-permute-start(bf16[8,576,128]{2,1,0:T(8,128)(2,1)S(1)} %get-tuple-element.58), channel_id=1, source_target_pairs={{0,8},{32,40},{1,9},{33,41},{2,10},{34,42},{3,11},{35,43},{4,12},{... | collective-permute-start | bytes 3538952 | tf_op jit(solution)/shard_map/ppermute | solution.py:36
  15.5 14.8 %collective-permute-start.3 = (bf16[4,576,128]{2,1,0:T(8,128)(2,1)S(1)}, bf16[4,576,128]{2,1,0:T(8,128)(2,1)S(1)}, u32[]{:S(2)}, u32[]{:S(2)}) collective-permute-start(bf16[4,576,128]{2,1,0:T(8,128)(2,1)S(1)} %pack_queries.1), channel_id=1, source_target_pairs={{0,64},{32,96},{1,65},{33,97},{2,66},{34,98},{3,67},{35,99},{4,68}... | collective-permute-start | bytes 1769480 | tf_op jit(solution)/shard_map/ppermute | solution.py:36
  17.0 13.3 %collective-permute-start.2 = (bf16[4,576,128]{2,1,0:T(8,128)(2,1)S(1)}, bf16[4,576,128]{2,1,0:T(8,128)(2,1)S(1)}, u32[]{:S(2)}, u32[]{:S(2)}) collective-permute-start(bf16[4,576,128]{2,1,0:T(8,128)(2,1)S(1)} %pack_queries.1), channel_id=1, source_target_pairs={{0,80},{32,112},{1,81},{33,113},{2,82},{34,114},{3,83},{35,115},{4... | collective-permute-start | bytes 1769480 | tf_op jit(solution)/shard_map/ppermute | solution.py:36
  30.3 15.4 %copy-start.3 = (s32[1,2]{1,0:T(1,128)S(1)}, s32[1,2]{1,0:T(1,128)}, u32[]{:S(2)}) copy-start(s32[1,2]{1,0:T(1,128)} %param.8) | copy-start | bytes 28
  31.3 40.5 %collective-permute-start.6 = (bf16[10,576,128]{2,1,0:T(8,128)(2,1)S(1)}, bf16[10,576,128]{2,1,0:T(8,128)(2,1)S(1)}, u32[]{:S(2)}, u32[]{:S(2)}) collective-permute-start(bf16[10,576,128]{2,1,0:T(8,128)(2,1)S(1)} %get-tuple-element.63), channel_id=1, source_target_pairs={{0,1},{32,33},{1,2},{33,34},{2,3},{34,35},{3,0},{35,32},{4,5},{36,... | collective-permute-start | bytes 4423688 | tf_op jit(solution)/shard_map/ppermute | solution.py:36
  32.6 39.2 %collective-permute-start.7 = (bf16[10,576,128]{2,1,0:T(8,128)(2,1)S(1)}, bf16[10,576,128]{2,1,0:T(8,128)(2,1)S(1)}, u32[]{:S(2)}, u32[]{:S(2)}) collective-permute-start(bf16[10,576,128]{2,1,0:T(8,128)(2,1)S(1)} %get-tuple-element.65), channel_id=1, source_target_pairs={{0,3},{32,35},{1,0},{33,32},{2,1},{34,33},{3,2},{35,34},{4,7},{36,... | collective-permute-start | bytes 4423688 | tf_op jit(solution)/shard_map/ppermute | solution.py:36
  34.5 37.4 %collective-permute-start.8 = (bf16[10,576,128]{2,1,0:T(8,128)(2,1)}, bf16[10,576,128]{2,1,0:T(8,128)(2,1)S(1)}, u32[]{:S(2)}, u32[]{:S(2)}) collective-permute-start(bf16[10,576,128]{2,1,0:T(8,128)(2,1)} %get-tuple-element.67), channel_id=1, source_target_pairs={{0,4},{32,36},{1,5},{33,37},{2,6},{34,38},{3,7},{35,39},{4,8},{36,... | collective-permute-start | bytes 4423688 | tf_op jit(solution)/shard_map/ppermute | solution.py:36
  42.6 30.6 %collective-permute-start.9 = (bf16[10,576,128]{2,1,0:T(8,128)(2,1)}, bf16[10,576,128]{2,1,0:T(8,128)(2,1)S(1)}, u32[]{:S(2)}, u32[]{:S(2)}) collective-permute-start(bf16[10,576,128]{2,1,0:T(8,128)(2,1)} %get-tuple-element.69), channel_id=1, source_target_pairs={{0,12},{32,44},{1,13},{33,45},{2,14},{34,46},{3,15},{35,47},{4,0},... | collective-permute-start | bytes 4423688 | tf_op jit(solution)/shard_map/ppermute | solution.py:36
  54.6 2.4 %copy-start.2 = (s32[4,64]{1,0:T(4,128)S(1)}, s32[4,64]{1,0:T(4,128)}, u32[]{:S(2)}) copy-start(s32[4,64]{1,0:T(4,128)} %lengths.1) | copy-start | bytes 3076
  74.6 11.2 %collective-permute-start.10 = (bf16[272,512]{1,0:T(8,128)(2,1)S(1)}, bf16[272,512]{1,0:T(8,128)(2,1)S(1)}, u32[]{:S(2)}, u32[]{:S(2)}) collective-permute-start(bf16[272,512]{1,0:T(8,128)(2,1)S(1)} %get-tuple-element.72), channel_id=1, source_target_pairs={{0,8},{32,40},{1,9},{33,41},{2,10},{34,42},{3,11},{35,43},{4,12},{... | collective-permute-start | bytes 835592 | tf_op jit(solution)/shard_map/ppermute | solution.py:36
  76.9 11.2 %collective-permute-start.13 = (bf16[272,512]{1,0:T(8,128)(2,1)S(1)}, bf16[272,512]{1,0:T(8,128)(2,1)S(1)}, u32[]{:S(2)}, u32[]{:S(2)}) collective-permute-start(bf16[272,512]{1,0:T(8,128)(2,1)S(1)} %get-tuple-element.85), channel_id=1, source_target_pairs={{0,2},{32,34},{1,3},{33,35},{2,0},{34,32},{3,1},{35,33},{4,6},{36,... | collective-permute-start | bytes 835592 | tf_op jit(solution)/shard_map/ppermute | solution.py:36
  81.0 8.7 %collective-permute-start.11 = (bf16[272,512]{1,0:T(8,128)(2,1)S(1)}, bf16[272,512]{1,0:T(8,128)(2,1)S(1)}, u32[]{:S(2)}, u32[]{:S(2)}) collective-permute-start(bf16[272,512]{1,0:T(8,128)(2,1)S(1)} %get-tuple-element.76), channel_id=1, source_target_pairs={{0,12},{32,44},{1,13},{33,45},{2,14},{34,46},{3,15},{35,47},{4,0},... | collective-permute-start | bytes 835592 | tf_op jit(solution)/shard_map/ppermute | solution.py:36
  82.5 9.8 %collective-permute-start.14 = (bf16[272,512]{1,0:T(8,128)(2,1)S(1)}, bf16[272,512]{1,0:T(8,128)(2,1)S(1)}, u32[]{:S(2)}, u32[]{:S(2)}) collective-permute-start(bf16[272,512]{1,0:T(8,128)(2,1)S(1)} %get-tuple-element.86), channel_id=1, source_target_pairs={{0,3},{32,35},{1,0},{33,32},{2,1},{34,33},{3,2},{35,34},{4,7},{36,... | collective-permute-start | bytes 835592 | tf_op jit(solution)/shard_map/ppermute | solution.py:36
  84.9 7.8 %collective-permute-start.12 = (bf16[272,512]{1,0:T(8,128)(2,1)S(1)}, bf16[272,512]{1,0:T(8,128)(2,1)S(1)}, u32[]{:S(2)}, u32[]{:S(2)}) collective-permute-start(bf16[272,512]{1,0:T(8,128)(2,1)S(1)} %get-tuple-element.80), channel_id=1, source_target_pairs={{0,4},{32,36},{1,5},{33,37},{2,6},{34,38},{3,7},{35,39},{4,8},{36,... | collective-permute-start | bytes 835592 | tf_op jit(solution)/shard_map/ppermute | solution.py:36
  85.8 7.9 %collective-permute-start.15 = (bf16[272,512]{1,0:T(8,128)(2,1)S(1)}, bf16[272,512]{1,0:T(8,128)(2,1)S(1)}, u32[]{:S(2)}, u32[]{:S(2)}) collective-permute-start(bf16[272,512]{1,0:T(8,128)(2,1)S(1)} %get-tuple-element.87), channel_id=1, source_target_pairs={{0,1},{32,33},{1,2},{33,34},{2,3},{34,35},{3,0},{35,32},{4,5},{36,... | collective-permute-start | bytes 835592 | tf_op jit(solution)/shard_map/ppermute | solution.py:36
  94.5 7.8 %collective-permute-start.16 = (bf16[272,512]{1,0:T(8,128)(2,1)S(1)}, bf16[272,512]{1,0:T(8,128)(2,1)S(1)}, u32[]{:S(2)}, u32[]{:S(2)}) collective-permute-start(bf16[272,512]{1,0:T(8,128)(2,1)S(1)} %get-tuple-element.89), channel_id=1, source_target_pairs={{0,64},{32,96},{1,65},{33,97},{2,66},{34,98},{3,67},{35,99},{4,68}... | collective-permute-start | bytes 835592 | tf_op jit(solution)/shard_map/ppermute | solution.py:36
  96.1 6.5 %collective-permute-start.17 = (bf16[272,512]{1,0:T(8,128)(2,1)S(1)}, bf16[272,512]{1,0:T(8,128)(2,1)S(1)}, u32[]{:S(2)}, u32[]{:S(2)}) collective-permute-start(bf16[272,512]{1,0:T(8,128)(2,1)S(1)} %get-tuple-element.90), channel_id=1, source_target_pairs={{0,80},{32,112},{1,81},{33,113},{2,82},{34,114},{3,83},{35,115},{4... | collective-permute-start | bytes 835592 | tf_op jit(solution)/shard_map/ppermute | solution.py:36
